TPU v7x, 32 devices: a whole 2x2x4 slice. The times are simulated.
32 devices in a mesh: member: 2 (over x), lon: 16 (over z, y, core).
Axes of the slice: x: 2, y: 2, z: 4, core: 2. Of those that a mesh axis runs over, the one named last changes fastest.
Arguments:
- right_side: float32 [512, 1024], P(('member', 'lon')), parts along dimension 0, may hold values from -72 to 72
- east_coef: float32 [256, 1024], P('lon'), may hold values from 0.5 to 2
- north_coef: float32 [256, 1024], P('lon'), may hold values from 0.5 to 2
- surface_term: float32 [256, 1024], P('lon'), may hold values from 0.02 to 1
- cell_mask: int32 [256, 1024], P('lon'), may hold values 0 or 1
- inverse_blocks: float32 [2048, 128, 128], P('lon'), may hold values from -0.2 to 0.2
- active_tiles: int32 [1536], replicated, may hold values from 0 to 2047, as said below
- low_bound: float32 [1], replicated, may hold values from 0.05 to 0.25
- high_bound: float32 [1], replicated, may hold values from 2 to 2.5
Outputs:
- solution_field: float32 [512, 1024], P(('member', 'lon')), parts along dimension 0
- residual: float32 [512, 1024], P(('member', 'lon')), parts along dimension 0
- norms: float32 [8], P('member'), parts along dimension 0
There are 2 independent parts, one for each index of `member`. A program takes and returns all parts, laid end to end along the dimension named above; an argument that names none is the same for every part. Nothing has to cross between parts.
Inputs may be any that keep to these rules, and one draw needn't show every extreme that they name: `active_tiles`: sorted ascending and distinct. Tile g belongs to device g // 128 of lon. For each device i below 8, one of the devices i and i + 8 has all its 128 tiles listed and the other exactly 64 of them.
All inputs are finite; a program needn't handle non-finite values. No bound on the sum of `cell_mask` on one device may be relied on, other than what follows from the above.
Results may differ from a plain program's by a relative error of at most 0.0001.
Values sent between devices are 32-bit elements; how exact they have to be, the bound alone decides.
No kernel may reach another device: no remote copies, remote signals or barrier semaphores. Data moves between devices by JAX's collectives and lax.ppermute only.
A program may use at most 64 MiB of HBM per device.

v0:
```python
import jax
import jax.numpy as jnp
from jax import lax
from jax.sharding import PartitionSpec as P

ITERS = 4


def extended(x, sides, width):
    for axis, dim in sides:
        devices, length = (lax.axis_size(axis), x.shape[dim])
        up = [(i, (i + 1) % devices) for i in range(devices)]
        down = [(j, i) for i, j in up]
        last = lax.slice_in_dim(x, length - width, length, axis=dim)
        first = lax.slice_in_dim(x, 0, width, axis=dim)
        before = lax.ppermute(last, axis, up)
        after = lax.ppermute(first, axis, down)
        x = jnp.concatenate([before, x, after], axis=dim)
    return x


def to_tiles(field, tiles_dev, lat_run, block):
    columns = field.shape[0]
    return field.reshape(columns, tiles_dev, lat_run).transpose(1, 0, 2).reshape(tiles_dev, block)


def from_tiles(tiles, columns, tiles_dev, lat_run):
    return (
        tiles.reshape(tiles_dev, columns, lat_run)
        .transpose(1, 0, 2)
        .reshape(columns, tiles_dev * lat_run)
    )


def apply_blocks(blocks, tiles):
    return jnp.einsum("gij,gj->gi", blocks, tiles, precision=lax.Precision.HIGHEST)


def on_device(
    right_side,
    east_coef,
    north_coef,
    surface_term,
    cell_mask,
    inverse_blocks,
    active_tiles,
    low_bound,
    high_bound,
):
    columns, rows = right_side.shape
    tiles_dev, block, _ = inverse_blocks.shape
    lat_run = rows // tiles_dev
    devices = lax.axis_size("lon")
    device = lax.axis_index("lon")
    first_tile = device * tiles_dev
    local_tile = active_tiles - first_tile
    owned = (local_tile >= 0) & (local_tile < tiles_dev)
    hits = (local_tile[:, None] == jnp.arange(tiles_dev, dtype=jnp.int32)[None, :]) & owned[:, None]
    tile_flags = jnp.sum(hits.astype(jnp.float32), axis=0)
    ocean = cell_mask.astype(jnp.float32) * jnp.repeat(tile_flags, lat_run)[None, :]
    stacked = jnp.stack([ocean, east_coef])
    widened = extended(stacked, (("lon", 1),), 1)
    ocean_wide = widened[0]
    east_wide = widened[1]
    east_faces = east_wide[:-1] * ocean_wide[:-1] * ocean_wide[1:]
    zero_row = jnp.zeros((columns, 1), jnp.float32)
    north_faces = north_coef * ocean * jnp.concatenate([ocean[:, 1:], zero_row], axis=1)
    south_faces = jnp.concatenate([zero_row, north_faces[:, :-1]], axis=1)
    cells_all = columns * devices * rows
    center = (high_bound[0] + low_bound[0]) / 2.0
    radius = (high_bound[0] - low_bound[0]) / 2.0
    ratio = center / radius
    solution_field = jnp.zeros((columns, rows), jnp.float32)
    residual = ocean * right_side
    weight_prev = 1.0 / ratio
    direction = jnp.zeros((columns, rows), jnp.float32)
    local_norms = []
    for step in range(ITERS):
        tiles = to_tiles(residual, tiles_dev, lat_run, block)
        result = apply_blocks(inverse_blocks, tiles)
        search = ocean * from_tiles(result, columns, tiles_dev, lat_run)
        if step == 0:
            direction = search / center
        else:
            weight = 1.0 / (2.0 * ratio - weight_prev)
            direction = weight * weight_prev * direction + 2.0 * weight / radius * search
            weight_prev = weight
        solution_field = solution_field + direction
        wide = extended(direction, (("lon", 0),), 1)
        north_vals = jnp.concatenate([direction[:, 1:], zero_row], axis=1)
        south_vals = jnp.concatenate([zero_row, direction[:, :-1]], axis=1)
        total = surface_term * direction
        total = total + east_faces[1:] * (direction - wide[2:])
        total = total + east_faces[:-1] * (direction - wide[:-2])
        total = total + north_faces * (direction - north_vals)
        total = total + south_faces * (direction - south_vals)
        residual = residual - ocean * total
        squares = jnp.sum(residual * residual)
        local_norms.append(lax.psum(squares, "lon") / cells_all)
    norms = jnp.stack(local_norms)
    return (solution_field, residual, norms)


def solution(mesh):
    in_specs = (
        P(("member", "lon"), None),
        P("lon", None),
        P("lon", None),
        P("lon", None),
        P("lon", None),
        P("lon", None, None),
        P(),
        P(),
        P(),
    )
    out_specs = (P(("member", "lon"), None), P(("member", "lon"), None), P("member"))
    return jax.shard_map(
        on_device, mesh=mesh, in_specs=in_specs, out_specs=out_specs, check_vma=False
    )
```

profile of v0, /device:TPU:0, one launch (start us, length us, event | category | flops | bytes accessed | tf_op | source)
XLA Modules:
  0.0 103.4 jit_solution(8447071232864406239)
XLA Ops:
  0.7 0.7 compare_and_fusion
  1.4 1.0 convert_reduce_fusion
  2.6 0.9 fusion.46
  3.5 0.8 pad_maximum_fusion.11
  4.3 5.5 %collective-permute-start.1 = (f32[2,1,1024]{2,0,1:T(2,128)S(1)}, f32[2,1,1024]{2,0,1:T(2,128)S(1)}, u32[]{:S(2)}, u32[]{:S(2)}) collective-permute-start(f32[2,1,1024]{2,0,1:T(2,128)S(1)} %copy.131), channel_id=1, source_target_pairs={{1,0},{2,1},{3,2},{4,3},{5,4},{6,5},{7,6},{8,7},{9,8},{10,9},{11,1... | collective-permute-start | bytes 24584 | tf_op jit(solution)/shard_map/ppermute | solution.py:17
  11.7 5.6 %multiply_reduce_fusion.3 = f32[128,128]{1,0:T(8,128)S(1)} fusion(f32[128,128,128]{2,1,0:T(8,128)} %param.14, f32[128,128]{1,0:T(8,128)S(1)} %copy.165), kind=kLoop, calls=%fused_computation.3 | loop fusion | flops 4177920 | bytes 8519680
  17.4 0.3 copy.127
  17.9 4.5 %collective-permute-start.2 = (f32[1,1024]{1,0:T(1,128)S(1)}, f32[1,1024]{1,0:T(1,128)S(1)}, u32[]{:S(2)}, u32[]{:S(2)}) collective-permute-start(f32[1,1024]{1,0:T(1,128)S(1)} %get-tuple-element.44), channel_id=1, source_target_pairs={{1,0},{2,1},{3,2},{4,3},{5,4},{6,5},{7,6},{8,7},{9,8},{10,9},{11,1... | collective-permute-start | bytes 12296 | tf_op jit(solution)/shard_map/ppermute | solution.py:17
  23.0 0.8 collective-permute-done.2
  23.7 4.4 %collective-permute-done.3 = f32[1,1024]{1,0:T(1,128)S(1)} collective-permute-done((f32[1,1024]{1,0:T(1,128)S(1)}, f32[1,1024]{1,0:T(1,128)S(1)}, u32[]{:S(2)}, u32[]{:S(2)}) %collective-permute-start.3) | collective-permute-done | bytes 4128 | tf_op jit(solution)/shard_map/ppermute | solution.py:16
  28.1 0.7 multiply_reduce_fusion.7
  29.4 5.6 %multiply_reduce_fusion.2 = f32[128,128]{1,0:T(8,128)S(1)} fusion(f32[128,128,128]{2,1,0:T(8,128)} %param.14, f32[128,128]{1,0:T(8,128)S(1)} %copy.166), kind=kLoop, calls=%fused_computation.2 | loop fusion | flops 4177920 | bytes 8519680
  35.1 0.3 copy.135
  35.6 0.5 collective-permute-start.5
  36.2 0.7 collective-permute-done.4
  36.9 4.5 %collective-permute-done.5 = f32[1,1024]{1,0:T(1,128)S(1)} collective-permute-done((f32[1,1024]{1,0:T(1,128)S(1)}, f32[1,1024]{1,0:T(1,128)S(1)}, u32[]{:S(2)}, u32[]{:S(2)}) %collective-permute-start.5) | collective-permute-done | bytes 4128 | tf_op jit(solution)/shard_map/ppermute | solution.py:16
  41.4 0.7 multiply_reduce_fusion.6
  42.6 5.6 %multiply_reduce_fusion.1 = f32[128,128]{1,0:T(8,128)S(1)} fusion(f32[128,128,128]{2,1,0:T(8,128)} %param.14, f32[128,128]{1,0:T(8,128)S(1)} %copy.167), kind=kLoop, calls=%fused_computation.1 | loop fusion | flops 4177920 | bytes 8519680
  48.4 0.3 copy.139
  48.9 0.5 collective-permute-start.7
  49.5 0.7 collective-permute-done.6
  50.2 4.6 %collective-permute-done.7 = f32[1,1024]{1,0:T(1,128)S(1)} collective-permute-done((f32[1,1024]{1,0:T(1,128)S(1)}, f32[1,1024]{1,0:T(1,128)S(1)}, u32[]{:S(2)}, u32[]{:S(2)}) %collective-permute-start.7) | collective-permute-done | bytes 4128 | tf_op jit(solution)/shard_map/ppermute | solution.py:16
  54.9 0.7 multiply_reduce_fusion.5
  56.1 5.6 %multiply_reduce_fusion = f32[128,128]{1,0:T(8,128)S(1)} fusion(f32[128,128,128]{2,1,0:T(8,128)} %param.14, f32[128,128]{1,0:T(8,128)S(1)} %copy.168), kind=kLoop, calls=%fused_computation | loop fusion | flops 4177920 | bytes 8519680
  61.8 0.3 copy.143
  62.2 0.7 multiply_add_fusion
  62.9 0.5 collective-permute-start.9
  63.5 0.7 collective-permute-done.8
  64.3 4.5 %collective-permute-done.9 = f32[1,1024]{1,0:T(1,128)S(1)} collective-permute-done((f32[1,1024]{1,0:T(1,128)S(1)}, f32[1,1024]{1,0:T(1,128)S(1)}, u32[]{:S(2)}, u32[]{:S(2)}) %collective-permute-start.9) | collective-permute-done | bytes 4128 | tf_op jit(solution)/shard_map/ppermute | solution.py:16
  68.7 1.4 %multiply_reduce_fusion.4 = (f32[]{:T(128)}, f32[16,1024]{1,0:T(8,128)}) fusion(f32[16,1024]{1,0:T(8,128)S(1)} %get-tuple-element.21, f32[16,1024]{1,0:T(8,128)S(1)} %get-tuple-element.25, f32[16,1024]{1,0:T(8,128)S(1)} %get-tuple-element.28, f32[16,1023]{1,0:T(8,128)S(1)} %get-tuple-element.35, f32[16,1023]{1,0:T(8,128)S(1)} %bitcast.83, ...), kind=kLoop, calls=%fused_computation.62 | loop fusion | flops 311295 | bytes 728900 | tf_op jit(solution)/shard_map/reduce_sum | solution.py:98
  70.1 30.2 %all-reduce.10 = (f32[]{:T(128)}, f32[]{:T(128)}, f32[]{:T(128)}, f32[]{:T(128)}) all-reduce(f32[]{:T(128)} %get-tuple-element.22, f32[]{:T(128)} %get-tuple-element.20, f32[]{:T(128)} %get-tuple-element.18, f32[]{:T(128)} %get-tuple-element.16), channel_id=1, replica_groups=mesh['member'=2,'lon'=16] {'lon'}, use_global_device_ids=true, to_apply=%region_8.0 | all-reduce | flops 4 | bytes 32 | tf_op jit(solution)/shard_map/psum | solution.py:99
  102.8 0.6 pad_maximum_fusion.12
  (53 shorter events, 3.9 us)
Async XLA Ops:
  0.6 22.2 %copy-start.1 = (f32[16,1024]{1,0:T(8,128)S(1)}, f32[16,1024]{1,0:T(8,128)}, u32[]{:S(2)}) copy-start(f32[16,1024]{1,0:T(8,128)} %param.10) | copy-start | bytes 196612
  0.6 17.2 %copy-start.2 = (f32[16,1024]{1,0:T(8,128)S(1)}, f32[16,1024]{1,0:T(8,128)}, u32[]{:S(2)}) copy-start(f32[16,1024]{1,0:T(8,128)} %param.11) | copy-start | bytes 196612
  0.7 27.5 %copy-start = (f32[16,1024]{1,0:T(8,128)S(1)}, f32[16,1024]{1,0:T(8,128)}, u32[]{:S(2)}) copy-start(f32[16,1024]{1,0:T(8,128)} %param.12) | copy-start | bytes 196612
  4.3 18.6 %collective-permute-start.1 = (f32[2,1,1024]{2,0,1:T(2,128)S(1)}, f32[2,1,1024]{2,0,1:T(2,128)S(1)}, u32[]{:S(2)}, u32[]{:S(2)}) collective-permute-start(f32[2,1,1024]{2,0,1:T(2,128)S(1)} %copy.131), channel_id=1, source_target_pairs={{1,0},{2,1},{3,2},{4,3},{5,4},{6,5},{7,6},{8,7},{9,8},{10,9},{11,1... | collective-permute-start | bytes 24584 | tf_op jit(solution)/shard_map/ppermute | solution.py:17
  9.8 13.0 %collective-permute-start = (f32[2,1,1024]{2,0,1:T(2,128)S(1)}, f32[2,1,1024]{2,0,1:T(2,128)S(1)}, u32[]{:S(2)}, u32[]{:S(2)}) collective-permute-start(f32[2,1,1024]{2,0,1:T(2,128)S(1)} %copy.129), channel_id=1, source_target_pairs={{0,1},{1,2},{2,3},{3,4},{4,5},{5,6},{6,7},{7,8},{8,9},{9,10},{10,1... | collective-permute-start | bytes 24584 | tf_op jit(solution)/shard_map/ppermute | solution.py:16
  17.9 5.8 %collective-permute-start.2 = (f32[1,1024]{1,0:T(1,128)S(1)}, f32[1,1024]{1,0:T(1,128)S(1)}, u32[]{:S(2)}, u32[]{:S(2)}) collective-permute-start(f32[1,1024]{1,0:T(1,128)S(1)} %get-tuple-element.44), channel_id=1, source_target_pairs={{1,0},{2,1},{3,2},{4,3},{5,4},{6,5},{7,6},{8,7},{9,8},{10,9},{11,1... | collective-permute-start | bytes 12296 | tf_op jit(solution)/shard_map/ppermute | solution.py:17
  22.4 5.7 %collective-permute-start.3 = (f32[1,1024]{1,0:T(1,128)S(1)}, f32[1,1024]{1,0:T(1,128)S(1)}, u32[]{:S(2)}, u32[]{:S(2)}) collective-permute-start(f32[1,1024]{1,0:T(1,128)S(1)} %get-tuple-element.45), channel_id=1, source_target_pairs={{0,1},{1,2},{2,3},{3,4},{4,5},{5,6},{6,7},{7,8},{8,9},{9,10},{10,1... | collective-permute-start | bytes 12296 | tf_op jit(solution)/shard_map/ppermute | solution.py:16
  35.6 1.4 %collective-permute-start.4 = (f32[1,1024]{1,0:T(1,128)S(1)}, f32[1,1024]{1,0:T(1,128)S(1)}, u32[]{:S(2)}, u32[]{:S(2)}) collective-permute-start(f32[1,1024]{1,0:T(1,128)S(1)} %get-tuple-element.40), channel_id=1, source_target_pairs={{1,0},{2,1},{3,2},{4,3},{5,4},{6,5},{7,6},{8,7},{9,8},{10,9},{11,1... | collective-permute-start | bytes 12296 | tf_op jit(solution)/shard_map/ppermute | solution.py:17
  35.6 5.8 %collective-permute-start.5 = (f32[1,1024]{1,0:T(1,128)S(1)}, f32[1,1024]{1,0:T(1,128)S(1)}, u32[]{:S(2)}, u32[]{:S(2)}) collective-permute-start(f32[1,1024]{1,0:T(1,128)S(1)} %get-tuple-element.41), channel_id=1, source_target_pairs={{0,1},{1,2},{2,3},{3,4},{4,5},{5,6},{6,7},{7,8},{8,9},{9,10},{10,1... | collective-permute-start | bytes 12296 | tf_op jit(solution)/shard_map/ppermute | solution.py:16
  48.8 1.4 %collective-permute-start.6 = (f32[1,1024]{1,0:T(1,128)S(1)}, f32[1,1024]{1,0:T(1,128)S(1)}, u32[]{:S(2)}, u32[]{:S(2)}) collective-permute-start(f32[1,1024]{1,0:T(1,128)S(1)} %get-tuple-element.36), channel_id=1, source_target_pairs={{1,0},{2,1},{3,2},{4,3},{5,4},{6,5},{7,6},{8,7},{9,8},{10,9},{11,1... | collective-permute-start | bytes 12296 | tf_op jit(solution)/shard_map/ppermute | solution.py:17
  48.9 6.0 %collective-permute-start.7 = (f32[1,1024]{1,0:T(1,128)S(1)}, f32[1,1024]{1,0:T(1,128)S(1)}, u32[]{:S(2)}, u32[]{:S(2)}) collective-permute-start(f32[1,1024]{1,0:T(1,128)S(1)} %get-tuple-element.37), channel_id=1, source_target_pairs={{0,1},{1,2},{2,3},{3,4},{4,5},{5,6},{6,7},{7,8},{8,9},{9,10},{10,1... | collective-permute-start | bytes 12296 | tf_op jit(solution)/shard_map/ppermute | solution.py:16
  62.9 1.4 %collective-permute-start.8 = (f32[1,1024]{1,0:T(1,128)S(1)}, f32[1,1024]{1,0:T(1,128)S(1)}, u32[]{:S(2)}, u32[]{:S(2)}) collective-permute-start(f32[1,1024]{1,0:T(1,128)S(1)} %get-tuple-element.32), channel_id=1, source_target_pairs={{1,0},{2,1},{3,2},{4,3},{5,4},{6,5},{7,6},{8,7},{9,8},{10,9},{11,1... | collective-permute-start | bytes 12296 | tf_op jit(solution)/shard_map/ppermute | solution.py:17
  62.9 5.8 %collective-permute-start.9 = (f32[1,1024]{1,0:T(1,128)S(1)}, f32[1,1024]{1,0:T(1,128)S(1)}, u32[]{:S(2)}, u32[]{:S(2)}) collective-permute-start(f32[1,1024]{1,0:T(1,128)S(1)} %get-tuple-element.33), channel_id=1, source_target_pairs={{0,1},{1,2},{2,3},{3,4},{4,5},{5,6},{6,7},{7,8},{8,9},{9,10},{10,1... | collective-permute-start | bytes 12296 | tf_op jit(solution)/shard_map/ppermute | solution.py:16
where the time goes:
time: 104 us; the launch traced here: 103 us
  other arithmetic  30.8 us (30%)
  blocking collectives  30.2 us (29%)
  waiting for transfers between devices  21 us (20%)
  starting transfers between devices  11.7 us (11%)
  between operations  5.16 us (5%)
  local copies, waits for them, and re-layouts  4.65 us (4%)
    psum x1, blocking collectives, on_device(): local_norms.append(lax.psum(squares, 'lon') / cells_all)  30.2 us
    unnamed x4, other arithmetic  22.5 us
    ppermute x5, waiting for transfers between devices, extended(): before = lax.ppermute(last, axis, up)  18 us
    ppermute x5, starting transfers between devices, extended(): after = lax.ppermute(first, axis, down)  10.2 us
    reduce_sum x4, other arithmetic, on_device(): squares = jnp.sum(residual * residual)  3.54 us
    ppermute x5, waiting for transfers between devices, extended(): after = lax.ppermute(first, axis, down)  3.01 us
  transfers between devices with their start and end apart: 10, of which 8 were waited for; matrix products, arithmetic and copies ran while one was open for 7% of the time, Pallas kernels for 0%

commit v1 on v0

v1 whole, which is shorter than its diff:
```python
import functools

import jax
import jax.numpy as jnp
from jax import lax
from jax.experimental import pallas as pl
from jax.experimental.pallas import tpu as pltpu
from jax.sharding import PartitionSpec as P

ITERS = 4
LANES = 128
SUBS = 8
F32 = jnp.float32
MIB = 2**20


def lane_blocks(rows):
    return rows // LANES


def roll(x, shift, axis):
    return pltpu.roll(x, shift % x.shape[axis], axis)


def repeat_row(row, times):
    return jnp.concatenate([row] * times, axis=1)


def gather_index():
    lane = lax.broadcasted_iota(jnp.int32, (SUBS, LANES), 1)
    sub = lax.broadcasted_iota(jnp.int32, (SUBS, LANES), 0)
    return (lane // SUBS) * SUBS + sub


def expand(field, block, index):
    part = field[:, block * LANES : (block + 1) * LANES]
    rows = [
        jnp.take_along_axis(jnp.broadcast_to(part[a : a + 1], (SUBS, LANES)), index, axis=1)
        for a in range(part.shape[0])
    ]
    return jnp.concatenate(rows, axis=0)


def blocks_product(bt_ref, field, out_ref):
    index = gather_index()
    columns, rows = field.shape
    for block in range(lane_blocks(rows)):
        spread = expand(field, block, index)
        for a in range(columns):
            out_ref[a : a + 1, block * LANES : (block + 1) * LANES] = jnp.sum(
                bt_ref[block, a] * spread, axis=0, keepdims=True
            )


def lane_partial(squares):
    total = jnp.sum(squares, axis=0, keepdims=True)
    parts = [total[:, i * LANES : (i + 1) * LANES] for i in range(total.shape[1] // LANES)]
    return functools.reduce(jnp.add, parts)


def tile_flags(active_ref, first, tiles):
    active = active_ref[...]
    before = jnp.sum((active < first).astype(jnp.int32))
    row = jnp.minimum(before // LANES, active_ref.shape[0] - 2)
    lane = lax.broadcasted_iota(jnp.int32, (LANES, tiles), 1) + first
    found = jnp.zeros((LANES, tiles), jnp.int32)
    for step in range(2):
        entries = jnp.broadcast_to(active_ref[pl.ds(row + step, 1), :], (LANES, LANES))
        found = found + (entries.T == lane).astype(jnp.int32)
    return (jnp.sum(found, axis=0, keepdims=True) > 0).astype(F32)


def first_kernel(
    device_ref, low_ref, high_ref, active_ref, right_ref, east_ref, north_ref, surface_ref, mask_ref, blocks_hbm,
    residual_ref, direction_ref, bt_ref, diag_ref, east_face_ref, north_face_ref, ocean_ref, coef_ref, up_ref, down_ref,
    raw, sems,
):
    columns, rows = right_ref.shape
    tiles = blocks_hbm.shape[0]
    count = lane_blocks(rows)
    step = tiles // count

    def fetch(i):
        part = pl.ds(i * step, step)
        return pltpu.make_async_copy(blocks_hbm.at[part], raw.at[part], sems.at[i])

    for i in range(count):
        fetch(i).start()
    low = jnp.full((1, LANES), low_ref[0], F32)
    high = jnp.full((1, LANES), high_ref[0], F32)
    center = (high + low) / 2.0
    radius = (high - low) / 2.0
    ratio = center / radius
    weight_prev = 1.0 / ratio
    coef_ref[0:1] = 1.0 / center
    for k in range(1, ITERS):
        weight = 1.0 / (2.0 * ratio - weight_prev)
        coef_ref[2 * k : 2 * k + 1] = weight * weight_prev
        coef_ref[2 * k + 1 : 2 * k + 2] = 2.0 * weight / radius
        weight_prev = weight
    flags = tile_flags(active_ref, device_ref[0] * tiles, tiles)
    lane = lax.broadcasted_iota(jnp.int32, (SUBS, LANES), 1)
    spread = [
        jnp.take_along_axis(jnp.broadcast_to(flags, (SUBS, tiles)), i * step + lane // SUBS, axis=1)
        for i in range(count)
    ]
    flag_lat = jnp.concatenate(spread, axis=1)[0:1]
    ocean = mask_ref[...].astype(F32) * flag_lat
    ocean_ref[...] = ocean
    lat = lax.broadcasted_iota(jnp.int32, (columns, rows), 1)
    lon = lax.broadcasted_iota(jnp.int32, (columns, rows), 0)
    east_ocean = east_ref[...] * ocean
    east_face = jnp.where(lon < columns - 1, east_ocean * roll(ocean, -1, 0), 0.0)
    north_face = jnp.where(lat < rows - 1, north_ref[...] * ocean * roll(ocean, -1, 1), 0.0)
    east_face_ref[...] = east_face
    north_face_ref[...] = north_face
    diag_ref[...] = surface_ref[...] * ocean + east_face + roll(east_face, 1, 0) + north_face + roll(north_face, 1, 1)
    residual = right_ref[...] * ocean
    residual_ref[...] = residual
    up_ref[1:2] = east_ocean[columns - 1 :]
    down_ref[1:2] = ocean[0:1]
    index = gather_index()
    for i in range(count):
        spread = expand(residual, i, index)
        fetch(i).wait()
        for a in range(columns):
            part = raw[i * step : (i + 1) * step, a * SUBS : (a + 1) * SUBS, :].reshape(LANES, LANES).T
            bt_ref[i, a] = part
            direction_ref[a : a + 1, i * LANES : (i + 1) * LANES] = jnp.sum(part * spread, axis=0, keepdims=True)
    direction = direction_ref[...] * ocean * repeat_row(coef_ref[0:1], count)
    direction_ref[...] = direction
    up_ref[0:1] = direction[columns - 1 :]
    down_ref[0:1] = direction[0:1]


def apply_operator(residual, direction, diag, east_face, north_face, west_term, east_term):
    flow = diag * direction
    flow = flow - east_face * roll(direction, -1, 0) - roll(east_face, 1, 0) * roll(direction, 1, 0)
    flow = flow - north_face * roll(direction, -1, 1) - roll(north_face, 1, 1) * roll(direction, 1, 1)
    lon = lax.broadcasted_iota(jnp.int32, residual.shape, 0)
    flow = jnp.where(lon == 0, flow - west_term, flow)
    flow = jnp.where(lon == residual.shape[0] - 1, flow - east_term, flow)
    return residual - flow


def search_step(bt_ref, residual, direction, ocean, coef_ref, k, search_ref, up_ref, down_ref, direction_out):
    count = lane_blocks(residual.shape[1])
    blocks_product(bt_ref, residual, search_ref)
    keep = repeat_row(coef_ref[2 * k : 2 * k + 1], count)
    gain = repeat_row(coef_ref[2 * k + 1 : 2 * k + 2], count)
    direction = keep * direction + gain * (ocean * search_ref[...])
    direction_out[...] = direction
    up_ref[...] = direction[-1:]
    down_ref[...] = direction[0:1]
    return direction


def second_kernel(
    west_ref, east_ref, residual_ref, direction_ref, diag_ref, east_face_ref, north_face_ref, ocean_ref, east_ocean_ref, coef_ref, bt_ref,
    residual_out, direction_out, solution_out, diag_out, faces_out, norms_out, up_ref, down_ref,
    search_ref,
):
    ocean = ocean_ref[...]
    direction = direction_ref[...]
    columns = ocean.shape[0]
    west_face = west_ref[1:2] * ocean[0:1]
    east_end = east_ocean_ref[1:2] * east_ref[1:2]
    faces_out[0:1] = west_face
    faces_out[1:2] = east_end
    lon = lax.broadcasted_iota(jnp.int32, ocean.shape, 0)
    diag = diag_ref[...]
    diag = jnp.where(lon == 0, diag + west_face, diag)
    diag = jnp.where(lon == columns - 1, diag + east_end, diag)
    diag_out[...] = diag
    residual = apply_operator(
        residual_ref[...], direction, diag, east_face_ref[...], north_face_ref[...],
        west_face * west_ref[0:1], east_end * east_ref[0:1],
    )
    residual_out[...] = residual
    norms_out[...] = jnp.zeros_like(norms_out)
    norms_out[0:1] = lane_partial(residual * residual)
    later = search_step(bt_ref, residual, direction, ocean, coef_ref, 1, search_ref, up_ref, down_ref, direction_out)
    solution_out[...] = direction + later


def middle_kernel(
    k,
    west_ref, east_ref, residual_ref, direction_ref, solution_ref, diag_ref, east_face_ref, north_face_ref, ocean_ref, faces_ref, coef_ref, norms_ref, bt_ref,
    residual_out, direction_out, solution_out, norms_out, up_ref, down_ref,
    search_ref,
):
    direction = direction_ref[...]
    residual = apply_operator(
        residual_ref[...], direction, diag_ref[...], east_face_ref[...], north_face_ref[...],
        faces_ref[0:1] * west_ref[...], faces_ref[1:2] * east_ref[...],
    )
    residual_out[...] = residual
    norms_out[...] = norms_ref[...]
    norms_out[k - 1 : k] = lane_partial(residual * residual)
    later = search_step(bt_ref, residual, direction, ocean_ref[...], coef_ref, k, search_ref, up_ref, down_ref, direction_out)
    solution_out[...] = solution_ref[...] + later


def last_kernel(
    west_ref, east_ref, residual_ref, direction_ref, diag_ref, east_face_ref, north_face_ref, faces_ref, norms_ref,
    residual_out, norms_out,
):
    residual = apply_operator(
        residual_ref[...], direction_ref[...], diag_ref[...], east_face_ref[...], north_face_ref[...],
        faces_ref[0:1] * west_ref[...], faces_ref[1:2] * east_ref[...],
    )
    residual_out[...] = residual
    norms_out[...] = norms_ref[...]
    norms_out[ITERS - 1 : ITERS] = lane_partial(residual * residual)


def vmem():
    return pl.BlockSpec(memory_space=pltpu.VMEM)


def smem():
    return pl.BlockSpec(memory_space=pltpu.SMEM)


def shape(*dims):
    return jax.ShapeDtypeStruct(dims, F32)


def call(body, in_specs, outs, scratch, limit):
    return pl.pallas_call(
        body,
        in_specs=in_specs,
        out_specs=[vmem()] * len(outs),
        out_shape=outs,
        scratch_shapes=scratch,
        compiler_params=pltpu.CompilerParams(vmem_limit_bytes=limit),
    )


def exchange(up, down):
    devices = lax.axis_size("lon")
    ahead = [(i, (i + 1) % devices) for i in range(devices)]
    back = [(j, i) for i, j in ahead]
    return lax.ppermute(up, "lon", ahead), lax.ppermute(down, "lon", back)


def reduce_stages(total):
    devices = lax.axis_size("lon")
    stride = 1
    while stride < devices:
        left = devices // stride
        radix = 4 if left % 4 == 0 else 2
        parts = [
            lax.ppermute(total, "lon", [(i, i ^ (s * stride)) for i in range(devices)])
            for s in range(1, radix)
        ]
        total = functools.reduce(jnp.add, parts, total)
        stride *= radix
    return total


def on_device(
    right_side, east_coef, north_coef, surface_term, cell_mask, inverse_blocks, active_tiles, low_bound, high_bound
):
    columns, rows = right_side.shape
    tiles = inverse_blocks.shape[0]
    count = lane_blocks(rows)
    cells_all = columns * lax.axis_size("lon") * rows
    device = lax.axis_index("lon").astype(jnp.int32).reshape(1)
    field = shape(columns, rows)
    norm_shape = shape(SUBS, LANES)
    row = shape(1, rows)
    two = shape(2, rows)
    bt_shape = shape(count, columns, LANES, LANES)
    residual, direction, bt, diag, east_face, north_face, ocean, coef, up, down = call(
        first_kernel,
        [smem()] * 3 + [vmem()] * 6 + [pl.BlockSpec(memory_space=pl.ANY)],
        [field, field, bt_shape, field, field, field, field, norm_shape, two, two],
        [pltpu.VMEM(inverse_blocks.shape, F32), pltpu.SemaphoreType.DMA((count,))],
        40 * MIB,
    )(
        device, low_bound, high_bound, active_tiles.reshape(-1, LANES), right_side, east_coef, north_coef, surface_term,
        cell_mask, inverse_blocks,
    )
    west, east = exchange(up, down)
    residual, direction, answer, diag, faces, norms, up2, down2 = call(
        second_kernel,
        [vmem()] * 11,
        [field, field, field, field, two, norm_shape, row, row],
        [pltpu.VMEM((columns, rows), F32)],
        24 * MIB,
    )(west, east, residual, direction, diag, east_face, north_face, ocean, up, coef, bt)
    for k in range(2, ITERS):
        west, east = exchange(up2, down2)
        residual, direction, answer, norms, up2, down2 = call(
            functools.partial(middle_kernel, k),
            [vmem()] * 13,
            [field, field, field, norm_shape, row, row],
            [pltpu.VMEM((columns, rows), F32)],
            24 * MIB,
        )(west, east, residual, direction, answer, diag, east_face, north_face, ocean, faces, coef, norms, bt)
    west, east = exchange(up2, down2)
    residual, norms = call(last_kernel, [vmem()] * 9, [field, norm_shape], [], 24 * MIB)(
        west, east, residual, direction, diag, east_face, north_face, faces, norms
    )
    norms = reduce_stages(norms)
    return answer, residual, jnp.sum(norms[:ITERS], axis=1) / cells_all


def solution(mesh):
    in_specs = (
        P(("member", "lon"), None),
        P("lon", None),
        P("lon", None),
        P("lon", None),
        P("lon", None),
        P("lon", None, None),
        P(),
        P(),
        P(),
    )
    out_specs = (P(("member", "lon"), None), P(("member", "lon"), None), P("member"))
    return jax.shard_map(on_device, mesh=mesh, in_specs=in_specs, out_specs=out_specs, check_vma=False)
```

time: 104 us -> 58.6 us (0.56)
  blocking collectives: 30.2 us -> 0 us
  other arithmetic: 30.8 us -> 0.64 us
  starting transfers between devices: 11.7 us -> 26.4 us
  Pallas kernels: 0 us -> 8.87 us
  waiting for transfers between devices: 21 us -> 15.4 us
  between operations: 5.16 us -> 1.99 us
    psum x1 -> x0, blocking collectives: 30.2 us -> none  [on_device(): local_norms.append(lax.psum(squares, 'lon') / cells_all)]
    unnamed x4 -> x0, other arithmetic: 22.5 us -> none
    ppermute x10 -> x14, starting transfers between devices: 11.7 us -> 26.4 us  [the longest x8 18.9 us: exchange(): return (lax.ppermute(up, 'lon', ahead), lax.ppermute(down, 'lon', back))]
    pallas_call x0 -> x5, Pallas kernels: none -> 8.87 us  [the longest x1 4.68 us: on_device(): call(first_kernel, [smem()] * 3 + [vmem()] * 6 + [pl.BlockSpec(memory_spa...]
    ppermute x10 -> x14, waiting for transfers between devices: 21 us -> 15.4 us  [the longest x8 9.75 us: exchange(): return (lax.ppermute(up, 'lon', ahead), lax.ppermute(down, 'lon', back))]
    reduce_sum x5 -> x1, other arithmetic: 4.56 us -> 0.11 us  [on_device(): return (answer, residual, jnp.sum(norms[:ITERS], axis=1) / cells_all)]
    unnamed x10 -> x12, local copies, waits for them, and re-layouts: 0.45 us -> 4.88 us
    transpose x8 -> x0, local copies, waits for them, and re-layouts: 1.8 us -> none  [the longest x4 1 us: from_tiles(): return tiles.reshape(tiles_dev, columns, lat_run).transpose(1, 0, 2).resh...]
  transfers between devices with their start and end apart: 10 -> 14, of which waited for: 8 -> 10; matrix products, arithmetic and copies ran while one was open for 7% -> 0% of each run, Pallas kernels for 0% -> 0%
where the time goes in v1:
time: 58.6 us; the launch traced here: 58.2 us
  starting transfers between devices  26.4 us (45%)
  waiting for transfers between devices  15.4 us (26%)
  Pallas kernels  8.87 us (15%)
  local copies, waits for them, and re-layouts  4.88 us (8%)
  between operations  1.99 us (3%)
  other arithmetic  0.64 us (1%)
    ppermute x8, starting transfers between devices, exchange(): return (lax.ppermute(up, 'lon', ahead), lax.ppermute(down, 'lon', back))  18.9 us
    ppermute x8, waiting for transfers between devices, exchange(): return (lax.ppermute(up, 'lon', ahead), lax.ppermute(down, 'lon', back))  9.75 us
    ppermute x6, starting transfers between devices, reduce_stages(): lax.ppermute(total, 'lon', [(i, i ^ s * stride) for i in range(devices)])  7.5 us
    ppermute x6, waiting for transfers between devices, reduce_stages(): lax.ppermute(total, 'lon', [(i, i ^ s * stride) for i in range(devices)])  5.65 us
    unnamed x12, local copies, waits for them, and re-layouts  4.88 us
    pallas_call x1, Pallas kernels, on_device(): call(first_kernel, [smem()] * 3 + [vmem()] * 6 + [pl.BlockSpec(memory_spa...  4.68 us
    pallas_call x2, Pallas kernels, on_device(): call(functools.partial(middle_kernel, k), [vmem()] * 13, [field, field, f...  2.49 us
  transfers between devices with their start and end apart: 14, of which 10 were waited for; matrix products, arithmetic and copies ran while one was open for 0% of the time, Pallas kernels for 0%

profile of v1, /device:TPU:0, one launch (start us, length us, event | category | flops | bytes accessed | tf_op | source)
XLA Modules:
  0.0 58.2 jit_solution(13127369171919314661)
XLA Ops:
  1.9 0.8 %copy-done = f32[16,1024]{1,0:T(8,128)S(1)} copy-done((f32[16,1024]{1,0:T(8,128)S(1)}, f32[16,1024]{1,0:T(8,128)}, u32[]{:S(2)}) %copy-start) | copy-done | bytes 65560
  2.8 0.8 %copy-done.1 = f32[16,1024]{1,0:T(8,128)S(1)} copy-done((f32[16,1024]{1,0:T(8,128)S(1)}, f32[16,1024]{1,0:T(8,128)}, u32[]{:S(2)}) %copy-start.1) | copy-done | bytes 65560
  3.6 0.8 %copy-done.2 = f32[16,1024]{1,0:T(8,128)S(1)} copy-done((f32[16,1024]{1,0:T(8,128)S(1)}, f32[16,1024]{1,0:T(8,128)}, u32[]{:S(2)}) %copy-start.2) | copy-done | bytes 65560
  4.5 0.8 %copy-done.3 = f32[16,1024]{1,0:T(8,128)S(1)} copy-done((f32[16,1024]{1,0:T(8,128)S(1)}, f32[16,1024]{1,0:T(8,128)}, u32[]{:S(2)}) %copy-start.3) | copy-done | bytes 65560
  5.3 0.8 %copy-done.4 = s32[16,1024]{1,0:T(8,128)S(1)} copy-done((s32[16,1024]{1,0:T(8,128)S(1)}, s32[16,1024]{1,0:T(8,128)}, u32[]{:S(2)}) %copy-start.4) | copy-done | bytes 65560
  6.1 0.7 %copy-done.5 = s32[1536]{0:T(1024)S(1)} copy-done((s32[1536]{0:T(1024)S(1)}, s32[1536]{0:T(1024)}, u32[]{:S(2)}) %copy-start.5) | copy-done | bytes 6168
  6.8 4.7 %shard_map.112 = (f32[16,1024]{1,0:T(8,128)S(1)}, f32[16,1024]{1,0:T(8,128)S(1)}, f32[8,16,128,128]{3,2,1,0:T(8,128)S(1)}, f32[16,1024]{1,0:T(8,128)S(1)}, f32[1...) custom-call(s32[1]{0:T(128)} %bitcast.device_ref, ...), custom_call_target="tpu_custom_call" | custom-call | tf_op jit(solution)/shard_map/pallas_call | solution.py:275
  11.5 5.5 %collective-permute-start.1 = (f32[2,1024]{1,0:T(2,128)S(1)}, f32[2,1024]{1,0:T(2,128)S(1)}, u32[]{:S(2)}, u32[]{:S(2)}) collective-permute-start(f32[2,1024]{1,0:T(2,128)S(1)} %get-tuple-element.36), channel_id=1, source_target_pairs={{1,0},{2,1},{3,2},{4,3},{5,4},{6,5},{7,6},{8,7},{9,8},{10,9},{11,1... | collective-permute-start | bytes 24584 | tf_op jit(solution)/shard_map/ppermute | solution.py:244
  17.0 1.4 %collective-permute-done.1.east_ref = f32[2,1024]{1,0:T(2,128)S(1)} collective-permute-done((f32[2,1024]{1,0:T(2,128)S(1)}, f32[2,1024]{1,0:T(2,128)S(1)}, u32[]{:S(2)}, u32[]{:S(2)}) %collective-permute-start.1) | collective-permute-done | bytes 8224 | tf_op jit(solution)/shard_map/ppermute | solution.py:244
  18.4 4.4 %collective-permute-done.west_ref = f32[2,1024]{1,0:T(2,128)S(1)} collective-permute-done((f32[2,1024]{1,0:T(2,128)S(1)}, f32[2,1024]{1,0:T(2,128)S(1)}, u32[]{:S(2)}, u32[]{:S(2)}) %collective-permute-start) | collective-permute-done | bytes 8224 | tf_op jit(solution)/shard_map/ppermute | solution.py:244
  22.8 0.9 %shard_map.113 = (f32[16,1024]{1,0:T(8,128)S(1)}, f32[16,1024]{1,0:T(8,128)S(1)}, f32[16,1024]{1,0:T(8,128)S(1)}, f32[16,1024]{1,0:T(8,128)S(1)}, f32[2,1024]{1,...) custom-call(f32[2,1024]{1,0:T(2,128)S(1)} %collective-permute-done.west_ref, ...), custom_call_target="tpu_custom_call" | custom-call | tf_op jit(solution)/shard_map/pallas_call | solution.py:286
  23.7 0.1 collective-permute-start.2
  23.8 4.4 %collective-permute-start.3 = (f32[1,1024]{1,0:T(1,128)S(1)}, f32[1,1024]{1,0:T(1,128)S(1)}, u32[]{:S(2)}, u32[]{:S(2)}) collective-permute-start(f32[1,1024]{1,0:T(1,128)S(1)} %get-tuple-element.46), channel_id=1, source_target_pairs={{1,0},{2,1},{3,2},{4,3},{5,4},{6,5},{7,6},{8,7},{9,8},{10,9},{11,1... | collective-permute-start | bytes 12296 | tf_op jit(solution)/shard_map/ppermute | solution.py:244
  28.2 1.3 %collective-permute-done.2.west_ref = f32[1,1024]{1,0:T(1,128)S(1)} collective-permute-done((f32[1,1024]{1,0:T(1,128)S(1)}, f32[1,1024]{1,0:T(1,128)S(1)}, u32[]{:S(2)}, u32[]{:S(2)}) %collective-permute-start.2) | collective-permute-done | bytes 4128 | tf_op jit(solution)/shard_map/ppermute | solution.py:244
  29.5 0.9 %shard_map.114 = (f32[16,1024]{1,0:T(8,128)S(1)}, f32[16,1024]{1,0:T(8,128)S(1)}, f32[16,1024]{1,0:T(8,128)S(1)}, f32[8,128]{1,0:T(8,128)S(1)}, f32[1,1024]{1,0:T(1,128)S(1)}, /*index=5*/f32[1,1024]{1,0:T(1,128)S(1)}) custom-call(f32[1,1024]{1,0:T(1,128)S(1)} %collective-permute-done.2.west_ref, f32[1,1024]{1,0:T(1,128)S(1)} %collective-permute-done.3.east_ref, ...), custom_call_target="tpu_custom_call" | custom-call | tf_op jit(solution)/shard_map/pallas_call | solution.py:295
  30.5 0.1 collective-permute-start.4
  30.6 4.5 %collective-permute-start.5 = (f32[1,1024]{1,0:T(1,128)S(1)}, f32[1,1024]{1,0:T(1,128)S(1)}, u32[]{:S(2)}, u32[]{:S(2)}) collective-permute-start(f32[1,1024]{1,0:T(1,128)S(1)} %get-tuple-element.54), channel_id=1, source_target_pairs={{1,0},{2,1},{3,2},{4,3},{5,4},{6,5},{7,6},{8,7},{9,8},{10,9},{11,1... | collective-permute-start | bytes 12296 | tf_op jit(solution)/shard_map/ppermute | solution.py:244
  35.0 1.3 %collective-permute-done.4.west_ref = f32[1,1024]{1,0:T(1,128)S(1)} collective-permute-done((f32[1,1024]{1,0:T(1,128)S(1)}, f32[1,1024]{1,0:T(1,128)S(1)}, u32[]{:S(2)}, u32[]{:S(2)}) %collective-permute-start.4) | collective-permute-done | bytes 4128 | tf_op jit(solution)/shard_map/ppermute | solution.py:244
  36.3 0.1 collective-permute-done.5.east_ref
  36.3 1.5 %shard_map.115 = (f32[16,1024]{1,0:T(8,128)S(1)}, f32[16,1024]{1,0:T(8,128)S(1)}, f32[16,1024]{1,0:T(8,128)}, f32[8,128]{1,0:T(8,128)S(1)}, f32[1,1024]{1,0:T(1,128)S(1)}, /*index=5*/f32[1,1024]{1,0:T(1,128)S(1)}) custom-call(f32[1,1024]{1,0:T(1,128)S(1)} %collective-permute-done.4.west_ref, f32[1,1024]{1,0:T(1,128)S(1)} %collective-permute-done.5.east_ref, ...), custom_call_target="tpu_custom_call" | custom-call | tf_op jit(solution)/shard_map/pallas_call | solution.py:295
  37.9 4.4 %collective-permute-start.7 = (f32[1,1024]{1,0:T(1,128)S(1)}, f32[1,1024]{1,0:T(1,128)S(1)}, u32[]{:S(2)}, u32[]{:S(2)}) collective-permute-start(f32[1,1024]{1,0:T(1,128)S(1)} %get-tuple-element.61), channel_id=1, source_target_pairs={{1,0},{2,1},{3,2},{4,3},{5,4},{6,5},{7,6},{8,7},{9,8},{10,9},{11,1... | collective-permute-start | bytes 12296 | tf_op jit(solution)/shard_map/ppermute | solution.py:244
  42.3 1.3 %collective-permute-done.6.west_ref = f32[1,1024]{1,0:T(1,128)S(1)} collective-permute-done((f32[1,1024]{1,0:T(1,128)S(1)}, f32[1,1024]{1,0:T(1,128)S(1)}, u32[]{:S(2)}, u32[]{:S(2)}) %collective-permute-start.6) | collective-permute-done | bytes 4128 | tf_op jit(solution)/shard_map/ppermute | solution.py:244
  43.7 0.8 %shard_map.116 = (f32[16,1024]{1,0:T(8,128)}, f32[8,128]{1,0:T(8,128)S(1)}) custom-call(f32[1,1024]{1,0:T(1,128)S(1)} %collective-permute-done.6.west_ref, f32[1,1024]{1,0:T(1,128)S(1)} %collective-permute-done.7.east_ref, f32[16,1024]{1,0:T(8,128)S(1)} %get-tuple-element.62.residual_ref, f32[16,1024]{1,0:T(8,128)S(1)} %get-tuple-element.63.direction_ref, ...), custom_call_target="tpu_custom_call" | custom-call | tf_op jit(solution)/shard_map/pallas_call | solution.py:303
  44.4 1.9 %collective-permute-start.8 = (f32[8,128]{1,0:T(8,128)S(1)}, f32[8,128]{1,0:T(8,128)S(1)}, u32[]{:S(2)}, u32[]{:S(2)}) collective-permute-start(f32[8,128]{1,0:T(8,128)S(1)} %get-tuple-element.66), channel_id=1, source_target_pairs={{0,1},{1,0},{2,3},{3,2},{4,5},{5,4},{6,7},{7,6},{8,9},{9,8},{10,11... | collective-permute-start | bytes 12296 | tf_op jit(solution)/shard_map/ppermute | solution.py:254
  46.3 1.2 %collective-permute-done.10 = f32[8,128]{1,0:T(8,128)S(1)} collective-permute-done((f32[8,128]{1,0:T(8,128)S(1)}, f32[8,128]{1,0:T(8,128)S(1)}, u32[]{:S(2)}, u32[]{:S(2)}) %collective-permute-start.10) | collective-permute-done | bytes 4128 | tf_op jit(solution)/shard_map/ppermute | solution.py:254
  47.5 0.6 %collective-permute-done.9 = f32[8,128]{1,0:T(8,128)S(1)} collective-permute-done((f32[8,128]{1,0:T(8,128)S(1)}, f32[8,128]{1,0:T(8,128)S(1)}, u32[]{:S(2)}, u32[]{:S(2)}) %collective-permute-start.9) | collective-permute-done | bytes 4128 | tf_op jit(solution)/shard_map/ppermute | solution.py:254
  48.1 5.0 %collective-permute-start.13 = (f32[8,128]{1,0:T(8,128)S(1)}, f32[8,128]{1,0:T(8,128)S(1)}, u32[]{:S(2)}, u32[]{:S(2)}) collective-permute-start(f32[8,128]{1,0:T(8,128)S(1)} %add_add_fusion.1), channel_id=1, source_target_pairs={{0,12},{1,13},{2,14},{3,15},{4,8},{5,9},{6,10},{7,11},{8,4},{9,5},... | collective-permute-start | bytes 12296 | tf_op jit(solution)/shard_map/ppermute | solution.py:254
  53.1 0.6 %collective-permute-start.11 = (f32[8,128]{1,0:T(8,128)S(1)}, f32[8,128]{1,0:T(8,128)S(1)}, u32[]{:S(2)}, u32[]{:S(2)}) collective-permute-start(f32[8,128]{1,0:T(8,128)S(1)} %add_add_fusion.1), channel_id=1, source_target_pairs={{0,4},{1,5},{2,6},{3,7},{4,0},{5,1},{6,2},{7,3},{8,12},{9,13},{10,... | collective-permute-start | bytes 12296 | tf_op jit(solution)/shard_map/ppermute | solution.py:254
  53.7 0.9 %collective-permute-done.13 = f32[8,128]{1,0:T(8,128)S(1)} collective-permute-done((f32[8,128]{1,0:T(8,128)S(1)}, f32[8,128]{1,0:T(8,128)S(1)}, u32[]{:S(2)}, u32[]{:S(2)}) %collective-permute-start.13) | collective-permute-done | bytes 4128 | tf_op jit(solution)/shard_map/ppermute | solution.py:254
  54.7 2.9 %collective-permute-done.12 = f32[8,128]{1,0:T(8,128)S(1)} collective-permute-done((f32[8,128]{1,0:T(8,128)S(1)}, f32[8,128]{1,0:T(8,128)S(1)}, u32[]{:S(2)}, u32[]{:S(2)}) %collective-permute-start.12) | collective-permute-done | bytes 4128 | tf_op jit(solution)/shard_map/ppermute | solution.py:254
  57.6 0.1 slice_reduce_fusion
  57.7 0.5 broadcast_multiply_fusion
  (17 shorter events, 0.1 us)
Async XLA Ops:
  1.9 0.8 %copy-start = (f32[16,1024]{1,0:T(8,128)S(1)}, f32[16,1024]{1,0:T(8,128)}, u32[]{:S(2)}) copy-start(f32[16,1024]{1,0:T(8,128)} %right_ref.1) | copy-start | bytes 196612
  2.8 0.8 %copy-start.1 = (f32[16,1024]{1,0:T(8,128)S(1)}, f32[16,1024]{1,0:T(8,128)}, u32[]{:S(2)}) copy-start(f32[16,1024]{1,0:T(8,128)} %east_ref.1) | copy-start | bytes 196612
  3.6 0.8 %copy-start.2 = (f32[16,1024]{1,0:T(8,128)S(1)}, f32[16,1024]{1,0:T(8,128)}, u32[]{:S(2)}) copy-start(f32[16,1024]{1,0:T(8,128)} %north_ref.1) | copy-start | bytes 196612
  4.4 0.8 %copy-start.3 = (f32[16,1024]{1,0:T(8,128)S(1)}, f32[16,1024]{1,0:T(8,128)}, u32[]{:S(2)}) copy-start(f32[16,1024]{1,0:T(8,128)} %surface_ref.1) | copy-start | bytes 196612
  5.3 0.8 %copy-start.4 = (s32[16,1024]{1,0:T(8,128)S(1)}, s32[16,1024]{1,0:T(8,128)}, u32[]{:S(2)}) copy-start(s32[16,1024]{1,0:T(8,128)} %mask_ref.1) | copy-start | bytes 196612
  6.1 0.7 %copy-start.5 = (s32[1536]{0:T(1024)S(1)}, s32[1536]{0:T(1024)}, u32[]{:S(2)}) copy-start(s32[1536]{0:T(1024)} %param.15) | copy-start | bytes 18436
  11.5 6.9 %collective-permute-start.1 = (f32[2,1024]{1,0:T(2,128)S(1)}, f32[2,1024]{1,0:T(2,128)S(1)}, u32[]{:S(2)}, u32[]{:S(2)}) collective-permute-start(f32[2,1024]{1,0:T(2,128)S(1)} %get-tuple-element.36), channel_id=1, source_target_pairs={{1,0},{2,1},{3,2},{4,3},{5,4},{6,5},{7,6},{8,7},{9,8},{10,9},{11,1... | collective-permute-start | bytes 24584 | tf_op jit(solution)/shard_map/ppermute | solution.py:244
  17.0 5.8 %collective-permute-start = (f32[2,1024]{1,0:T(2,128)S(1)}, f32[2,1024]{1,0:T(2,128)S(1)}, u32[]{:S(2)}, u32[]{:S(2)}) collective-permute-start(f32[2,1024]{1,0:T(2,128)S(1)} %get-tuple-element.35.east_ocean_ref), channel_id=1, source_target_pairs={{0,1},{1,2},{2,3},{3,4},{4,5},{5,6},{6,7},{7,8},{8,9},{9,10},{10,1... | collective-permute-start | bytes 24584 | tf_op jit(solution)/shard_map/ppermute | solution.py:244
  23.7 5.8 %collective-permute-start.2 = (f32[1,1024]{1,0:T(1,128)S(1)}, f32[1,1024]{1,0:T(1,128)S(1)}, u32[]{:S(2)}, u32[]{:S(2)}) collective-permute-start(f32[1,1024]{1,0:T(1,128)S(1)} %get-tuple-element.45), channel_id=1, source_target_pairs={{0,1},{1,2},{2,3},{3,4},{4,5},{5,6},{6,7},{7,8},{8,9},{9,10},{10,1... | collective-permute-start | bytes 12296 | tf_op jit(solution)/shard_map/ppermute | solution.py:244
  23.8 5.8 %collective-permute-start.3 = (f32[1,1024]{1,0:T(1,128)S(1)}, f32[1,1024]{1,0:T(1,128)S(1)}, u32[]{:S(2)}, u32[]{:S(2)}) collective-permute-start(f32[1,1024]{1,0:T(1,128)S(1)} %get-tuple-element.46), channel_id=1, source_target_pairs={{1,0},{2,1},{3,2},{4,3},{5,4},{6,5},{7,6},{8,7},{9,8},{10,9},{11,1... | collective-permute-start | bytes 12296 | tf_op jit(solution)/shard_map/ppermute | solution.py:244
  30.5 5.8 %collective-permute-start.4 = (f32[1,1024]{1,0:T(1,128)S(1)}, f32[1,1024]{1,0:T(1,128)S(1)}, u32[]{:S(2)}, u32[]{:S(2)}) collective-permute-start(f32[1,1024]{1,0:T(1,128)S(1)} %get-tuple-element.53), channel_id=1, source_target_pairs={{0,1},{1,2},{2,3},{3,4},{4,5},{5,6},{6,7},{7,8},{8,9},{9,10},{10,1... | collective-permute-start | bytes 12296 | tf_op jit(solution)/shard_map/ppermute | solution.py:244
  30.6 5.8 %collective-permute-start.5 = (f32[1,1024]{1,0:T(1,128)S(1)}, f32[1,1024]{1,0:T(1,128)S(1)}, u32[]{:S(2)}, u32[]{:S(2)}) collective-permute-start(f32[1,1024]{1,0:T(1,128)S(1)} %get-tuple-element.54), channel_id=1, source_target_pairs={{1,0},{2,1},{3,2},{4,3},{5,4},{6,5},{7,6},{8,7},{9,8},{10,9},{11,1... | collective-permute-start | bytes 12296 | tf_op jit(solution)/shard_map/ppermute | solution.py:244
  37.9 5.7 %collective-permute-start.6 = (f32[1,1024]{1,0:T(1,128)S(1)}, f32[1,1024]{1,0:T(1,128)S(1)}, u32[]{:S(2)}, u32[]{:S(2)}) collective-permute-start(f32[1,1024]{1,0:T(1,128)S(1)} %get-tuple-element.60), channel_id=1, source_target_pairs={{0,1},{1,2},{2,3},{3,4},{4,5},{5,6},{6,7},{7,8},{8,9},{9,10},{10,1... | collective-permute-start | bytes 12296 | tf_op jit(solution)/shard_map/ppermute | solution.py:244
  37.9 5.8 %collective-permute-start.7 = (f32[1,1024]{1,0:T(1,128)S(1)}, f32[1,1024]{1,0:T(1,128)S(1)}, u32[]{:S(2)}, u32[]{:S(2)}) collective-permute-start(f32[1,1024]{1,0:T(1,128)S(1)} %get-tuple-element.61), channel_id=1, source_target_pairs={{1,0},{2,1},{3,2},{4,3},{5,4},{6,5},{7,6},{8,7},{9,8},{10,9},{11,1... | collective-permute-start | bytes 12296 | tf_op jit(solution)/shard_map/ppermute | solution.py:244
  44.4 3.0 %collective-permute-start.10 = (f32[8,128]{1,0:T(8,128)S(1)}, f32[8,128]{1,0:T(8,128)S(1)}, u32[]{:S(2)}, u32[]{:S(2)}) collective-permute-start(f32[8,128]{1,0:T(8,128)S(1)} %get-tuple-element.66), channel_id=1, source_target_pairs={{0,3},{1,2},{2,1},{3,0},{4,7},{5,6},{6,5},{7,4},{8,11},{9,10},{10,... | collective-permute-start | bytes 12296 | tf_op jit(solution)/shard_map/ppermute | solution.py:254
  44.4 3.6 %collective-permute-start.9 = (f32[8,128]{1,0:T(8,128)S(1)}, f32[8,128]{1,0:T(8,128)S(1)}, u32[]{:S(2)}, u32[]{:S(2)}) collective-permute-start(f32[8,128]{1,0:T(8,128)S(1)} %get-tuple-element.66), channel_id=1, source_target_pairs={{0,2},{1,3},{2,0},{3,1},{4,6},{5,7},{6,4},{7,5},{8,10},{9,11},{10,... | collective-permute-start | bytes 12296 | tf_op jit(solution)/shard_map/ppermute | solution.py:254
  44.4 3.6 %collective-permute-start.8 = (f32[8,128]{1,0:T(8,128)S(1)}, f32[8,128]{1,0:T(8,128)S(1)}, u32[]{:S(2)}, u32[]{:S(2)}) collective-permute-start(f32[8,128]{1,0:T(8,128)S(1)} %get-tuple-element.66), channel_id=1, source_target_pairs={{0,1},{1,0},{2,3},{3,2},{4,5},{5,4},{6,7},{7,6},{8,9},{9,8},{10,11... | collective-permute-start | bytes 12296 | tf_op jit(solution)/shard_map/ppermute | solution.py:254
  48.1 6.6 %collective-permute-start.13 = (f32[8,128]{1,0:T(8,128)S(1)}, f32[8,128]{1,0:T(8,128)S(1)}, u32[]{:S(2)}, u32[]{:S(2)}) collective-permute-start(f32[8,128]{1,0:T(8,128)S(1)} %add_add_fusion.1), channel_id=1, source_target_pairs={{0,12},{1,13},{2,14},{3,15},{4,8},{5,9},{6,10},{7,11},{8,4},{9,5},... | collective-permute-start | bytes 12296 | tf_op jit(solution)/shard_map/ppermute | solution.py:254
  53.1 4.5 %collective-permute-start.12 = (f32[8,128]{1,0:T(8,128)S(1)}, f32[8,128]{1,0:T(8,128)S(1)}, u32[]{:S(2)}, u32[]{:S(2)}) collective-permute-start(f32[8,128]{1,0:T(8,128)S(1)} %add_add_fusion.1), channel_id=1, source_target_pairs={{0,8},{1,9},{2,10},{3,11},{4,12},{5,13},{6,14},{7,15},{8,0},{9,1},... | collective-permute-start | bytes 12296 | tf_op jit(solution)/shard_map/ppermute | solution.py:254
  53.1 4.5 %collective-permute-start.11 = (f32[8,128]{1,0:T(8,128)S(1)}, f32[8,128]{1,0:T(8,128)S(1)}, u32[]{:S(2)}, u32[]{:S(2)}) collective-permute-start(f32[8,128]{1,0:T(8,128)S(1)} %add_add_fusion.1), channel_id=1, source_target_pairs={{0,4},{1,5},{2,6},{3,7},{4,0},{5,1},{6,2},{7,3},{8,12},{9,13},{10,... | collective-permute-start | bytes 12296 | tf_op jit(solution)/shard_map/ppermute | solution.py:254

commit v2 on v1

v2 whole, which is shorter than its diff:
```python
import functools

import jax
import jax.numpy as jnp
from jax import lax
from jax.experimental import pallas as pl
from jax.experimental.pallas import tpu as pltpu
from jax.sharding import PartitionSpec as P

ITERS = 4
LANES = 128
SUBS = 8
F32 = jnp.float32
MIB = 2**20


def lane_blocks(rows):
    return rows // LANES


def roll(x, shift, axis):
    return pltpu.roll(x, shift % x.shape[axis], axis)


def repeat_row(row, times):
    return jnp.concatenate([row] * times, axis=1)


def gather_index():
    lane = lax.broadcasted_iota(jnp.int32, (SUBS, LANES), 1)
    sub = lax.broadcasted_iota(jnp.int32, (SUBS, LANES), 0)
    return (lane // SUBS) * SUBS + sub


def expand(field, block, index):
    part = field[:, block * LANES : (block + 1) * LANES]
    rows = [
        jnp.take_along_axis(jnp.broadcast_to(part[a : a + 1], (SUBS, LANES)), index, axis=1)
        for a in range(part.shape[0])
    ]
    return jnp.concatenate(rows, axis=0)


def blocks_product(bt_ref, field, out_ref):
    index = gather_index()
    columns, rows = field.shape
    for block in range(lane_blocks(rows)):
        spread = expand(field, block, index)
        for a in range(columns):
            out_ref[a : a + 1, block * LANES : (block + 1) * LANES] = jnp.sum(
                bt_ref[block, a] * spread, axis=0, keepdims=True
            )


def even_device():
    return lax.rem(lax.axis_index("lon"), 2) == 0


def store_edges(inner_ref, outer_ref, row, even, first, last):
    inner_ref[row : row + 1] = jnp.where(even, last, first)
    outer_ref[row : row + 1] = jnp.where(even, first, last)


def halo_rows(inner_ref, outer_ref, row, even):
    inner, outer = inner_ref[row : row + 1], outer_ref[row : row + 1]
    return jnp.where(even, outer, inner), jnp.where(even, inner, outer)


def lane_partial(squares):
    total = jnp.sum(squares, axis=0, keepdims=True)
    parts = [total[:, i * LANES : (i + 1) * LANES] for i in range(total.shape[1] // LANES)]
    return functools.reduce(jnp.add, parts)


def tile_flags(active_ref, first, tiles):
    active = active_ref[...]
    before = jnp.sum((active < first).astype(jnp.int32))
    row = jnp.minimum(before // LANES, active_ref.shape[0] - 2)
    lane = lax.broadcasted_iota(jnp.int32, (LANES, tiles), 1) + first
    found = jnp.zeros((LANES, tiles), jnp.int32)
    for step in range(2):
        entries = jnp.broadcast_to(active_ref[pl.ds(row + step, 1), :], (LANES, LANES))
        found = found + (entries.T == lane).astype(jnp.int32)
    return (jnp.sum(found, axis=0, keepdims=True) > 0).astype(F32)


def transpose_kernel(blocks_hbm, bt_ref, raw, sems):
    count, columns = bt_ref.shape[:2]
    step = blocks_hbm.shape[0] // count

    def fetch(i):
        part = pl.ds(i * step, step)
        return pltpu.make_async_copy(blocks_hbm.at[part], raw.at[part], sems.at[i])

    for i in range(count):
        fetch(i).start()
    for i in range(count):
        fetch(i).wait()
        for a in range(columns):
            bt_ref[i, a] = raw[i * step : (i + 1) * step, a * SUBS : (a + 1) * SUBS, :].reshape(LANES, LANES).T


def first_kernel(
    low_ref, high_ref, active_ref, right_ref, east_ref, north_ref, surface_ref, mask_ref, bt_ref,
    residual_ref, direction_ref, diag_ref, east_face_ref, north_face_ref, ocean_ref, east_end_ref, coef_ref, inner_ref, outer_ref,
):
    columns, rows = right_ref.shape
    count = lane_blocks(rows)
    tiles = rows // SUBS
    even = even_device()
    low = jnp.broadcast_to(low_ref[...].reshape(1, 1), (1, LANES))
    high = jnp.broadcast_to(high_ref[...].reshape(1, 1), (1, LANES))
    center = (high + low) / 2.0
    radius = (high - low) / 2.0
    ratio = center / radius
    weight_prev = 1.0 / ratio
    coef_ref[0:1] = 1.0 / center
    for k in range(1, ITERS):
        weight = 1.0 / (2.0 * ratio - weight_prev)
        coef_ref[2 * k : 2 * k + 1] = weight * weight_prev
        coef_ref[2 * k + 1 : 2 * k + 2] = 2.0 * weight / radius
        weight_prev = weight
    flags = tile_flags(active_ref, lax.axis_index("lon") * tiles, tiles)
    lane = lax.broadcasted_iota(jnp.int32, (SUBS, LANES), 1)
    spread = [
        jnp.take_along_axis(jnp.broadcast_to(flags, (SUBS, tiles)), i * (LANES // SUBS) + lane // SUBS, axis=1)
        for i in range(count)
    ]
    flag_lat = jnp.concatenate(spread, axis=1)[0:1]
    ocean = mask_ref[...].astype(F32) * flag_lat
    ocean_ref[...] = ocean
    lat = lax.broadcasted_iota(jnp.int32, (columns, rows), 1)
    lon = lax.broadcasted_iota(jnp.int32, (columns, rows), 0)
    east_ocean = east_ref[...] * ocean
    east_face = jnp.where(lon < columns - 1, east_ocean * roll(ocean, -1, 0), 0.0)
    north_face = jnp.where(lat < rows - 1, north_ref[...] * ocean * roll(ocean, -1, 1), 0.0)
    east_face_ref[...] = east_face
    north_face_ref[...] = north_face
    diag_ref[...] = surface_ref[...] * ocean + east_face + roll(east_face, 1, 0) + north_face + roll(north_face, 1, 1)
    residual = right_ref[...] * ocean
    residual_ref[...] = residual
    east_end_ref[...] = east_ocean[columns - 1 :]
    store_edges(inner_ref, outer_ref, 1, even, ocean[0:1], east_ocean[columns - 1 :])
    blocks_product(bt_ref, residual, direction_ref)
    direction = direction_ref[...] * ocean * repeat_row(coef_ref[0:1], count)
    direction_ref[...] = direction
    store_edges(inner_ref, outer_ref, 0, even, direction[0:1], direction[columns - 1 :])


def apply_operator(residual, direction, diag, east_face, north_face, west_term, east_term):
    flow = diag * direction
    flow = flow - east_face * roll(direction, -1, 0) - roll(east_face, 1, 0) * roll(direction, 1, 0)
    flow = flow - north_face * roll(direction, -1, 1) - roll(north_face, 1, 1) * roll(direction, 1, 1)
    lon = lax.broadcasted_iota(jnp.int32, residual.shape, 0)
    flow = jnp.where(lon == 0, flow - west_term, flow)
    flow = jnp.where(lon == residual.shape[0] - 1, flow - east_term, flow)
    return residual - flow


def search_step(bt_ref, residual, direction, ocean, coef_ref, k, search_ref, inner_out, outer_out, direction_out):
    count = lane_blocks(residual.shape[1])
    blocks_product(bt_ref, residual, search_ref)
    keep = repeat_row(coef_ref[2 * k : 2 * k + 1], count)
    gain = repeat_row(coef_ref[2 * k + 1 : 2 * k + 2], count)
    direction = keep * direction + gain * (ocean * search_ref[...])
    direction_out[...] = direction
    store_edges(inner_out, outer_out, 0, even_device(), direction[0:1], direction[-1:])
    return direction


def second_kernel(
    inner_ref, outer_ref, residual_ref, direction_ref, diag_ref, east_face_ref, north_face_ref, ocean_ref, east_end_ref, coef_ref, bt_ref,
    residual_out, direction_out, solution_out, diag_out, faces_out, norms_out, inner_out, outer_out,
    search_ref,
):
    ocean = ocean_ref[...]
    direction = direction_ref[...]
    columns = ocean.shape[0]
    even = even_device()
    west, east = halo_rows(inner_ref, outer_ref, 0, even)
    west_static, east_static = halo_rows(inner_ref, outer_ref, 1, even)
    west_face = west_static * ocean[0:1]
    east_end = east_end_ref[...] * east_static
    faces_out[0:1] = west_face
    faces_out[1:2] = east_end
    lon = lax.broadcasted_iota(jnp.int32, ocean.shape, 0)
    diag = diag_ref[...]
    diag = jnp.where(lon == 0, diag + west_face, diag)
    diag = jnp.where(lon == columns - 1, diag + east_end, diag)
    diag_out[...] = diag
    residual = apply_operator(
        residual_ref[...], direction, diag, east_face_ref[...], north_face_ref[...],
        west_face * west, east_end * east,
    )
    residual_out[...] = residual
    norms_out[...] = jnp.zeros_like(norms_out)
    norms_out[0:1] = lane_partial(residual * residual)
    later = search_step(bt_ref, residual, direction, ocean, coef_ref, 1, search_ref, inner_out, outer_out, direction_out)
    solution_out[...] = direction + later


def middle_kernel(
    k,
    inner_ref, outer_ref, residual_ref, direction_ref, solution_ref, diag_ref, east_face_ref, north_face_ref, ocean_ref, faces_ref, coef_ref, norms_ref, bt_ref,
    residual_out, direction_out, solution_out, norms_out, inner_out, outer_out,
    search_ref,
):
    direction = direction_ref[...]
    west, east = halo_rows(inner_ref, outer_ref, 0, even_device())
    residual = apply_operator(
        residual_ref[...], direction, diag_ref[...], east_face_ref[...], north_face_ref[...],
        faces_ref[0:1] * west, faces_ref[1:2] * east,
    )
    residual_out[...] = residual
    norms_out[...] = norms_ref[...]
    norms_out[k - 1 : k] = lane_partial(residual * residual)
    later = search_step(bt_ref, residual, direction, ocean_ref[...], coef_ref, k, search_ref, inner_out, outer_out, direction_out)
    solution_out[...] = solution_ref[...] + later


def last_kernel(
    inner_ref, outer_ref, residual_ref, direction_ref, diag_ref, east_face_ref, north_face_ref, faces_ref, norms_ref,
    residual_out, norms_out,
):
    west, east = halo_rows(inner_ref, outer_ref, 0, even_device())
    residual = apply_operator(
        residual_ref[...], direction_ref[...], diag_ref[...], east_face_ref[...], north_face_ref[...],
        faces_ref[0:1] * west, faces_ref[1:2] * east,
    )
    residual_out[...] = residual
    norms_out[...] = norms_ref[...]
    norms_out[ITERS - 1 : ITERS] = lane_partial(residual * residual)


def vmem():
    return pl.BlockSpec(memory_space=pltpu.VMEM)


def shape(*dims):
    return jax.ShapeDtypeStruct(dims, F32)


def call(body, in_specs, outs, scratch, limit, cost=None):
    return pl.pallas_call(
        body,
        in_specs=in_specs,
        out_specs=[vmem()] * len(outs),
        out_shape=outs,
        scratch_shapes=scratch,
        compiler_params=pltpu.CompilerParams(vmem_limit_bytes=limit),
        cost_estimate=cost,
    )


def exchange(inner, outer):
    devices = lax.axis_size("lon")
    pairs = [(i, i ^ 1) for i in range(devices)]
    across = [(i, (i + 1 if i % 2 else i - 1) % devices) for i in range(devices)]
    return lax.ppermute(inner, "lon", pairs), lax.ppermute(outer, "lon", across)


def reduce_stages(total):
    devices = lax.axis_size("lon")
    stride = 1
    while stride < devices:
        left = devices // stride
        radix = 4 if left % 4 == 0 else 2
        parts = [
            lax.ppermute(total, "lon", [(i, i ^ (s * stride)) for i in range(devices)])
            for s in range(1, radix)
        ]
        total = functools.reduce(jnp.add, parts, total)
        stride *= radix
    return total


def on_device(
    right_side, east_coef, north_coef, surface_term, cell_mask, inverse_blocks, active_tiles, low_bound, high_bound
):
    columns, rows = right_side.shape
    tiles = inverse_blocks.shape[0]
    count = lane_blocks(rows)
    cells_all = columns * lax.axis_size("lon") * rows
    field = shape(columns, rows)
    norm_shape = shape(SUBS, LANES)
    row = shape(1, rows)
    two = shape(2, rows)
    bt_shape = shape(count, columns, LANES, LANES)
    (bt,) = call(
        transpose_kernel,
        [pl.BlockSpec(memory_space=pl.ANY)],
        [bt_shape],
        [pltpu.VMEM(inverse_blocks.shape, F32), pltpu.SemaphoreType.DMA((count,))],
        40 * MIB,
        pl.CostEstimate(flops=10**9, bytes_accessed=2 * inverse_blocks.size * 4, transcendentals=0),
    )(inverse_blocks)
    residual, direction, diag, east_face, north_face, ocean, east_end, coef, inner, outer = call(
        first_kernel,
        [vmem()] * 9,
        [field, field, field, field, field, field, row, norm_shape, two, two],
        [],
        24 * MIB,
    )(
        low_bound, high_bound, active_tiles.reshape(-1, LANES),
        right_side, east_coef, north_coef, surface_term, cell_mask, bt,
    )
    inner, outer = exchange(inner, outer)
    residual, direction, answer, diag, faces, norms, inner, outer = call(
        second_kernel,
        [vmem()] * 11,
        [field, field, field, field, two, norm_shape, row, row],
        [pltpu.VMEM((columns, rows), F32)],
        24 * MIB,
    )(inner, outer, residual, direction, diag, east_face, north_face, ocean, east_end, coef, bt)
    for k in range(2, ITERS):
        inner, outer = exchange(inner, outer)
        residual, direction, answer, norms, inner, outer = call(
            functools.partial(middle_kernel, k),
            [vmem()] * 13,
            [field, field, field, norm_shape, row, row],
            [pltpu.VMEM((columns, rows), F32)],
            24 * MIB,
        )(inner, outer, residual, direction, answer, diag, east_face, north_face, ocean, faces, coef, norms, bt)
    inner, outer = exchange(inner, outer)
    residual, norms = call(last_kernel, [vmem()] * 9, [field, norm_shape], [], 24 * MIB)(
        inner, outer, residual, direction, diag, east_face, north_face, faces, norms
    )
    norms = reduce_stages(norms)
    return answer, residual, jnp.sum(norms[:ITERS], axis=1) / cells_all


def solution(mesh):
    in_specs = (
        P(("member", "lon"), None),
        P("lon", None),
        P("lon", None),
        P("lon", None),
        P("lon", None),
        P("lon", None, None),
        P(),
        P(),
        P(),
    )
    out_specs = (P(("member", "lon"), None), P(("member", "lon"), None), P("member"))
    return jax.shard_map(on_device, mesh=mesh, in_specs=in_specs, out_specs=out_specs, check_vma=False)
```

time: 58.6 us -> 50.5 us (0.86)
  local copies, waits for them, and re-layouts: 4.88 us -> 0.03 us
  waiting for transfers between devices: 15.4 us -> 11 us
  starting transfers between devices: 26.4 us -> 27.2 us
    unnamed x12, local copies, waits for them, and re-layouts: 4.88 us -> 0.03 us
    ppermute x8, waiting for transfers between devices: 9.75 us -> 5.35 us  [the longest x4 5.34 us: exchange(): lax.ppermute(outer, 'lon', across)]
    ppermute x8, starting transfers between devices: 18.9 us -> 19.7 us  [the longest x4 19 us: exchange(): lax.ppermute(outer, 'lon', across)]
    pallas_call x1 -> x2, Pallas kernels: 4.68 us -> 5.29 us  [the longest x1 4.08 us: on_device(): call(transpose_kernel, [pl.BlockSpec(memory_space=pl.ANY)], [bt_shape], [...]
  transfers between devices with their start and end apart: 14 -> 14, of which waited for: 10 -> 8; matrix products, arithmetic and copies ran while one was open for 0% -> 0% of each run, Pallas kernels for 0% -> 0%
where the time goes in v2:
time: 50.5 us; the launch traced here: 50.3 us
  starting transfers between devices  27.2 us (54%)
  waiting for transfers between devices  11 us (22%)
  Pallas kernels  9.45 us (19%)
  between operations  2.07 us (4%)
  other arithmetic  0.64 us (1%)
    ppermute x4, starting transfers between devices, exchange(): lax.ppermute(outer, 'lon', across)  19 us
    ppermute x6, starting transfers between devices, reduce_stages(): lax.ppermute(total, 'lon', [(i, i ^ s * stride) for i in range(devices)])  7.5 us
    ppermute x6, waiting for transfers between devices, reduce_stages(): lax.ppermute(total, 'lon', [(i, i ^ s * stride) for i in range(devices)])  5.65 us
    ppermute x4, waiting for transfers between devices, exchange(): lax.ppermute(outer, 'lon', across)  5.34 us
    pallas_call x1, Pallas kernels, on_device(): call(transpose_kernel, [pl.BlockSpec(memory_space=pl.ANY)], [bt_shape], [...  4.08 us
    pallas_call x2, Pallas kernels, on_device(): call(functools.partial(middle_kernel, k), [vmem()] * 13, [field, field, f...  2.47 us
    pallas_call x1, Pallas kernels, on_device(): call(first_kernel, [vmem()] * 9, [field, field, field, field, field, fiel...  1.22 us
  transfers between devices with their start and end apart: 14, of which 8 were waited for; matrix products, arithmetic and copies ran while one was open for 0% of the time, Pallas kernels for 0%

profile of v2, /device:TPU:0, one launch (start us, length us, event | category | flops | bytes accessed | tf_op | source)
XLA Modules:
  0.0 50.3 jit_solution(6591057064570709139)
XLA Ops:
  2.0 4.1 %shard_map.112.bt_ref = f32[8,16,128,128]{3,2,1,0:T(8,128)S(1)} custom-call(f32[128,128,128]{2,1,0:T(8,128)} %blocks_hbm.1), custom_call_target="tpu_custom_call" | custom-call | flops 1000000000 | bytes 16777216 | tf_op jit(solution)/shard_map/pallas_call | solution.py:289
  6.1 1.2 %shard_map.113 = (f32[16,1024]{1,0:T(8,128)S(1)}, f32[16,1024]{1,0:T(8,128)S(1)}, f32[16,1024]{1,0:T(8,128)S(1)}, f32[16,1024]{1,0:T(8,128)S(1)}, f32[16,1024]{1...) custom-call(f32[1]{0:T(128)S(6)} %copy.12.low_ref, ...), custom_call_target="tpu_custom_call" | custom-call | tf_op jit(solution)/shard_map/pallas_call | solution.py:297
  7.3 0.5 %collective-permute-start = (f32[2,1024]{1,0:T(2,128)S(1)}, f32[2,1024]{1,0:T(2,128)S(1)}, u32[]{:S(2)}, u32[]{:S(2)}) collective-permute-start(f32[2,1024]{1,0:T(2,128)S(1)} %get-tuple-element.35), channel_id=1, source_target_pairs={{0,1},{1,0},{2,3},{3,2},{4,5},{5,4},{6,7},{7,6},{8,9},{9,8},{10,11... | collective-permute-start | bytes 24584 | tf_op jit(solution)/shard_map/ppermute | solution.py:259
  7.9 5.7 %collective-permute-start.1 = (f32[2,1024]{1,0:T(2,128)S(1)}, f32[2,1024]{1,0:T(2,128)S(1)}, u32[]{:S(2)}, u32[]{:S(2)}) collective-permute-start(f32[2,1024]{1,0:T(2,128)S(1)} %get-tuple-element.36), channel_id=1, source_target_pairs={{0,15},{1,2},{2,1},{3,4},{4,3},{5,6},{6,5},{7,8},{8,7},{9,10},{10,... | collective-permute-start | bytes 24584 | tf_op jit(solution)/shard_map/ppermute | solution.py:259
  13.5 0.0 collective-permute-done.inner_ref
  13.5 1.4 %collective-permute-done.1.outer_ref = f32[2,1024]{1,0:T(2,128)S(1)} collective-permute-done((f32[2,1024]{1,0:T(2,128)S(1)}, f32[2,1024]{1,0:T(2,128)S(1)}, u32[]{:S(2)}, u32[]{:S(2)}) %collective-permute-start.1) | collective-permute-done | bytes 8224 | tf_op jit(solution)/shard_map/ppermute | solution.py:259
  14.9 0.9 %shard_map.114 = (f32[16,1024]{1,0:T(8,128)S(1)}, f32[16,1024]{1,0:T(8,128)S(1)}, f32[16,1024]{1,0:T(8,128)S(1)}, f32[16,1024]{1,0:T(8,128)S(1)}, f32[2,1024]{1,...) custom-call(f32[2,1024]{1,0:T(2,128)S(1)} %collective-permute-done.inner_ref, ...), custom_call_target="tpu_custom_call" | custom-call | tf_op jit(solution)/shard_map/pallas_call | solution.py:308
  15.8 0.1 collective-permute-start.2
  15.9 4.5 %collective-permute-start.3 = (f32[1,1024]{1,0:T(1,128)S(1)}, f32[1,1024]{1,0:T(1,128)S(1)}, u32[]{:S(2)}, u32[]{:S(2)}) collective-permute-start(f32[1,1024]{1,0:T(1,128)S(1)} %get-tuple-element.46), channel_id=1, source_target_pairs={{0,15},{1,2},{2,1},{3,4},{4,3},{5,6},{6,5},{7,8},{8,7},{9,10},{10,... | collective-permute-start | bytes 12296 | tf_op jit(solution)/shard_map/ppermute | solution.py:259
  20.4 1.3 %collective-permute-done.3.outer_ref = f32[1,1024]{1,0:T(1,128)S(1)} collective-permute-done((f32[1,1024]{1,0:T(1,128)S(1)}, f32[1,1024]{1,0:T(1,128)S(1)}, u32[]{:S(2)}, u32[]{:S(2)}) %collective-permute-start.3) | collective-permute-done | bytes 4128 | tf_op jit(solution)/shard_map/ppermute | solution.py:259
  21.7 0.9 %shard_map.115 = (f32[16,1024]{1,0:T(8,128)S(1)}, f32[16,1024]{1,0:T(8,128)S(1)}, f32[16,1024]{1,0:T(8,128)S(1)}, f32[8,128]{1,0:T(8,128)S(1)}, f32[1,1024]{1,0:T(1,128)S(1)}, /*index=5*/f32[1,1024]{1,0:T(1,128)S(1)}) custom-call(f32[1,1024]{1,0:T(1,128)S(1)} %collective-permute-done.2.inner_ref, f32[1,1024]{1,0:T(1,128)S(1)} %collective-permute-done.3.outer_ref, ...), custom_call_target="tpu_custom_call" | custom-call | tf_op jit(solution)/shard_map/pallas_call | solution.py:317
  22.6 0.1 collective-permute-start.4
  22.7 4.5 %collective-permute-start.5 = (f32[1,1024]{1,0:T(1,128)S(1)}, f32[1,1024]{1,0:T(1,128)S(1)}, u32[]{:S(2)}, u32[]{:S(2)}) collective-permute-start(f32[1,1024]{1,0:T(1,128)S(1)} %get-tuple-element.54), channel_id=1, source_target_pairs={{0,15},{1,2},{2,1},{3,4},{4,3},{5,6},{6,5},{7,8},{8,7},{9,10},{10,... | collective-permute-start | bytes 12296 | tf_op jit(solution)/shard_map/ppermute | solution.py:259
  27.2 0.0 collective-permute-done.4.inner_ref
  27.2 1.3 %collective-permute-done.5.outer_ref = f32[1,1024]{1,0:T(1,128)S(1)} collective-permute-done((f32[1,1024]{1,0:T(1,128)S(1)}, f32[1,1024]{1,0:T(1,128)S(1)}, u32[]{:S(2)}, u32[]{:S(2)}) %collective-permute-start.5) | collective-permute-done | bytes 4128 | tf_op jit(solution)/shard_map/ppermute | solution.py:259
  28.5 1.5 %shard_map.116 = (f32[16,1024]{1,0:T(8,128)S(1)}, f32[16,1024]{1,0:T(8,128)S(1)}, f32[16,1024]{1,0:T(8,128)}, f32[8,128]{1,0:T(8,128)S(1)}, f32[1,1024]{1,0:T(1,128)S(1)}, /*index=5*/f32[1,1024]{1,0:T(1,128)S(1)}) custom-call(f32[1,1024]{1,0:T(1,128)S(1)} %collective-permute-done.4.inner_ref, f32[1,1024]{1,0:T(1,128)S(1)} %collective-permute-done.5.outer_ref, ...), custom_call_target="tpu_custom_call" | custom-call | tf_op jit(solution)/shard_map/pallas_call | solution.py:317
  30.1 0.0 collective-permute-start.6
  30.1 4.4 %collective-permute-start.7 = (f32[1,1024]{1,0:T(1,128)S(1)}, f32[1,1024]{1,0:T(1,128)S(1)}, u32[]{:S(2)}, u32[]{:S(2)}) collective-permute-start(f32[1,1024]{1,0:T(1,128)S(1)} %get-tuple-element.61), channel_id=1, source_target_pairs={{0,15},{1,2},{2,1},{3,4},{4,3},{5,6},{6,5},{7,8},{8,7},{9,10},{10,... | collective-permute-start | bytes 12296 | tf_op jit(solution)/shard_map/ppermute | solution.py:259
  34.5 0.0 collective-permute-done.6.inner_ref
  34.5 1.3 %collective-permute-done.7.outer_ref = f32[1,1024]{1,0:T(1,128)S(1)} collective-permute-done((f32[1,1024]{1,0:T(1,128)S(1)}, f32[1,1024]{1,0:T(1,128)S(1)}, u32[]{:S(2)}, u32[]{:S(2)}) %collective-permute-start.7) | collective-permute-done | bytes 4128 | tf_op jit(solution)/shard_map/ppermute | solution.py:259
  35.8 0.8 %shard_map.117 = (f32[16,1024]{1,0:T(8,128)}, f32[8,128]{1,0:T(8,128)S(1)}) custom-call(f32[1,1024]{1,0:T(1,128)S(1)} %collective-permute-done.6.inner_ref, f32[1,1024]{1,0:T(1,128)S(1)} %collective-permute-done.7.outer_ref, f32[16,1024]{1,0:T(8,128)S(1)} %get-tuple-element.62.residual_ref, f32[16,1024]{1,0:T(8,128)S(1)} %get-tuple-element.63.direction_ref, ...), custom_call_target="tpu_custom_call" | custom-call | tf_op jit(solution)/shard_map/pallas_call | solution.py:325
  36.5 0.0 collective-permute-start.10
  36.5 0.0 collective-permute-start.9
  36.6 1.9 %collective-permute-start.8 = (f32[8,128]{1,0:T(8,128)S(1)}, f32[8,128]{1,0:T(8,128)S(1)}, u32[]{:S(2)}, u32[]{:S(2)}) collective-permute-start(f32[8,128]{1,0:T(8,128)S(1)} %get-tuple-element.66), channel_id=1, source_target_pairs={{0,1},{1,0},{2,3},{3,2},{4,5},{5,4},{6,7},{7,6},{8,9},{9,8},{10,11... | collective-permute-start | bytes 12296 | tf_op jit(solution)/shard_map/ppermute | solution.py:269
  38.4 1.2 %collective-permute-done.10 = f32[8,128]{1,0:T(8,128)S(1)} collective-permute-done((f32[8,128]{1,0:T(8,128)S(1)}, f32[8,128]{1,0:T(8,128)S(1)}, u32[]{:S(2)}, u32[]{:S(2)}) %collective-permute-start.10) | collective-permute-done | bytes 4128 | tf_op jit(solution)/shard_map/ppermute | solution.py:269
  39.6 0.6 %collective-permute-done.9 = f32[8,128]{1,0:T(8,128)S(1)} collective-permute-done((f32[8,128]{1,0:T(8,128)S(1)}, f32[8,128]{1,0:T(8,128)S(1)}, u32[]{:S(2)}, u32[]{:S(2)}) %collective-permute-start.9) | collective-permute-done | bytes 4128 | tf_op jit(solution)/shard_map/ppermute | solution.py:269
  40.2 5.0 %collective-permute-start.13 = (f32[8,128]{1,0:T(8,128)S(1)}, f32[8,128]{1,0:T(8,128)S(1)}, u32[]{:S(2)}, u32[]{:S(2)}) collective-permute-start(f32[8,128]{1,0:T(8,128)S(1)} %add_add_fusion.1), channel_id=1, source_target_pairs={{0,12},{1,13},{2,14},{3,15},{4,8},{5,9},{6,10},{7,11},{8,4},{9,5},... | collective-permute-start | bytes 12296 | tf_op jit(solution)/shard_map/ppermute | solution.py:269
  45.2 0.6 %collective-permute-start.11 = (f32[8,128]{1,0:T(8,128)S(1)}, f32[8,128]{1,0:T(8,128)S(1)}, u32[]{:S(2)}, u32[]{:S(2)}) collective-permute-start(f32[8,128]{1,0:T(8,128)S(1)} %add_add_fusion.1), channel_id=1, source_target_pairs={{0,4},{1,5},{2,6},{3,7},{4,0},{5,1},{6,2},{7,3},{8,12},{9,13},{10,... | collective-permute-start | bytes 12296 | tf_op jit(solution)/shard_map/ppermute | solution.py:269
  45.8 0.9 %collective-permute-done.13 = f32[8,128]{1,0:T(8,128)S(1)} collective-permute-done((f32[8,128]{1,0:T(8,128)S(1)}, f32[8,128]{1,0:T(8,128)S(1)}, u32[]{:S(2)}, u32[]{:S(2)}) %collective-permute-start.13) | collective-permute-done | bytes 4128 | tf_op jit(solution)/shard_map/ppermute | solution.py:269
  46.8 2.9 %collective-permute-done.12 = f32[8,128]{1,0:T(8,128)S(1)} collective-permute-done((f32[8,128]{1,0:T(8,128)S(1)}, f32[8,128]{1,0:T(8,128)S(1)}, u32[]{:S(2)}, u32[]{:S(2)}) %collective-permute-start.12) | collective-permute-done | bytes 4128 | tf_op jit(solution)/shard_map/ppermute | solution.py:269
  49.7 0.1 slice_reduce_fusion
  49.8 0.5 %broadcast_multiply_fusion = f32[4]{0:T(128)} fusion(f32[4]{0:T(128)S(1)} %slice_reduce_fusion), kind=kLoop, calls=%fused_computation.3 | loop fusion | flops 4 | bytes 32 | tf_op jit(solution)/shard_map/div | solution.py:329
  (18 shorter events, 0.0 us)
Async XLA Ops:
  1.9 4.1 %copy-start = (f32[16,1024]{1,0:T(8,128)S(1)}, f32[16,1024]{1,0:T(8,128)}, u32[]{:S(2)}) copy-start(f32[16,1024]{1,0:T(8,128)} %right_ref.1) | copy-start | bytes 196612
  1.9 4.1 %copy-start.1 = (f32[16,1024]{1,0:T(8,128)S(1)}, f32[16,1024]{1,0:T(8,128)}, u32[]{:S(2)}) copy-start(f32[16,1024]{1,0:T(8,128)} %east_ref.1) | copy-start | bytes 196612
  1.9 4.1 %copy-start.2 = (f32[16,1024]{1,0:T(8,128)S(1)}, f32[16,1024]{1,0:T(8,128)}, u32[]{:S(2)}) copy-start(f32[16,1024]{1,0:T(8,128)} %north_ref.1) | copy-start | bytes 196612
  2.0 4.1 %copy-start.3 = (f32[16,1024]{1,0:T(8,128)S(1)}, f32[16,1024]{1,0:T(8,128)}, u32[]{:S(2)}) copy-start(f32[16,1024]{1,0:T(8,128)} %surface_ref.1) | copy-start | bytes 196612
  2.0 4.1 %copy-start.4 = (s32[16,1024]{1,0:T(8,128)S(1)}, s32[16,1024]{1,0:T(8,128)}, u32[]{:S(2)}) copy-start(s32[16,1024]{1,0:T(8,128)} %mask_ref.1) | copy-start | bytes 196612
  2.0 4.1 %copy-start.5 = (s32[1536]{0:T(1024)S(1)}, s32[1536]{0:T(1024)}, u32[]{:S(2)}) copy-start(s32[1536]{0:T(1024)} %param.15) | copy-start | bytes 18436
  7.3 6.2 %collective-permute-start = (f32[2,1024]{1,0:T(2,128)S(1)}, f32[2,1024]{1,0:T(2,128)S(1)}, u32[]{:S(2)}, u32[]{:S(2)}) collective-permute-start(f32[2,1024]{1,0:T(2,128)S(1)} %get-tuple-element.35), channel_id=1, source_target_pairs={{0,1},{1,0},{2,3},{3,2},{4,5},{5,4},{6,7},{7,6},{8,9},{9,8},{10,11... | collective-permute-start | bytes 24584 | tf_op jit(solution)/shard_map/ppermute | solution.py:259
  7.9 7.0 %collective-permute-start.1 = (f32[2,1024]{1,0:T(2,128)S(1)}, f32[2,1024]{1,0:T(2,128)S(1)}, u32[]{:S(2)}, u32[]{:S(2)}) collective-permute-start(f32[2,1024]{1,0:T(2,128)S(1)} %get-tuple-element.36), channel_id=1, source_target_pairs={{0,15},{1,2},{2,1},{3,4},{4,3},{5,6},{6,5},{7,8},{8,7},{9,10},{10,... | collective-permute-start | bytes 24584 | tf_op jit(solution)/shard_map/ppermute | solution.py:259
  15.8 4.6 %collective-permute-start.2 = (f32[1,1024]{1,0:T(1,128)S(1)}, f32[1,1024]{1,0:T(1,128)S(1)}, u32[]{:S(2)}, u32[]{:S(2)}) collective-permute-start(f32[1,1024]{1,0:T(1,128)S(1)} %get-tuple-element.45), channel_id=1, source_target_pairs={{0,1},{1,0},{2,3},{3,2},{4,5},{5,4},{6,7},{7,6},{8,9},{9,8},{10,11... | collective-permute-start | bytes 12296 | tf_op jit(solution)/shard_map/ppermute | solution.py:259
  15.9 5.8 %collective-permute-start.3 = (f32[1,1024]{1,0:T(1,128)S(1)}, f32[1,1024]{1,0:T(1,128)S(1)}, u32[]{:S(2)}, u32[]{:S(2)}) collective-permute-start(f32[1,1024]{1,0:T(1,128)S(1)} %get-tuple-element.46), channel_id=1, source_target_pairs={{0,15},{1,2},{2,1},{3,4},{4,3},{5,6},{6,5},{7,8},{8,7},{9,10},{10,... | collective-permute-start | bytes 12296 | tf_op jit(solution)/shard_map/ppermute | solution.py:259
  22.6 4.5 %collective-permute-start.4 = (f32[1,1024]{1,0:T(1,128)S(1)}, f32[1,1024]{1,0:T(1,128)S(1)}, u32[]{:S(2)}, u32[]{:S(2)}) collective-permute-start(f32[1,1024]{1,0:T(1,128)S(1)} %get-tuple-element.53), channel_id=1, source_target_pairs={{0,1},{1,0},{2,3},{3,2},{4,5},{5,4},{6,7},{7,6},{8,9},{9,8},{10,11... | collective-permute-start | bytes 12296 | tf_op jit(solution)/shard_map/ppermute | solution.py:259
  22.7 5.8 %collective-permute-start.5 = (f32[1,1024]{1,0:T(1,128)S(1)}, f32[1,1024]{1,0:T(1,128)S(1)}, u32[]{:S(2)}, u32[]{:S(2)}) collective-permute-start(f32[1,1024]{1,0:T(1,128)S(1)} %get-tuple-element.54), channel_id=1, source_target_pairs={{0,15},{1,2},{2,1},{3,4},{4,3},{5,6},{6,5},{7,8},{8,7},{9,10},{10,... | collective-permute-start | bytes 12296 | tf_op jit(solution)/shard_map/ppermute | solution.py:259
  30.1 4.4 %collective-permute-start.6 = (f32[1,1024]{1,0:T(1,128)S(1)}, f32[1,1024]{1,0:T(1,128)S(1)}, u32[]{:S(2)}, u32[]{:S(2)}) collective-permute-start(f32[1,1024]{1,0:T(1,128)S(1)} %get-tuple-element.60), channel_id=1, source_target_pairs={{0,1},{1,0},{2,3},{3,2},{4,5},{5,4},{6,7},{7,6},{8,9},{9,8},{10,11... | collective-permute-start | bytes 12296 | tf_op jit(solution)/shard_map/ppermute | solution.py:259
  30.1 5.7 %collective-permute-start.7 = (f32[1,1024]{1,0:T(1,128)S(1)}, f32[1,1024]{1,0:T(1,128)S(1)}, u32[]{:S(2)}, u32[]{:S(2)}) collective-permute-start(f32[1,1024]{1,0:T(1,128)S(1)} %get-tuple-element.61), channel_id=1, source_target_pairs={{0,15},{1,2},{2,1},{3,4},{4,3},{5,6},{6,5},{7,8},{8,7},{9,10},{10,... | collective-permute-start | bytes 12296 | tf_op jit(solution)/shard_map/ppermute | solution.py:259
  36.5 3.0 %collective-permute-start.10 = (f32[8,128]{1,0:T(8,128)S(1)}, f32[8,128]{1,0:T(8,128)S(1)}, u32[]{:S(2)}, u32[]{:S(2)}) collective-permute-start(f32[8,128]{1,0:T(8,128)S(1)} %get-tuple-element.66), channel_id=1, source_target_pairs={{0,3},{1,2},{2,1},{3,0},{4,7},{5,6},{6,5},{7,4},{8,11},{9,10},{10,... | collective-permute-start | bytes 12296 | tf_op jit(solution)/shard_map/ppermute | solution.py:269
  36.5 3.6 %collective-permute-start.9 = (f32[8,128]{1,0:T(8,128)S(1)}, f32[8,128]{1,0:T(8,128)S(1)}, u32[]{:S(2)}, u32[]{:S(2)}) collective-permute-start(f32[8,128]{1,0:T(8,128)S(1)} %get-tuple-element.66), channel_id=1, source_target_pairs={{0,2},{1,3},{2,0},{3,1},{4,6},{5,7},{6,4},{7,5},{8,10},{9,11},{10,... | collective-permute-start | bytes 12296 | tf_op jit(solution)/shard_map/ppermute | solution.py:269
  36.6 3.6 %collective-permute-start.8 = (f32[8,128]{1,0:T(8,128)S(1)}, f32[8,128]{1,0:T(8,128)S(1)}, u32[]{:S(2)}, u32[]{:S(2)}) collective-permute-start(f32[8,128]{1,0:T(8,128)S(1)} %get-tuple-element.66), channel_id=1, source_target_pairs={{0,1},{1,0},{2,3},{3,2},{4,5},{5,4},{6,7},{7,6},{8,9},{9,8},{10,11... | collective-permute-start | bytes 12296 | tf_op jit(solution)/shard_map/ppermute | solution.py:269
  40.2 6.6 %collective-permute-start.13 = (f32[8,128]{1,0:T(8,128)S(1)}, f32[8,128]{1,0:T(8,128)S(1)}, u32[]{:S(2)}, u32[]{:S(2)}) collective-permute-start(f32[8,128]{1,0:T(8,128)S(1)} %add_add_fusion.1), channel_id=1, source_target_pairs={{0,12},{1,13},{2,14},{3,15},{4,8},{5,9},{6,10},{7,11},{8,4},{9,5},... | collective-permute-start | bytes 12296 | tf_op jit(solution)/shard_map/ppermute | solution.py:269
  45.2 4.5 %collective-permute-start.12 = (f32[8,128]{1,0:T(8,128)S(1)}, f32[8,128]{1,0:T(8,128)S(1)}, u32[]{:S(2)}, u32[]{:S(2)}) collective-permute-start(f32[8,128]{1,0:T(8,128)S(1)} %add_add_fusion.1), channel_id=1, source_target_pairs={{0,8},{1,9},{2,10},{3,11},{4,12},{5,13},{6,14},{7,15},{8,0},{9,1},... | collective-permute-start | bytes 12296 | tf_op jit(solution)/shard_map/ppermute | solution.py:269
  45.2 4.5 %collective-permute-start.11 = (f32[8,128]{1,0:T(8,128)S(1)}, f32[8,128]{1,0:T(8,128)S(1)}, u32[]{:S(2)}, u32[]{:S(2)}) collective-permute-start(f32[8,128]{1,0:T(8,128)S(1)} %add_add_fusion.1), channel_id=1, source_target_pairs={{0,4},{1,5},{2,6},{3,7},{4,0},{5,1},{6,2},{7,3},{8,12},{9,13},{10,... | collective-permute-start | bytes 12296 | tf_op jit(solution)/shard_map/ppermute | solution.py:269

commit v3 on v2

--- a/solution.py
+++ b/solution.py
@@ -101,25 +101,13 @@
 
 
 def first_kernel(
-    low_ref, high_ref, active_ref, right_ref, east_ref, north_ref, surface_ref, mask_ref, bt_ref,
-    residual_ref, direction_ref, diag_ref, east_face_ref, north_face_ref, ocean_ref, east_end_ref, coef_ref, inner_ref, outer_ref,
+    active_ref, right_ref, east_ref, north_ref, surface_ref, mask_ref, bt_ref,
+    residual_ref, search_ref, diag_ref, east_face_ref, north_face_ref, ocean_ref, east_end_ref, inner_ref, outer_ref,
 ):
     columns, rows = right_ref.shape
     count = lane_blocks(rows)
     tiles = rows // SUBS
     even = even_device()
-    low = jnp.broadcast_to(low_ref[...].reshape(1, 1), (1, LANES))
-    high = jnp.broadcast_to(high_ref[...].reshape(1, 1), (1, LANES))
-    center = (high + low) / 2.0
-    radius = (high - low) / 2.0
-    ratio = center / radius
-    weight_prev = 1.0 / ratio
-    coef_ref[0:1] = 1.0 / center
-    for k in range(1, ITERS):
-        weight = 1.0 / (2.0 * ratio - weight_prev)
-        coef_ref[2 * k : 2 * k + 1] = weight * weight_prev
-        coef_ref[2 * k + 1 : 2 * k + 2] = 2.0 * weight / radius
-        weight_prev = weight
     flags = tile_flags(active_ref, lax.axis_index("lon") * tiles, tiles)
     lane = lax.broadcasted_iota(jnp.int32, (SUBS, LANES), 1)
     spread = [
@@ -141,10 +129,10 @@
     residual_ref[...] = residual
     east_end_ref[...] = east_ocean[columns - 1 :]
     store_edges(inner_ref, outer_ref, 1, even, ocean[0:1], east_ocean[columns - 1 :])
-    blocks_product(bt_ref, residual, direction_ref)
-    direction = direction_ref[...] * ocean * repeat_row(coef_ref[0:1], count)
-    direction_ref[...] = direction
-    store_edges(inner_ref, outer_ref, 0, even, direction[0:1], direction[columns - 1 :])
+    blocks_product(bt_ref, residual, search_ref)
+    search = search_ref[...] * ocean
+    search_ref[...] = search
+    store_edges(inner_ref, outer_ref, 0, even, search[0:1], search[columns - 1 :])
 
 
 def apply_operator(residual, direction, diag, east_face, north_face, west_term, east_term):
@@ -157,25 +145,39 @@
     return residual - flow
 
 
-def search_step(bt_ref, residual, direction, ocean, coef_ref, k, search_ref, inner_out, outer_out, direction_out):
+def search_step(bt_ref, residual, direction, ocean, coef_ref, k, search_ref):
     count = lane_blocks(residual.shape[1])
     blocks_product(bt_ref, residual, search_ref)
     keep = repeat_row(coef_ref[2 * k : 2 * k + 1], count)
     gain = repeat_row(coef_ref[2 * k + 1 : 2 * k + 2], count)
-    direction = keep * direction + gain * (ocean * search_ref[...])
-    direction_out[...] = direction
-    store_edges(inner_out, outer_out, 0, even_device(), direction[0:1], direction[-1:])
-    return direction
+    return keep * direction + gain * (ocean * search_ref[...])
+
+
+def store_coefficients(low_ref, high_ref, coef_ref):
+    low = jnp.full((1, LANES), low_ref[0], F32)
+    high = jnp.full((1, LANES), high_ref[0], F32)
+    center = (high + low) / 2.0
+    radius = (high - low) / 2.0
+    ratio = center / radius
+    weight_prev = 1.0 / ratio
+    coef_ref[0:1] = 1.0 / center
+    for k in range(1, ITERS):
+        weight = 1.0 / (2.0 * ratio - weight_prev)
+        coef_ref[2 * k : 2 * k + 1] = weight * weight_prev
+        coef_ref[2 * k + 1 : 2 * k + 2] = 2.0 * weight / radius
+        weight_prev = weight
 
 
 def second_kernel(
-    inner_ref, outer_ref, residual_ref, direction_ref, diag_ref, east_face_ref, north_face_ref, ocean_ref, east_end_ref, coef_ref, bt_ref,
-    residual_out, direction_out, solution_out, diag_out, faces_out, norms_out, inner_out, outer_out,
+    low_ref, high_ref, inner_ref, outer_ref, residual_ref, search_in, diag_ref, east_face_ref, north_face_ref, ocean_ref, east_end_ref, bt_ref,
+    residual_out, direction_out, solution_out, diag_out, faces_out, norms_out, coef_out, inner_out, outer_out,
     search_ref,
 ):
+    store_coefficients(low_ref, high_ref, coef_out)
     ocean = ocean_ref[...]
-    direction = direction_ref[...]
-    columns = ocean.shape[0]
+    columns, rows = ocean.shape
+    scale = repeat_row(coef_out[0:1], lane_blocks(rows))
+    direction = search_in[...] * scale
     even = even_device()
     west, east = halo_rows(inner_ref, outer_ref, 0, even)
     west_static, east_static = halo_rows(inner_ref, outer_ref, 1, even)
@@ -190,13 +192,30 @@
     diag_out[...] = diag
     residual = apply_operator(
         residual_ref[...], direction, diag, east_face_ref[...], north_face_ref[...],
-        west_face * west, east_end * east,
+        west_face * (scale * west), east_end * (scale * east),
     )
     residual_out[...] = residual
     norms_out[...] = jnp.zeros_like(norms_out)
-    norms_out[0:1] = lane_partial(residual * residual)
-    later = search_step(bt_ref, residual, direction, ocean, coef_ref, 1, search_ref, inner_out, outer_out, direction_out)
+    norms_out[0:1, 0:LANES] = lane_partial(residual * residual)
+    later = search_step(bt_ref, residual, direction, ocean, coef_out, 1, search_ref)
+    direction_out[...] = later
+    store_edges(inner_out, outer_out, 0, even, later[0:1], later[columns - 1 :])
     solution_out[...] = direction + later
+
+
+def advance(k, west, east, residual_ref, direction_ref, solution_ref, diag_ref, east_face_ref, north_face_ref, ocean_ref, faces_ref, coef_ref, bt_ref, search_ref):
+    direction = direction_ref[...]
+    residual = apply_operator(
+        residual_ref[...], direction, diag_ref[...], east_face_ref[...], north_face_ref[...],
+        faces_ref[0:1] * west, faces_ref[1:2] * east,
+    )
+    later = search_step(bt_ref, residual, direction, ocean_ref[...], coef_ref, k, search_ref)
+    return residual, later, solution_ref[...] + later
+
+
+def store_norm(norms_out, norms_ref, k, squares):
+    norms_out[...] = norms_ref[...]
+    norms_out[0:1, k * LANES : (k + 1) * LANES] = lane_partial(squares)
 
 
 def middle_kernel(
@@ -205,31 +224,107 @@
     residual_out, direction_out, solution_out, norms_out, inner_out, outer_out,
     search_ref,
 ):
-    direction = direction_ref[...]
-    west, east = halo_rows(inner_ref, outer_ref, 0, even_device())
-    residual = apply_operator(
-        residual_ref[...], direction, diag_ref[...], east_face_ref[...], north_face_ref[...],
-        faces_ref[0:1] * west, faces_ref[1:2] * east,
+    even = even_device()
+    west, east = halo_rows(inner_ref, outer_ref, 0, even)
+    residual, later, answer = advance(
+        k, west, east, residual_ref, direction_ref, solution_ref, diag_ref, east_face_ref, north_face_ref, ocean_ref, faces_ref, coef_ref, bt_ref, search_ref
     )
     residual_out[...] = residual
-    norms_out[...] = norms_ref[...]
-    norms_out[k - 1 : k] = lane_partial(residual * residual)
-    later = search_step(bt_ref, residual, direction, ocean_ref[...], coef_ref, k, search_ref, inner_out, outer_out, direction_out)
-    solution_out[...] = solution_ref[...] + later
-
-
-def last_kernel(
-    inner_ref, outer_ref, residual_ref, direction_ref, diag_ref, east_face_ref, north_face_ref, faces_ref, norms_ref,
-    residual_out, norms_out,
+    store_norm(norms_out, norms_ref, k - 1, residual * residual)
+    direction_out[...] = later
+    store_edges(inner_out, outer_out, 0, even, later[0:1], later[-1:])
+    solution_out[...] = answer
+
+
+FIRST_RES, FIRST_DIR, LAST_RES, LAST_DIR, LAST_FACE, SUMS, PACK_ROWS = 0, 1, 2, 3, 4, 5, 8
+
+
+def closing_kernel(
+    inner_ref, outer_ref, residual_ref, direction_ref, solution_ref, diag_ref, east_face_ref, north_face_ref, ocean_ref, faces_ref, coef_ref, norms_ref, bt_ref,
+    residual_out, solution_out, pack_out,
+    search_ref,
 ):
     west, east = halo_rows(inner_ref, outer_ref, 0, even_device())
-    residual = apply_operator(
-        residual_ref[...], direction_ref[...], diag_ref[...], east_face_ref[...], north_face_ref[...],
-        faces_ref[0:1] * west, faces_ref[1:2] * east,
-    )
+    residual, later, answer = advance(
+        ITERS - 1, west, east, residual_ref, direction_ref, solution_ref, diag_ref, east_face_ref, north_face_ref, ocean_ref, faces_ref, coef_ref, bt_ref, search_ref
+    )
+    solution_out[...] = answer
+    columns = residual.shape[0]
+    sums = pack_out.at[SUMS : SUMS + 1]
+    store_norm(sums, norms_ref, ITERS - 2, residual * residual)
+    nothing = jnp.zeros_like(west)
+    residual = apply_operator(residual, later, diag_ref[...], east_face_ref[...], north_face_ref[...], nothing, nothing)
     residual_out[...] = residual
-    norms_out[...] = norms_ref[...]
-    norms_out[ITERS - 1 : ITERS] = lane_partial(residual * residual)
+    lon = lax.broadcasted_iota(jnp.int32, residual.shape, 0)
+    inside = jnp.where((lon > 0) & (lon < columns - 1), residual, 0.0)
+    sums[0:1, (ITERS - 1) * LANES : ITERS * LANES] = lane_partial(inside * inside)
+    pack_out[FIRST_RES : FIRST_RES + 1] = residual[0:1]
+    pack_out[FIRST_DIR : FIRST_DIR + 1] = later[0:1]
+    pack_out[LAST_RES : LAST_RES + 1] = residual[columns - 1 :]
+    pack_out[LAST_DIR : LAST_DIR + 1] = later[columns - 1 :]
+    pack_out[LAST_FACE : LAST_FACE + 1] = faces_ref[1:2]
+    pack_out[SUMS + 1 :] = jnp.zeros_like(pack_out[SUMS + 1 :])
+
+
+def join_packs(size, radix, is_last, pack_ref, others, halo, packs):
+    me = lax.axis_index("lon")
+    mine = lax.rem(me // size, radix)
+    packs[mine] = pack_ref[...]
+    for s, other in enumerate(others, start=1):
+        packs[mine ^ s] = other[...]
+
+    def row(run, name):
+        return packs[run % radix, name : name + 1, :]
+
+    sums = functools.reduce(jnp.add, [row(run, SUMS) for run in range(radix)])
+    total = None
+    for run in range(radix if is_last else radix - 1):
+        face = row(run, LAST_FACE)
+        left = row(run, LAST_RES) + face * row(run + 1, FIRST_DIR)
+        right = row(run + 1, FIRST_RES) + face * row(run, LAST_DIR)
+        squares = lane_partial(left * left + right * right)
+        total = squares if total is None else total + squares
+    parts = [sums[:, i * LANES : (i + 1) * LANES] for i in range(sums.shape[1] // LANES)]
+    parts[ITERS - 1] = parts[ITERS - 1] + total
+    before = packs[lax.rem(mine + radix - 1, radix)][LAST_DIR : LAST_DIR + 1]
+    after = packs[lax.rem(mine + 1, radix)][FIRST_DIR : FIRST_DIR + 1]
+    place = lax.rem(me, size)
+    west_now = place == 0
+    east_now = place == size - 1
+    if not is_last:
+        west_now = west_now & (mine > 0)
+        east_now = east_now & (mine < radix - 1)
+    west, east = halo
+    return parts, jnp.where(west_now, before, west), jnp.where(east_now, after, east)
+
+
+def stage_kernel(size, radix, *refs):
+    pack_ref, others, halo_ref = refs[0], refs[1:radix], refs[radix] if size > 1 else None
+    pack_out, halo_out, packs = refs[-3:]
+    nothing = jnp.zeros((1, pack_ref.shape[1]), F32)
+    halo = (nothing, nothing) if halo_ref is None else (halo_ref[0:1], halo_ref[1:2])
+    parts, west, east = join_packs(size, radix, False, pack_ref, others, halo, packs)
+    pack_out[...] = packs[0]
+    for name in (LAST_RES, LAST_DIR, LAST_FACE):
+        pack_out[name : name + 1] = packs[radix - 1, name : name + 1, :]
+    pack_out[SUMS : SUMS + 1] = jnp.concatenate(parts, axis=1)
+    halo_out[0:1] = west
+    halo_out[1:2] = east
+
+
+def finish_kernel(size, radix, cells_all, *refs):
+    pack_ref, others, halo_ref = refs[0], refs[1:radix], refs[radix]
+    residual_ref, faces_ref, answer_ref = refs[radix + 1 : radix + 4]
+    residual_out, answer_out, norms_out, packs = refs[radix + 4 :]
+    parts, west, east = join_packs(size, radix, True, pack_ref, others, (halo_ref[0:1], halo_ref[1:2]), packs)
+    answer_out[...] = answer_ref[...]
+    residual = residual_ref[...]
+    lon = lax.broadcasted_iota(jnp.int32, residual.shape, 0)
+    residual = jnp.where(lon == 0, residual + faces_ref[0:1] * west, residual)
+    residual = jnp.where(lon == residual.shape[0] - 1, residual + faces_ref[1:2] * east, residual)
+    residual_out[...] = residual
+    for k in range(ITERS):
+        norms_out[k] = jnp.sum(parts[k]) / cells_all
 
 
 def vmem():
@@ -240,11 +335,15 @@
     return jax.ShapeDtypeStruct(dims, F32)
 
 
-def call(body, in_specs, outs, scratch, limit, cost=None):
+def smem():
+    return pl.BlockSpec(memory_space=pltpu.SMEM)
+
+
+def call(body, in_specs, outs, scratch, limit, cost=None, out_specs=None):
     return pl.pallas_call(
         body,
         in_specs=in_specs,
-        out_specs=[vmem()] * len(outs),
+        out_specs=out_specs or [vmem()] * len(outs),
         out_shape=outs,
         scratch_shapes=scratch,
         compiler_params=pltpu.CompilerParams(vmem_limit_bytes=limit),
@@ -259,19 +358,11 @@
     return lax.ppermute(inner, "lon", pairs), lax.ppermute(outer, "lon", across)
 
 
-def reduce_stages(total):
+def swap_runs(pack, size, radix):
     devices = lax.axis_size("lon")
-    stride = 1
-    while stride < devices:
-        left = devices // stride
-        radix = 4 if left % 4 == 0 else 2
-        parts = [
-            lax.ppermute(total, "lon", [(i, i ^ (s * stride)) for i in range(devices)])
-            for s in range(1, radix)
-        ]
-        total = functools.reduce(jnp.add, parts, total)
-        stride *= radix
-    return total
+    return [
+        lax.ppermute(pack, "lon", [(i, i ^ (s * size)) for i in range(devices)]) for s in range(radix - 1, 0, -1)
+    ][::-1]
 
 
 def on_device(
@@ -280,9 +371,7 @@
     columns, rows = right_side.shape
     tiles = inverse_blocks.shape[0]
     count = lane_blocks(rows)
-    cells_all = columns * lax.axis_size("lon") * rows
     field = shape(columns, rows)
-    norm_shape = shape(SUBS, LANES)
     row = shape(1, rows)
     two = shape(2, rows)
     bt_shape = shape(count, columns, LANES, LANES)
@@ -294,39 +383,65 @@
         40 * MIB,
         pl.CostEstimate(flops=10**9, bytes_accessed=2 * inverse_blocks.size * 4, transcendentals=0),
     )(inverse_blocks)
-    residual, direction, diag, east_face, north_face, ocean, east_end, coef, inner, outer = call(
+    residual, search, diag, east_face, north_face, ocean, east_end, inner, outer = call(
         first_kernel,
-        [vmem()] * 9,
-        [field, field, field, field, field, field, row, norm_shape, two, two],
+        [vmem()] * 7,
+        [field, field, field, field, field, field, row, two, two],
         [],
         24 * MIB,
-    )(
-        low_bound, high_bound, active_tiles.reshape(-1, LANES),
-        right_side, east_coef, north_coef, surface_term, cell_mask, bt,
-    )
+    )(active_tiles.reshape(-1, LANES), right_side, east_coef, north_coef, surface_term, cell_mask, bt)
+    low_bound, high_bound, inner = lax.optimization_barrier((low_bound, high_bound, inner))
     inner, outer = exchange(inner, outer)
-    residual, direction, answer, diag, faces, norms, inner, outer = call(
+    residual, direction, answer, diag, faces, norms, coef, inner, outer = call(
         second_kernel,
-        [vmem()] * 11,
-        [field, field, field, field, two, norm_shape, row, row],
+        [smem()] * 2 + [vmem()] * 10,
+        [field, field, field, field, two, row, shape(SUBS, LANES), row, row],
         [pltpu.VMEM((columns, rows), F32)],
         24 * MIB,
-    )(inner, outer, residual, direction, diag, east_face, north_face, ocean, east_end, coef, bt)
-    for k in range(2, ITERS):
+    )(low_bound, high_bound, inner, outer, residual, search, diag, east_face, north_face, ocean, east_end, bt)
+    for k in range(2, ITERS - 1):
         inner, outer = exchange(inner, outer)
         residual, direction, answer, norms, inner, outer = call(
             functools.partial(middle_kernel, k),
             [vmem()] * 13,
-            [field, field, field, norm_shape, row, row],
+            [field, field, field, row, row, row],
             [pltpu.VMEM((columns, rows), F32)],
             24 * MIB,
         )(inner, outer, residual, direction, answer, diag, east_face, north_face, ocean, faces, coef, norms, bt)
     inner, outer = exchange(inner, outer)
-    residual, norms = call(last_kernel, [vmem()] * 9, [field, norm_shape], [], 24 * MIB)(
-        inner, outer, residual, direction, diag, east_face, north_face, faces, norms
-    )
-    norms = reduce_stages(norms)
-    return answer, residual, jnp.sum(norms[:ITERS], axis=1) / cells_all
+    pack_shape = shape(PACK_ROWS, rows)
+    residual, answer, pack = call(
+        closing_kernel,
+        [vmem()] * 13,
+        [field, field, pack_shape],
+        [pltpu.VMEM((columns, rows), F32)],
+        24 * MIB,
+    )(inner, outer, residual, direction, answer, diag, east_face, north_face, ocean, faces, coef, norms, bt)
+    devices = lax.axis_size("lon")
+    size, halo = 1, []
+    while True:
+        radix = 4 if (devices // size) % 4 == 0 else 2
+        others = swap_runs(pack, size, radix)
+        packs = [pltpu.VMEM((radix, PACK_ROWS, rows), F32)]
+        if size * radix == devices:
+            break
+        pack, *halo = call(
+            functools.partial(stage_kernel, size, radix),
+            [vmem()] * (radix + len(halo)),
+            [pack_shape, two],
+            packs,
+            24 * MIB,
+        )(pack, *others, *halo)
+        size *= radix
+    residual, answer, norms = call(
+        functools.partial(finish_kernel, size, radix, float(columns * devices * rows)),
+        [vmem()] * (radix + 4),
+        [field, field, shape(ITERS)],
+        packs,
+        24 * MIB,
+        out_specs=[vmem(), vmem(), smem()],
+    )(pack, *others, *halo, residual, faces, answer)
+    return answer, residual, norms
 
 
 def solution(mesh):

time: 50.5 us -> 43.1 us (0.85)
  starting transfers between devices: 27.2 us -> 22.7 us
  waiting for transfers between devices: 11 us -> 9.07 us
  other arithmetic: 0.64 us -> 0 us
    ppermute x4 -> x3, starting transfers between devices: 19 us -> 14.6 us  [exchange(): lax.ppermute(outer, 'lon', across)]
    ppermute x4 -> x3, waiting for transfers between devices: 5.34 us -> 2.71 us  [exchange(): lax.ppermute(outer, 'lon', across)]
    pallas_call x2 -> x1, Pallas kernels: 2.47 us -> 0.94 us  [on_device(): call(functools.partial(middle_kernel, k), [vmem()] * 13, [field, field, f...]
    pallas_call x3 -> x5, Pallas kernels: 2.9 us -> 3.98 us  [the longest x1 1.22 us: on_device(): call(first_kernel, [vmem()] * 7, [field, field, field, field, field, fiel...]
    ppermute x6, waiting for transfers between devices: 5.65 us -> 6.35 us  [swap_runs(): lax.ppermute(pack, 'lon', [(i, i ^ s * size) for i in range(devices)])]
    div x1 -> x0, other arithmetic: 0.52 us -> none  [on_device(): return (answer, residual, jnp.sum(norms[:ITERS], axis=1) / cells_all)]
  transfers between devices with their start and end apart: 14 -> 12, of which waited for: 8 -> 7; matrix products, arithmetic and copies ran while one was open for 0% -> 0% of each run, Pallas kernels for 0% -> 0%
where the time goes in v3:
time: 43.1 us; the launch traced here: 42.9 us
  starting transfers between devices  22.7 us (53%)
  waiting for transfers between devices  9.07 us (21%)
  Pallas kernels  8.99 us (21%)
  between operations  2.1 us (5%)
    ppermute x3, starting transfers between devices, exchange(): lax.ppermute(outer, 'lon', across)  14.6 us
    ppermute x6, starting transfers between devices, swap_runs(): lax.ppermute(pack, 'lon', [(i, i ^ s * size) for i in range(devices)])  7.46 us
    ppermute x6, waiting for transfers between devices, swap_runs(): lax.ppermute(pack, 'lon', [(i, i ^ s * size) for i in range(devices)])  6.35 us
    pallas_call x1, Pallas kernels, on_device(): call(transpose_kernel, [pl.BlockSpec(memory_space=pl.ANY)], [bt_shape], [...  4.07 us
    ppermute x3, waiting for transfers between devices, exchange(): lax.ppermute(outer, 'lon', across)  2.71 us
    pallas_call x1, Pallas kernels, on_device(): call(first_kernel, [vmem()] * 7, [field, field, field, field, field, fiel...  1.22 us
    pallas_call x1, Pallas kernels, on_device(): call(closing_kernel, [vmem()] * 13, [field, field, pack_shape], [pltpu.VM...  1.04 us
    pallas_call x1, Pallas kernels, on_device(): call(second_kernel, [smem()] * 2 + [vmem()] * 10, [field, field, field, f...  0.95 us
  transfers between devices with their start and end apart: 12, of which 7 were waited for; matrix products, arithmetic and copies ran while one was open for 0% of the time, Pallas kernels for 0%

profile of v3, /device:TPU:0, one launch (start us, length us, event | category | flops | bytes accessed | tf_op | source)
XLA Modules:
  0.0 42.9 jit_solution(1921559725603095688)
XLA Ops:
  0.6 0.0 copy-start.5
  0.6 0.0 copy-start.4
  0.7 4.1 %shard_map.112.bt_ref = f32[8,16,128,128]{3,2,1,0:T(8,128)S(1)} custom-call(f32[128,128,128]{2,1,0:T(8,128)} %blocks_hbm.1), custom_call_target="tpu_custom_call" | custom-call | flops 1000000000 | bytes 16777216 | tf_op jit(solution)/shard_map/pallas_call | solution.py:378
  4.8 1.2 %shard_map.113 = (f32[16,1024]{1,0:T(8,128)S(1)}, f32[16,1024]{1,0:T(8,128)S(1)}, f32[16,1024]{1,0:T(8,128)S(1)}, f32[16,1024]{1,0:T(8,128)S(1)}, f32[16,1024]{1...) custom-call(s32[12,128]{1,0:T(8,128)S(1)} %bitcast.1, ...), custom_call_target="tpu_custom_call" | custom-call | tf_op jit(solution)/shard_map/pallas_call | solution.py:386
  6.1 0.5 %collective-permute-start = (f32[2,1024]{1,0:T(2,128)S(1)}, f32[2,1024]{1,0:T(2,128)S(1)}, u32[]{:S(2)}, u32[]{:S(2)}) collective-permute-start(f32[2,1024]{1,0:T(2,128)S(1)} %get-tuple-element.41), channel_id=1, source_target_pairs={{0,1},{1,0},{2,3},{3,2},{4,5},{5,4},{6,7},{7,6},{8,9},{9,8},{10,11... | collective-permute-start | bytes 24584 | tf_op jit(solution)/shard_map/ppermute | solution.py:358
  6.6 5.7 %collective-permute-start.1 = (f32[2,1024]{1,0:T(2,128)S(1)}, f32[2,1024]{1,0:T(2,128)S(1)}, u32[]{:S(2)}, u32[]{:S(2)}) collective-permute-start(f32[2,1024]{1,0:T(2,128)S(1)} %get-tuple-element.42), channel_id=1, source_target_pairs={{0,15},{1,2},{2,1},{3,4},{4,3},{5,6},{6,5},{7,8},{8,7},{9,10},{10,... | collective-permute-start | bytes 24584 | tf_op jit(solution)/shard_map/ppermute | solution.py:358
  13.5 0.0 collective-permute-done.inner_ref
  13.5 0.1 collective-permute-done.1.outer_ref
  13.6 1.0 %shard_map.114 = (f32[16,1024]{1,0:T(8,128)S(1)}, f32[16,1024]{1,0:T(8,128)S(1)}, f32[16,1024]{1,0:T(8,128)S(1)}, f32[16,1024]{1,0:T(8,128)S(1)}, f32[2,1024]{1,...) custom-call(f32[1]{0:T(128)S(6)} %copy.12.low_ref, ...), custom_call_target="tpu_custom_call" | custom-call | tf_op jit(solution)/shard_map/pallas_call | solution.py:395
  14.6 0.1 collective-permute-start.2
  14.6 4.5 %collective-permute-start.3 = (f32[1,1024]{1,0:T(1,128)S(1)}, f32[1,1024]{1,0:T(1,128)S(1)}, u32[]{:S(2)}, u32[]{:S(2)}) collective-permute-start(f32[1,1024]{1,0:T(1,128)S(1)} %get-tuple-element.51), channel_id=1, source_target_pairs={{0,15},{1,2},{2,1},{3,4},{4,3},{5,6},{6,5},{7,8},{8,7},{9,10},{10,... | collective-permute-start | bytes 12296 | tf_op jit(solution)/shard_map/ppermute | solution.py:358
  19.1 0.0 collective-permute-done.2.inner_ref
  19.1 1.3 %collective-permute-done.3.outer_ref = f32[1,1024]{1,0:T(1,128)S(1)} collective-permute-done((f32[1,1024]{1,0:T(1,128)S(1)}, f32[1,1024]{1,0:T(1,128)S(1)}, u32[]{:S(2)}, u32[]{:S(2)}) %collective-permute-start.3) | collective-permute-done | bytes 4128 | tf_op jit(solution)/shard_map/ppermute | solution.py:358
  20.4 0.9 %shard_map.115 = (f32[16,1024]{1,0:T(8,128)S(1)}, f32[16,1024]{1,0:T(8,128)S(1)}, f32[16,1024]{1,0:T(8,128)S(1)}, f32[1,1024]{1,0:T(1,128)S(1)}, f32[1,1024]{1,0:T(1,128)S(1)}, /*index=5*/f32[1,1024]{1,0:T(1,128)S(1)}) custom-call(f32[1,1024]{1,0:T(1,128)S(1)} %collective-permute-done.2.inner_ref, f32[1,1024]{1,0:T(1,128)S(1)} %collective-permute-done.3.outer_ref, ...), custom_call_target="tpu_custom_call" | custom-call | tf_op jit(solution)/shard_map/pallas_call | solution.py:404
  21.4 0.1 collective-permute-start.4
  21.5 4.5 %collective-permute-start.5 = (f32[1,1024]{1,0:T(1,128)S(1)}, f32[1,1024]{1,0:T(1,128)S(1)}, u32[]{:S(2)}, u32[]{:S(2)}) collective-permute-start(f32[1,1024]{1,0:T(1,128)S(1)} %get-tuple-element.60), channel_id=1, source_target_pairs={{0,15},{1,2},{2,1},{3,4},{4,3},{5,6},{6,5},{7,8},{8,7},{9,10},{10,... | collective-permute-start | bytes 12296 | tf_op jit(solution)/shard_map/ppermute | solution.py:358
  25.9 0.0 collective-permute-done.4.inner_ref
  25.9 1.3 %collective-permute-done.5.outer_ref = f32[1,1024]{1,0:T(1,128)S(1)} collective-permute-done((f32[1,1024]{1,0:T(1,128)S(1)}, f32[1,1024]{1,0:T(1,128)S(1)}, u32[]{:S(2)}, u32[]{:S(2)}) %collective-permute-start.5) | collective-permute-done | bytes 4128 | tf_op jit(solution)/shard_map/ppermute | solution.py:358
  27.3 1.0 %shard_map.116 = (f32[16,1024]{1,0:T(8,128)S(1)}, f32[16,1024]{1,0:T(8,128)S(1)}, f32[8,1024]{1,0:T(8,128)S(1)}) custom-call(f32[1,1024]{1,0:T(1,128)S(1)} %collective-permute-done.4.inner_ref, f32[1,1024]{1,0:T(1,128)S(1)} %collective-permute-done.5.outer_ref, f32[16,1024]{1,0:T(8,128)S(1)} %get-tuple-element.61.residual_ref, ...), custom_call_target="tpu_custom_call" | custom-call | tf_op jit(solution)/shard_map/pallas_call | solution.py:413
  28.3 0.1 collective-permute-start.8
  28.4 0.1 collective-permute-start.7
  28.5 1.8 %collective-permute-start.6 = (f32[8,1024]{1,0:T(8,128)S(1)}, f32[8,1024]{1,0:T(8,128)S(1)}, u32[]{:S(2)}, u32[]{:S(2)}) collective-permute-start(f32[8,1024]{1,0:T(8,128)S(1)} %get-tuple-element.65.refs_0_), channel_id=1, source_target_pairs={{0,1},{1,0},{2,3},{3,2},{4,5},{5,4},{6,7},{7,6},{8,9},{9,8},{10,11... | collective-permute-start | bytes 98312 | tf_op jit(solution)/shard_map/ppermute | solution.py:364
  30.2 1.5 %collective-permute-done.8.refs_3_ = f32[8,1024]{1,0:T(8,128)S(1)} collective-permute-done((f32[8,1024]{1,0:T(8,128)S(1)}, f32[8,1024]{1,0:T(8,128)S(1)}, u32[]{:S(2)}, u32[]{:S(2)}) %collective-permute-start.8) | collective-permute-done | bytes 32800 | tf_op jit(solution)/shard_map/ppermute | solution.py:364
  31.7 0.7 %collective-permute-done.7.refs_2_ = f32[8,1024]{1,0:T(8,128)S(1)} collective-permute-done((f32[8,1024]{1,0:T(8,128)S(1)}, f32[8,1024]{1,0:T(8,128)S(1)}, u32[]{:S(2)}, u32[]{:S(2)}) %collective-permute-start.7) | collective-permute-done | bytes 32800 | tf_op jit(solution)/shard_map/ppermute | solution.py:364
  32.4 0.0 collective-permute-done.6.refs_1_
  32.5 4.9 %collective-permute-start.11 = (f32[8,1024]{1,0:T(8,128)S(1)}, f32[8,1024]{1,0:T(8,128)S(1)}, u32[]{:S(2)}, u32[]{:S(2)}) collective-permute-start(f32[8,1024]{1,0:T(8,128)S(1)} %get-tuple-element.66.refs_0_), channel_id=1, source_target_pairs={{0,12},{1,13},{2,14},{3,15},{4,8},{5,9},{6,10},{7,11},{8,4},{9,5},... | collective-permute-start | bytes 98312 | tf_op jit(solution)/shard_map/ppermute | solution.py:364
  37.4 0.0 collective-permute-start.10
  37.4 0.6 %collective-permute-start.9 = (f32[8,1024]{1,0:T(8,128)S(1)}, f32[8,1024]{1,0:T(8,128)S(1)}, u32[]{:S(2)}, u32[]{:S(2)}) collective-permute-start(f32[8,1024]{1,0:T(8,128)S(1)} %get-tuple-element.66.refs_0_), channel_id=1, source_target_pairs={{0,4},{1,5},{2,6},{3,7},{4,0},{5,1},{6,2},{7,3},{8,12},{9,13},{10,... | collective-permute-start | bytes 98312 | tf_op jit(solution)/shard_map/ppermute | solution.py:364
  38.0 1.3 %collective-permute-done.11.refs_3_ = f32[8,1024]{1,0:T(8,128)S(1)} collective-permute-done((f32[8,1024]{1,0:T(8,128)S(1)}, f32[8,1024]{1,0:T(8,128)S(1)}, u32[]{:S(2)}, u32[]{:S(2)}) %collective-permute-start.11) | collective-permute-done | bytes 32800 | tf_op jit(solution)/shard_map/ppermute | solution.py:364
  39.3 2.9 %collective-permute-done.10.refs_2_ = f32[8,1024]{1,0:T(8,128)S(1)} collective-permute-done((f32[8,1024]{1,0:T(8,128)S(1)}, f32[8,1024]{1,0:T(8,128)S(1)}, u32[]{:S(2)}, u32[]{:S(2)}) %collective-permute-start.10) | collective-permute-done | bytes 32800 | tf_op jit(solution)/shard_map/ppermute | solution.py:364
  42.2 0.0 collective-permute-done.9.refs_1_
  42.2 0.7 %shard_map.118 = (f32[16,1024]{1,0:T(8,128)}, f32[16,1024]{1,0:T(8,128)}, f32[4]{0:T(128)}) custom-call(f32[8,1024]{1,0:T(8,128)S(1)} %get-tuple-element.66.refs_0_, f32[8,1024]{1,0:T(8,128)S(1)} %collective-permute-done.9.refs_1_, f32[8,1024]{1,0:T(8,128)S(1)} %collective-permute-done.10.refs_2_, f32[8,1024]{1,0:T(8,128)S(1)} %collective-permute-done.11.refs_3_, ...), custom_call_target="tpu_custom_call" | custom-call | tf_op jit(solution)/shard_map/pallas_call | solution.py:436
  (11 shorter events, 0.1 us)
Async XLA Ops:
  0.6 4.1 %copy-start.5 = (s32[1536]{0:T(1024)S(1)}, s32[1536]{0:T(1024)}, u32[]{:S(2)}) copy-start(s32[1536]{0:T(1024)} %param.15) | copy-start | bytes 18436
  0.6 4.1 %copy-start.4 = (s32[16,1024]{1,0:T(8,128)S(1)}, s32[16,1024]{1,0:T(8,128)}, u32[]{:S(2)}) copy-start(s32[16,1024]{1,0:T(8,128)} %mask_ref.1) | copy-start | bytes 196612
  0.7 4.1 %copy-start.3 = (f32[16,1024]{1,0:T(8,128)S(1)}, f32[16,1024]{1,0:T(8,128)}, u32[]{:S(2)}) copy-start(f32[16,1024]{1,0:T(8,128)} %surface_ref.1) | copy-start | bytes 196612
  0.7 4.1 %copy-start.2 = (f32[16,1024]{1,0:T(8,128)S(1)}, f32[16,1024]{1,0:T(8,128)}, u32[]{:S(2)}) copy-start(f32[16,1024]{1,0:T(8,128)} %north_ref.1) | copy-start | bytes 196612
  0.7 4.1 %copy-start.1 = (f32[16,1024]{1,0:T(8,128)S(1)}, f32[16,1024]{1,0:T(8,128)}, u32[]{:S(2)}) copy-start(f32[16,1024]{1,0:T(8,128)} %east_ref.1) | copy-start | bytes 196612
  0.7 4.1 %copy-start = (f32[16,1024]{1,0:T(8,128)S(1)}, f32[16,1024]{1,0:T(8,128)}, u32[]{:S(2)}) copy-start(f32[16,1024]{1,0:T(8,128)} %right_ref.1) | copy-start | bytes 196612
  6.1 7.5 %collective-permute-start = (f32[2,1024]{1,0:T(2,128)S(1)}, f32[2,1024]{1,0:T(2,128)S(1)}, u32[]{:S(2)}, u32[]{:S(2)}) collective-permute-start(f32[2,1024]{1,0:T(2,128)S(1)} %get-tuple-element.41), channel_id=1, source_target_pairs={{0,1},{1,0},{2,3},{3,2},{4,5},{5,4},{6,7},{7,6},{8,9},{9,8},{10,11... | collective-permute-start | bytes 24584 | tf_op jit(solution)/shard_map/ppermute | solution.py:358
  6.6 7.0 %collective-permute-start.1 = (f32[2,1024]{1,0:T(2,128)S(1)}, f32[2,1024]{1,0:T(2,128)S(1)}, u32[]{:S(2)}, u32[]{:S(2)}) collective-permute-start(f32[2,1024]{1,0:T(2,128)S(1)} %get-tuple-element.42), channel_id=1, source_target_pairs={{0,15},{1,2},{2,1},{3,4},{4,3},{5,6},{6,5},{7,8},{8,7},{9,10},{10,... | collective-permute-start | bytes 24584 | tf_op jit(solution)/shard_map/ppermute | solution.py:358
  14.6 4.6 %collective-permute-start.2 = (f32[1,1024]{1,0:T(1,128)S(1)}, f32[1,1024]{1,0:T(1,128)S(1)}, u32[]{:S(2)}, u32[]{:S(2)}) collective-permute-start(f32[1,1024]{1,0:T(1,128)S(1)} %get-tuple-element.50), channel_id=1, source_target_pairs={{0,1},{1,0},{2,3},{3,2},{4,5},{5,4},{6,7},{7,6},{8,9},{9,8},{10,11... | collective-permute-start | bytes 12296 | tf_op jit(solution)/shard_map/ppermute | solution.py:358
  14.6 5.8 %collective-permute-start.3 = (f32[1,1024]{1,0:T(1,128)S(1)}, f32[1,1024]{1,0:T(1,128)S(1)}, u32[]{:S(2)}, u32[]{:S(2)}) collective-permute-start(f32[1,1024]{1,0:T(1,128)S(1)} %get-tuple-element.51), channel_id=1, source_target_pairs={{0,15},{1,2},{2,1},{3,4},{4,3},{5,6},{6,5},{7,8},{8,7},{9,10},{10,... | collective-permute-start | bytes 12296 | tf_op jit(solution)/shard_map/ppermute | solution.py:358
  21.4 4.5 %collective-permute-start.4 = (f32[1,1024]{1,0:T(1,128)S(1)}, f32[1,1024]{1,0:T(1,128)S(1)}, u32[]{:S(2)}, u32[]{:S(2)}) collective-permute-start(f32[1,1024]{1,0:T(1,128)S(1)} %get-tuple-element.59), channel_id=1, source_target_pairs={{0,1},{1,0},{2,3},{3,2},{4,5},{5,4},{6,7},{7,6},{8,9},{9,8},{10,11... | collective-permute-start | bytes 12296 | tf_op jit(solution)/shard_map/ppermute | solution.py:358
  21.5 5.8 %collective-permute-start.5 = (f32[1,1024]{1,0:T(1,128)S(1)}, f32[1,1024]{1,0:T(1,128)S(1)}, u32[]{:S(2)}, u32[]{:S(2)}) collective-permute-start(f32[1,1024]{1,0:T(1,128)S(1)} %get-tuple-element.60), channel_id=1, source_target_pairs={{0,15},{1,2},{2,1},{3,4},{4,3},{5,6},{6,5},{7,8},{8,7},{9,10},{10,... | collective-permute-start | bytes 12296 | tf_op jit(solution)/shard_map/ppermute | solution.py:358
  28.3 3.4 %collective-permute-start.8 = (f32[8,1024]{1,0:T(8,128)S(1)}, f32[8,1024]{1,0:T(8,128)S(1)}, u32[]{:S(2)}, u32[]{:S(2)}) collective-permute-start(f32[8,1024]{1,0:T(8,128)S(1)} %get-tuple-element.65.refs_0_), channel_id=1, source_target_pairs={{0,3},{1,2},{2,1},{3,0},{4,7},{5,6},{6,5},{7,4},{8,11},{9,10},{10,... | collective-permute-start | bytes 98312 | tf_op jit(solution)/shard_map/ppermute | solution.py:364
  28.4 4.0 %collective-permute-start.7 = (f32[8,1024]{1,0:T(8,128)S(1)}, f32[8,1024]{1,0:T(8,128)S(1)}, u32[]{:S(2)}, u32[]{:S(2)}) collective-permute-start(f32[8,1024]{1,0:T(8,128)S(1)} %get-tuple-element.65.refs_0_), channel_id=1, source_target_pairs={{0,2},{1,3},{2,0},{3,1},{4,6},{5,7},{6,4},{7,5},{8,10},{9,11},{10,... | collective-permute-start | bytes 98312 | tf_op jit(solution)/shard_map/ppermute | solution.py:364
  28.5 4.0 %collective-permute-start.6 = (f32[8,1024]{1,0:T(8,128)S(1)}, f32[8,1024]{1,0:T(8,128)S(1)}, u32[]{:S(2)}, u32[]{:S(2)}) collective-permute-start(f32[8,1024]{1,0:T(8,128)S(1)} %get-tuple-element.65.refs_0_), channel_id=1, source_target_pairs={{0,1},{1,0},{2,3},{3,2},{4,5},{5,4},{6,7},{7,6},{8,9},{9,8},{10,11... | collective-permute-start | bytes 98312 | tf_op jit(solution)/shard_map/ppermute | solution.py:364
  32.5 6.8 %collective-permute-start.11 = (f32[8,1024]{1,0:T(8,128)S(1)}, f32[8,1024]{1,0:T(8,128)S(1)}, u32[]{:S(2)}, u32[]{:S(2)}) collective-permute-start(f32[8,1024]{1,0:T(8,128)S(1)} %get-tuple-element.66.refs_0_), channel_id=1, source_target_pairs={{0,12},{1,13},{2,14},{3,15},{4,8},{5,9},{6,10},{7,11},{8,4},{9,5},... | collective-permute-start | bytes 98312 | tf_op jit(solution)/shard_map/ppermute | solution.py:364
  37.4 4.8 %collective-permute-start.10 = (f32[8,1024]{1,0:T(8,128)S(1)}, f32[8,1024]{1,0:T(8,128)S(1)}, u32[]{:S(2)}, u32[]{:S(2)}) collective-permute-start(f32[8,1024]{1,0:T(8,128)S(1)} %get-tuple-element.66.refs_0_), channel_id=1, source_target_pairs={{0,8},{1,9},{2,10},{3,11},{4,12},{5,13},{6,14},{7,15},{8,0},{9,1},... | collective-permute-start | bytes 98312 | tf_op jit(solution)/shard_map/ppermute | solution.py:364
  37.4 4.8 %collective-permute-start.9 = (f32[8,1024]{1,0:T(8,128)S(1)}, f32[8,1024]{1,0:T(8,128)S(1)}, u32[]{:S(2)}, u32[]{:S(2)}) collective-permute-start(f32[8,1024]{1,0:T(8,128)S(1)} %get-tuple-element.66.refs_0_), channel_id=1, source_target_pairs={{0,4},{1,5},{2,6},{3,7},{4,0},{5,1},{6,2},{7,3},{8,12},{9,13},{10,... | collective-permute-start | bytes 98312 | tf_op jit(solution)/shard_map/ppermute | solution.py:364

commit v4 on v3

--- a/solution.py
+++ b/solution.py
@@ -64,6 +64,10 @@
 def halo_rows(inner_ref, outer_ref, row, even):
     inner, outer = inner_ref[row : row + 1], outer_ref[row : row + 1]
     return jnp.where(even, outer, inner), jnp.where(even, inner, outer)
+
+
+def low_device():
+    return lax.rem(lax.axis_index("lon"), 4) < 2
 
 
 def lane_partial(squares):
@@ -100,9 +104,23 @@
             bt_ref[i, a] = raw[i * step : (i + 1) * step, a * SUBS : (a + 1) * SUBS, :].reshape(LANES, LANES).T
 
 
+PAIR_SEARCH, PAIR_FLOW, PAIR_FACE, PAIR_BACK_SEARCH, PAIR_BACK_FACE, PAIR_OWN, PAIR_OPPOSITE, PAIR_ROWS = 0, 1, 2, 3, 4, 8, 16, 24
+
+
+def edge_products(bt_ref, field):
+    columns, rows = field.shape
+    index = gather_index()
+    first, last = [], []
+    for block in range(lane_blocks(rows)):
+        spread = expand(field, block, index)
+        first.append(jnp.sum(bt_ref[block, 0] * spread, axis=0, keepdims=True))
+        last.append(jnp.sum(bt_ref[block, columns - 1] * spread, axis=0, keepdims=True))
+    return jnp.concatenate(first, axis=1), jnp.concatenate(last, axis=1)
+
+
 def first_kernel(
     active_ref, right_ref, east_ref, north_ref, surface_ref, mask_ref, bt_ref,
-    residual_ref, search_ref, diag_ref, east_face_ref, north_face_ref, ocean_ref, east_end_ref, inner_ref, outer_ref,
+    residual_ref, search_ref, diag_ref, east_face_ref, north_face_ref, ocean_ref, east_end_ref, inner_ref, outer_ref, near_ref, far_ref,
 ):
     columns, rows = right_ref.shape
     count = lane_blocks(rows)
@@ -124,15 +142,38 @@
     north_face = jnp.where(lat < rows - 1, north_ref[...] * ocean * roll(ocean, -1, 1), 0.0)
     east_face_ref[...] = east_face
     north_face_ref[...] = north_face
-    diag_ref[...] = surface_ref[...] * ocean + east_face + roll(east_face, 1, 0) + north_face + roll(north_face, 1, 1)
+    diag = surface_ref[...] * ocean + east_face + roll(east_face, 1, 0) + north_face + roll(north_face, 1, 1)
+    diag_ref[...] = diag
     residual = right_ref[...] * ocean
     residual_ref[...] = residual
-    east_end_ref[...] = east_ocean[columns - 1 :]
-    store_edges(inner_ref, outer_ref, 1, even, ocean[0:1], east_ocean[columns - 1 :])
+    east_end = east_ocean[columns - 1 :]
+    east_end_ref[...] = east_end
     blocks_product(bt_ref, residual, search_ref)
     search = search_ref[...] * ocean
     search_ref[...] = search
-    store_edges(inner_ref, outer_ref, 0, even, search[0:1], search[columns - 1 :])
+    nothing = jnp.zeros_like(east_end)
+    flow = apply_operator(jnp.zeros_like(search), -search, diag, east_face, north_face, nothing, nothing)
+    edges = edge_products(bt_ref, flow)
+    fields = (
+        (PAIR_SEARCH, search[0:1], search[columns - 1 :]),
+        (PAIR_FLOW, edges[0] * ocean[0:1], edges[1] * ocean[columns - 1 :]),
+        (PAIR_FACE, ocean[0:1], east_end),
+        (PAIR_BACK_SEARCH, search[columns - 1 :], search[0:1]),
+        (PAIR_BACK_FACE, east_end, ocean[0:1]),
+    )
+    for row, west, east in fields:
+        store_edges(inner_ref, outer_ref, row, even, west, east)
+    for ref, edge in ((inner_ref, jnp.where(even, columns - 1, 0)), (outer_ref, jnp.where(even, 0, columns - 1))):
+        ref[len(fields) : SUBS] = jnp.zeros((SUBS - len(fields), rows), F32)
+        for i in range(count):
+            lanes = slice(i * LANES, (i + 1) * LANES)
+            ref[PAIR_OWN : PAIR_OWN + SUBS, lanes] = bt_ref[i, edge, pl.ds(pl.multiple_of(edge * SUBS, SUBS), SUBS), :]
+            back = columns - 1 - edge
+            ref[PAIR_OPPOSITE : PAIR_OPPOSITE + SUBS, lanes] = bt_ref[i, edge, pl.ds(pl.multiple_of(back * SUBS, SUBS), SUBS), :]
+    low = low_device()
+    for row, west, east in ((0, search[0:1], search[columns - 1 :]), (1, ocean[0:1], east_end)):
+        near_ref[row : row + 1] = jnp.where(low, east, west)
+        far_ref[row : row + 1] = jnp.where(low, west, east)
 
 
 def apply_operator(residual, direction, diag, east_face, north_face, west_term, east_term):
@@ -168,8 +209,21 @@
         weight_prev = weight
 
 
+def neighbour_direction(own, opposite, search, flow, own_push, opposite_push, coef_ref):
+    rows = search.shape[1]
+    count = lane_blocks(rows)
+    index = gather_index()
+    parts = []
+    for block in range(count):
+        lanes = slice(block * LANES, (block + 1) * LANES)
+        product = own[:, lanes] * expand(own_push, block, index) + opposite[:, lanes] * expand(opposite_push, block, index)
+        parts.append(jnp.sum(product, axis=0, keepdims=True))
+    scale, keep, gain = (repeat_row(coef_ref[n : n + 1], count) for n in (0, 2, 3))
+    return keep * (scale * search) + gain * (search - scale * flow + jnp.concatenate(parts, axis=1))
+
+
 def second_kernel(
-    low_ref, high_ref, inner_ref, outer_ref, residual_ref, search_in, diag_ref, east_face_ref, north_face_ref, ocean_ref, east_end_ref, bt_ref,
+    low_ref, high_ref, inner_ref, outer_ref, near_ref, far_ref, residual_ref, search_in, diag_ref, east_face_ref, north_face_ref, ocean_ref, east_end_ref, bt_ref,
     residual_out, direction_out, solution_out, diag_out, faces_out, norms_out, coef_out, inner_out, outer_out,
     search_ref,
 ):
@@ -177,30 +231,49 @@
     ocean = ocean_ref[...]
     columns, rows = ocean.shape
     scale = repeat_row(coef_out[0:1], lane_blocks(rows))
-    direction = search_in[...] * scale
-    even = even_device()
-    west, east = halo_rows(inner_ref, outer_ref, 0, even)
-    west_static, east_static = halo_rows(inner_ref, outer_ref, 1, even)
-    west_face = west_static * ocean[0:1]
-    east_end = east_end_ref[...] * east_static
-    faces_out[0:1] = west_face
-    faces_out[1:2] = east_end
+    search = search_in[...]
+    even, low = even_device(), low_device()
+    sides = [halo_rows(inner_ref, outer_ref, row, even) for row in range(PAIR_BACK_FACE + 1)]
+    beyond = [
+        (jnp.where(low, far, near), jnp.where(low, near, far))
+        for near, far in ((near_ref[row : row + 1], far_ref[row : row + 1]) for row in range(2))
+    ]
+    here = (search[0:1], search[columns - 1 :])
+    static = (ocean[0:1], east_end_ref[...])
+    faces, halos, later_halos = [], [], []
+    for side in range(2):
+        there, flow, face, back, back_face = (pair[side] for pair in sides)
+        face = static[side] * face
+        own_push = face * (scale * (here[side] - there))
+        opposite_push = back_face * beyond[1][side] * (scale * (beyond[0][side] - back))
+        from_inner = even if side == 1 else jnp.logical_not(even)
+        own, opposite = (
+            jnp.where(from_inner, inner_ref[row : row + SUBS], outer_ref[row : row + SUBS]) for row in (PAIR_OWN, PAIR_OPPOSITE)
+        )
+        faces.append(face)
+        halos.append(face * (scale * there))
+        later_halos.append(face * neighbour_direction(own, opposite, there, flow, own_push, opposite_push, coef_out))
+    faces_out[0:1] = faces[0]
+    faces_out[1:2] = faces[1]
     lon = lax.broadcasted_iota(jnp.int32, ocean.shape, 0)
     diag = diag_ref[...]
-    diag = jnp.where(lon == 0, diag + west_face, diag)
-    diag = jnp.where(lon == columns - 1, diag + east_end, diag)
+    diag = jnp.where(lon == 0, diag + faces[0], diag)
+    diag = jnp.where(lon == columns - 1, diag + faces[1], diag)
     diag_out[...] = diag
-    residual = apply_operator(
-        residual_ref[...], direction, diag, east_face_ref[...], north_face_ref[...],
-        west_face * (scale * west), east_end * (scale * east),
-    )
-    residual_out[...] = residual
+    east_face, north_face = east_face_ref[...], north_face_ref[...]
+    direction = search * scale
+    residual = apply_operator(residual_ref[...], direction, diag, east_face, north_face, halos[0], halos[1])
     norms_out[...] = jnp.zeros_like(norms_out)
     norms_out[0:1, 0:LANES] = lane_partial(residual * residual)
     later = search_step(bt_ref, residual, direction, ocean, coef_out, 1, search_ref)
+    answer = direction + later
+    residual = apply_operator(residual, later, diag, east_face, north_face, later_halos[0], later_halos[1])
+    norms_out[0:1, LANES : 2 * LANES] = lane_partial(residual * residual)
+    residual_out[...] = residual
+    later = search_step(bt_ref, residual, later, ocean, coef_out, 2, search_ref)
     direction_out[...] = later
     store_edges(inner_out, outer_out, 0, even, later[0:1], later[columns - 1 :])
-    solution_out[...] = direction + later
+    solution_out[...] = answer + later
 
 
 def advance(k, west, east, residual_ref, direction_ref, solution_ref, diag_ref, east_face_ref, north_face_ref, ocean_ref, faces_ref, coef_ref, bt_ref, search_ref):
@@ -358,6 +431,13 @@
     return lax.ppermute(inner, "lon", pairs), lax.ppermute(outer, "lon", across)
 
 
+def exchange_beyond(near, far):
+    devices = lax.axis_size("lon")
+    within = [(i, i ^ 2) for i in range(devices)]
+    across = [(i, (i + 2 if i % 4 >= 2 else i - 2) % devices) for i in range(devices)]
+    return lax.ppermute(near, "lon", within), lax.ppermute(far, "lon", across)
+
+
 def swap_runs(pack, size, radix):
     devices = lax.axis_size("lon")
     return [
@@ -383,23 +463,25 @@
         40 * MIB,
         pl.CostEstimate(flops=10**9, bytes_accessed=2 * inverse_blocks.size * 4, transcendentals=0),
     )(inverse_blocks)
-    residual, search, diag, east_face, north_face, ocean, east_end, inner, outer = call(
+    pair_shape = shape(PAIR_ROWS, rows)
+    residual, search, diag, east_face, north_face, ocean, east_end, inner, outer, near, far = call(
         first_kernel,
         [vmem()] * 7,
-        [field, field, field, field, field, field, row, two, two],
+        [field, field, field, field, field, field, row, pair_shape, pair_shape, two, two],
         [],
         24 * MIB,
     )(active_tiles.reshape(-1, LANES), right_side, east_coef, north_coef, surface_term, cell_mask, bt)
     low_bound, high_bound, inner = lax.optimization_barrier((low_bound, high_bound, inner))
     inner, outer = exchange(inner, outer)
+    near, far = exchange_beyond(near, far)
     residual, direction, answer, diag, faces, norms, coef, inner, outer = call(
         second_kernel,
-        [smem()] * 2 + [vmem()] * 10,
+        [smem()] * 2 + [vmem()] * 12,
         [field, field, field, field, two, row, shape(SUBS, LANES), row, row],
         [pltpu.VMEM((columns, rows), F32)],
         24 * MIB,
-    )(low_bound, high_bound, inner, outer, residual, search, diag, east_face, north_face, ocean, east_end, bt)
-    for k in range(2, ITERS - 1):
+    )(low_bound, high_bound, inner, outer, near, far, residual, search, diag, east_face, north_face, ocean, east_end, bt)
+    for k in range(3, ITERS - 1):
         inner, outer = exchange(inner, outer)
         residual, direction, answer, norms, inner, outer = call(
             functools.partial(middle_kernel, k),

time: 43.1 us -> 40.1 us (0.930)
  starting transfers between devices: 22.7 us -> 16.5 us
  waiting for transfers between devices: 9.07 us -> 11.9 us
    ppermute x3 -> x2, starting transfers between devices: 14.6 us -> 7.68 us  [exchange(): lax.ppermute(outer, 'lon', across)]
    ppermute x0 -> x2, waiting for transfers between devices: none -> 3.14 us  [exchange_beyond(): return (lax.ppermute(near, 'lon', within), lax.ppermute(far, 'lon', across))]
    ppermute x0 -> x2, starting transfers between devices: none -> 1.91 us  [exchange_beyond(): return (lax.ppermute(near, 'lon', within), lax.ppermute(far, 'lon', across))]
    ppermute x6, waiting for transfers between devices: 6.35 us -> 4.99 us  [swap_runs(): lax.ppermute(pack, 'lon', [(i, i ^ s * size) for i in range(devices)])]
    ppermute x6, starting transfers between devices: 7.46 us -> 6.36 us  [swap_runs(): lax.ppermute(pack, 'lon', [(i, i ^ s * size) for i in range(devices)])]
    ppermute x3 -> x2, waiting for transfers between devices: 2.71 us -> 3.78 us  [exchange(): lax.ppermute(outer, 'lon', across)]
    pallas_call x2 -> x1, Pallas kernels: 1.89 us -> 1.92 us  [on_device(): call(second_kernel, [smem()] * 2 + [vmem()] * 12, [field, field, field, f...]
where the time goes in v4:
time: 40.1 us; the launch traced here: 39.9 us
  starting transfers between devices  16.5 us (41%)
  waiting for transfers between devices  11.9 us (30%)
  Pallas kernels  9.34 us (23%)
  between operations  2.09 us (5%)
    ppermute x2, starting transfers between devices, exchange(): lax.ppermute(outer, 'lon', across)  7.68 us
    ppermute x6, starting transfers between devices, swap_runs(): lax.ppermute(pack, 'lon', [(i, i ^ s * size) for i in range(devices)])  6.36 us
    ppermute x6, waiting for transfers between devices, swap_runs(): lax.ppermute(pack, 'lon', [(i, i ^ s * size) for i in range(devices)])  4.99 us
    pallas_call x1, Pallas kernels, on_device(): call(transpose_kernel, [pl.BlockSpec(memory_space=pl.ANY)], [bt_shape], [...  4.07 us
    ppermute x2, waiting for transfers between devices, exchange(): lax.ppermute(outer, 'lon', across)  3.78 us
    ppermute x2, waiting for transfers between devices, exchange_beyond(): return (lax.ppermute(near, 'lon', within), lax.ppermute(far, 'lon', across))  3.14 us
    pallas_call x1, Pallas kernels, on_device(): call(second_kernel, [smem()] * 2 + [vmem()] * 12, [field, field, field, f...  1.92 us
    ppermute x2, starting transfers between devices, exchange_beyond(): return (lax.ppermute(near, 'lon', within), lax.ppermute(far, 'lon', across))  1.91 us
  transfers between devices with their start and end apart: 12, of which 7 were waited for; matrix products, arithmetic and copies ran while one was open for 0% of the time, Pallas kernels for 0%

profile of v4, /device:TPU:0, one launch (start us, length us, event | category | flops | bytes accessed | tf_op | source)
XLA Modules:
  0.0 39.9 jit_solution(12818634872617987099)
XLA Ops:
  0.6 0.0 copy-start.5
  0.6 0.0 copy-start.4
  0.7 0.0 copy-start.3
  0.7 4.1 %shard_map.112.bt_ref = f32[8,16,128,128]{3,2,1,0:T(8,128)S(1)} custom-call(f32[128,128,128]{2,1,0:T(8,128)} %blocks_hbm.1), custom_call_target="tpu_custom_call" | custom-call | flops 1000000000 | bytes 16777216 | tf_op jit(solution)/shard_map/pallas_call | solution.py:458
  4.8 1.5 %shard_map.113 = (f32[16,1024]{1,0:T(8,128)S(1)}, f32[16,1024]{1,0:T(8,128)S(1)}, f32[16,1024]{1,0:T(8,128)S(1)}, f32[16,1024]{1,0:T(8,128)S(1)}, f32[16,1024]{1...) custom-call(s32[12,128]{1,0:T(8,128)S(1)} %bitcast.1, ...), custom_call_target="tpu_custom_call" | custom-call | tf_op jit(solution)/shard_map/pallas_call | solution.py:467
  6.4 0.5 %collective-permute-start = (f32[24,1024]{1,0:T(8,128)S(1)}, f32[24,1024]{1,0:T(8,128)S(1)}, u32[]{:S(2)}, u32[]{:S(2)}) collective-permute-start(f32[24,1024]{1,0:T(8,128)S(1)} %get-tuple-element.37), channel_id=1, source_target_pairs={{0,1},{1,0},{2,3},{3,2},{4,5},{5,4},{6,7},{7,6},{8,9},{9,8},{10,11... | collective-permute-start | bytes 294920 | tf_op jit(solution)/shard_map/ppermute | solution.py:431
  6.9 5.7 %collective-permute-start.1 = (f32[24,1024]{1,0:T(8,128)S(1)}, f32[24,1024]{1,0:T(8,128)S(1)}, u32[]{:S(2)}, u32[]{:S(2)}) collective-permute-start(f32[24,1024]{1,0:T(8,128)S(1)} %get-tuple-element.38), channel_id=1, source_target_pairs={{0,15},{1,2},{2,1},{3,4},{4,3},{5,6},{6,5},{7,8},{8,7},{9,10},{10,... | collective-permute-start | bytes 294920 | tf_op jit(solution)/shard_map/ppermute | solution.py:431
  12.6 0.0 collective-permute-start.2
  12.6 1.9 %collective-permute-start.3 = (f32[2,1024]{1,0:T(2,128)S(1)}, f32[2,1024]{1,0:T(2,128)S(1)}, u32[]{:S(2)}, u32[]{:S(2)}) collective-permute-start(f32[2,1024]{1,0:T(2,128)S(1)} %get-tuple-element.40), channel_id=1, source_target_pairs={{0,14},{1,15},{2,4},{3,5},{4,2},{5,3},{6,8},{7,9},{8,6},{9,7},{10,... | collective-permute-start | bytes 24584 | tf_op jit(solution)/shard_map/ppermute | solution.py:438
  15.8 0.5 %collective-permute-done.2.near_ref = f32[2,1024]{1,0:T(2,128)S(1)} collective-permute-done((f32[2,1024]{1,0:T(2,128)S(1)}, f32[2,1024]{1,0:T(2,128)S(1)}, u32[]{:S(2)}, u32[]{:S(2)}) %collective-permute-start.2) | collective-permute-done | bytes 8224 | tf_op jit(solution)/shard_map/ppermute | solution.py:438
  16.2 2.7 %collective-permute-done.3.far_ref = f32[2,1024]{1,0:T(2,128)S(1)} collective-permute-done((f32[2,1024]{1,0:T(2,128)S(1)}, f32[2,1024]{1,0:T(2,128)S(1)}, u32[]{:S(2)}, u32[]{:S(2)}) %collective-permute-start.3) | collective-permute-done | bytes 8224 | tf_op jit(solution)/shard_map/ppermute | solution.py:438
  18.9 0.0 collective-permute-done.inner_ref
  18.9 0.0 collective-permute-done.1.outer_ref
  18.9 1.9 %shard_map.114 = (f32[16,1024]{1,0:T(8,128)S(1)}, f32[16,1024]{1,0:T(8,128)S(1)}, f32[16,1024]{1,0:T(8,128)S(1)}, f32[16,1024]{1,0:T(8,128)S(1)}, f32[2,1024]{1,...) custom-call(f32[1]{0:T(128)S(6)} %copy.12.low_ref, ...), custom_call_target="tpu_custom_call" | custom-call | tf_op jit(solution)/shard_map/pallas_call | solution.py:477
  20.8 0.1 collective-permute-start.4
  20.9 2.0 %collective-permute-start.5 = (f32[1,1024]{1,0:T(1,128)S(1)}, f32[1,1024]{1,0:T(1,128)S(1)}, u32[]{:S(2)}, u32[]{:S(2)}) collective-permute-start(f32[1,1024]{1,0:T(1,128)S(1)} %get-tuple-element.49), channel_id=1, source_target_pairs={{0,15},{1,2},{2,1},{3,4},{4,3},{5,6},{6,5},{7,8},{8,7},{9,10},{10,... | collective-permute-start | bytes 12296 | tf_op jit(solution)/shard_map/ppermute | solution.py:431
  22.9 0.0 collective-permute-done.4.inner_ref
  22.9 3.8 %collective-permute-done.5.outer_ref = f32[1,1024]{1,0:T(1,128)S(1)} collective-permute-done((f32[1,1024]{1,0:T(1,128)S(1)}, f32[1,1024]{1,0:T(1,128)S(1)}, u32[]{:S(2)}, u32[]{:S(2)}) %collective-permute-start.5) | collective-permute-done | bytes 4128 | tf_op jit(solution)/shard_map/ppermute | solution.py:431
  26.7 1.0 %shard_map.115 = (f32[16,1024]{1,0:T(8,128)S(1)}, f32[16,1024]{1,0:T(8,128)S(1)}, f32[8,1024]{1,0:T(8,128)S(1)}) custom-call(f32[1,1024]{1,0:T(1,128)S(1)} %collective-permute-done.4.inner_ref, f32[1,1024]{1,0:T(1,128)S(1)} %collective-permute-done.5.outer_ref, f32[16,1024]{1,0:T(8,128)S(1)} %get-tuple-element.50.residual_ref, ...), custom_call_target="tpu_custom_call" | custom-call | tf_op jit(solution)/shard_map/pallas_call | solution.py:495
  27.8 0.1 collective-permute-start.8
  27.8 0.1 collective-permute-start.7
  27.9 1.8 %collective-permute-start.6 = (f32[8,1024]{1,0:T(8,128)S(1)}, f32[8,1024]{1,0:T(8,128)S(1)}, u32[]{:S(2)}, u32[]{:S(2)}) collective-permute-start(f32[8,1024]{1,0:T(8,128)S(1)} %get-tuple-element.57.refs_0_), channel_id=1, source_target_pairs={{0,1},{1,0},{2,3},{3,2},{4,5},{5,4},{6,7},{7,6},{8,9},{9,8},{10,11... | collective-permute-start | bytes 98312 | tf_op jit(solution)/shard_map/ppermute | solution.py:444
  29.7 1.5 %collective-permute-done.8.refs_3_ = f32[8,1024]{1,0:T(8,128)S(1)} collective-permute-done((f32[8,1024]{1,0:T(8,128)S(1)}, f32[8,1024]{1,0:T(8,128)S(1)}, u32[]{:S(2)}, u32[]{:S(2)}) %collective-permute-start.8) | collective-permute-done | bytes 32800 | tf_op jit(solution)/shard_map/ppermute | solution.py:444
  31.2 0.7 %collective-permute-done.7.refs_2_ = f32[8,1024]{1,0:T(8,128)S(1)} collective-permute-done((f32[8,1024]{1,0:T(8,128)S(1)}, f32[8,1024]{1,0:T(8,128)S(1)}, u32[]{:S(2)}, u32[]{:S(2)}) %collective-permute-start.7) | collective-permute-done | bytes 32800 | tf_op jit(solution)/shard_map/ppermute | solution.py:444
  31.9 0.0 collective-permute-done.6.refs_1_
  31.9 2.4 %collective-permute-start.11 = (f32[8,1024]{1,0:T(8,128)S(1)}, f32[8,1024]{1,0:T(8,128)S(1)}, u32[]{:S(2)}, u32[]{:S(2)}) collective-permute-start(f32[8,1024]{1,0:T(8,128)S(1)} %get-tuple-element.58.refs_0_), channel_id=1, source_target_pairs={{0,12},{1,13},{2,14},{3,15},{4,8},{5,9},{6,10},{7,11},{8,4},{9,5},... | collective-permute-start | bytes 98312 | tf_op jit(solution)/shard_map/ppermute | solution.py:444
  34.4 0.0 collective-permute-start.10
  34.4 2.0 %collective-permute-start.9 = (f32[8,1024]{1,0:T(8,128)S(1)}, f32[8,1024]{1,0:T(8,128)S(1)}, u32[]{:S(2)}, u32[]{:S(2)}) collective-permute-start(f32[8,1024]{1,0:T(8,128)S(1)} %get-tuple-element.58.refs_0_), channel_id=1, source_target_pairs={{0,4},{1,5},{2,6},{3,7},{4,0},{5,1},{6,2},{7,3},{8,12},{9,13},{10,... | collective-permute-start | bytes 98312 | tf_op jit(solution)/shard_map/ppermute | solution.py:444
  36.4 1.3 %collective-permute-done.11.refs_3_ = f32[8,1024]{1,0:T(8,128)S(1)} collective-permute-done((f32[8,1024]{1,0:T(8,128)S(1)}, f32[8,1024]{1,0:T(8,128)S(1)}, u32[]{:S(2)}, u32[]{:S(2)}) %collective-permute-start.11) | collective-permute-done | bytes 32800 | tf_op jit(solution)/shard_map/ppermute | solution.py:444
  37.7 1.5 %collective-permute-done.10.refs_2_ = f32[8,1024]{1,0:T(8,128)S(1)} collective-permute-done((f32[8,1024]{1,0:T(8,128)S(1)}, f32[8,1024]{1,0:T(8,128)S(1)}, u32[]{:S(2)}, u32[]{:S(2)}) %collective-permute-start.10) | collective-permute-done | bytes 32800 | tf_op jit(solution)/shard_map/ppermute | solution.py:444
  39.2 0.0 collective-permute-done.9.refs_1_
  39.2 0.7 %shard_map.117 = (f32[16,1024]{1,0:T(8,128)}, f32[16,1024]{1,0:T(8,128)}, f32[4]{0:T(128)}) custom-call(f32[8,1024]{1,0:T(8,128)S(1)} %get-tuple-element.58.refs_0_, f32[8,1024]{1,0:T(8,128)S(1)} %collective-permute-done.9.refs_1_, f32[8,1024]{1,0:T(8,128)S(1)} %collective-permute-done.10.refs_2_, f32[8,1024]{1,0:T(8,128)S(1)} %collective-permute-done.11.refs_3_, ...), custom_call_target="tpu_custom_call" | custom-call | tf_op jit(solution)/shard_map/pallas_call | solution.py:518
  (10 shorter events, 0.1 us)
Async XLA Ops:
  0.6 4.1 %copy-start.5 = (s32[1536]{0:T(1024)S(1)}, s32[1536]{0:T(1024)}, u32[]{:S(2)}) copy-start(s32[1536]{0:T(1024)} %param.15) | copy-start | bytes 18436
  0.6 4.1 %copy-start.4 = (s32[16,1024]{1,0:T(8,128)S(1)}, s32[16,1024]{1,0:T(8,128)}, u32[]{:S(2)}) copy-start(s32[16,1024]{1,0:T(8,128)} %mask_ref.1) | copy-start | bytes 196612
  0.7 4.1 %copy-start.3 = (f32[16,1024]{1,0:T(8,128)S(1)}, f32[16,1024]{1,0:T(8,128)}, u32[]{:S(2)}) copy-start(f32[16,1024]{1,0:T(8,128)} %surface_ref.1) | copy-start | bytes 196612
  0.7 4.1 %copy-start.2 = (f32[16,1024]{1,0:T(8,128)S(1)}, f32[16,1024]{1,0:T(8,128)}, u32[]{:S(2)}) copy-start(f32[16,1024]{1,0:T(8,128)} %north_ref.1) | copy-start | bytes 196612
  0.7 4.1 %copy-start.1 = (f32[16,1024]{1,0:T(8,128)S(1)}, f32[16,1024]{1,0:T(8,128)}, u32[]{:S(2)}) copy-start(f32[16,1024]{1,0:T(8,128)} %east_ref.1) | copy-start | bytes 196612
  0.7 4.1 %copy-start = (f32[16,1024]{1,0:T(8,128)S(1)}, f32[16,1024]{1,0:T(8,128)}, u32[]{:S(2)}) copy-start(f32[16,1024]{1,0:T(8,128)} %right_ref.1) | copy-start | bytes 196612
  6.4 12.5 %collective-permute-start = (f32[24,1024]{1,0:T(8,128)S(1)}, f32[24,1024]{1,0:T(8,128)S(1)}, u32[]{:S(2)}, u32[]{:S(2)}) collective-permute-start(f32[24,1024]{1,0:T(8,128)S(1)} %get-tuple-element.37), channel_id=1, source_target_pairs={{0,1},{1,0},{2,3},{3,2},{4,5},{5,4},{6,7},{7,6},{8,9},{9,8},{10,11... | collective-permute-start | bytes 294920 | tf_op jit(solution)/shard_map/ppermute | solution.py:431
  6.9 12.0 %collective-permute-start.1 = (f32[24,1024]{1,0:T(8,128)S(1)}, f32[24,1024]{1,0:T(8,128)S(1)}, u32[]{:S(2)}, u32[]{:S(2)}) collective-permute-start(f32[24,1024]{1,0:T(8,128)S(1)} %get-tuple-element.38), channel_id=1, source_target_pairs={{0,15},{1,2},{2,1},{3,4},{4,3},{5,6},{6,5},{7,8},{8,7},{9,10},{10,... | collective-permute-start | bytes 294920 | tf_op jit(solution)/shard_map/ppermute | solution.py:431
  12.6 3.7 %collective-permute-start.2 = (f32[2,1024]{1,0:T(2,128)S(1)}, f32[2,1024]{1,0:T(2,128)S(1)}, u32[]{:S(2)}, u32[]{:S(2)}) collective-permute-start(f32[2,1024]{1,0:T(2,128)S(1)} %get-tuple-element.39), channel_id=1, source_target_pairs={{0,2},{1,3},{2,0},{3,1},{4,6},{5,7},{6,4},{7,5},{8,10},{9,11},{10,... | collective-permute-start | bytes 24584 | tf_op jit(solution)/shard_map/ppermute | solution.py:438
  12.6 6.3 %collective-permute-start.3 = (f32[2,1024]{1,0:T(2,128)S(1)}, f32[2,1024]{1,0:T(2,128)S(1)}, u32[]{:S(2)}, u32[]{:S(2)}) collective-permute-start(f32[2,1024]{1,0:T(2,128)S(1)} %get-tuple-element.40), channel_id=1, source_target_pairs={{0,14},{1,15},{2,4},{3,5},{4,2},{5,3},{6,8},{7,9},{8,6},{9,7},{10,... | collective-permute-start | bytes 24584 | tf_op jit(solution)/shard_map/ppermute | solution.py:438
  20.8 2.1 %collective-permute-start.4 = (f32[1,1024]{1,0:T(1,128)S(1)}, f32[1,1024]{1,0:T(1,128)S(1)}, u32[]{:S(2)}, u32[]{:S(2)}) collective-permute-start(f32[1,1024]{1,0:T(1,128)S(1)} %get-tuple-element.48), channel_id=1, source_target_pairs={{0,1},{1,0},{2,3},{3,2},{4,5},{5,4},{6,7},{7,6},{8,9},{9,8},{10,11... | collective-permute-start | bytes 12296 | tf_op jit(solution)/shard_map/ppermute | solution.py:431
  20.9 5.8 %collective-permute-start.5 = (f32[1,1024]{1,0:T(1,128)S(1)}, f32[1,1024]{1,0:T(1,128)S(1)}, u32[]{:S(2)}, u32[]{:S(2)}) collective-permute-start(f32[1,1024]{1,0:T(1,128)S(1)} %get-tuple-element.49), channel_id=1, source_target_pairs={{0,15},{1,2},{2,1},{3,4},{4,3},{5,6},{6,5},{7,8},{8,7},{9,10},{10,... | collective-permute-start | bytes 12296 | tf_op jit(solution)/shard_map/ppermute | solution.py:431
  27.8 3.4 %collective-permute-start.8 = (f32[8,1024]{1,0:T(8,128)S(1)}, f32[8,1024]{1,0:T(8,128)S(1)}, u32[]{:S(2)}, u32[]{:S(2)}) collective-permute-start(f32[8,1024]{1,0:T(8,128)S(1)} %get-tuple-element.57.refs_0_), channel_id=1, source_target_pairs={{0,3},{1,2},{2,1},{3,0},{4,7},{5,6},{6,5},{7,4},{8,11},{9,10},{10,... | collective-permute-start | bytes 98312 | tf_op jit(solution)/shard_map/ppermute | solution.py:444
  27.8 4.0 %collective-permute-start.7 = (f32[8,1024]{1,0:T(8,128)S(1)}, f32[8,1024]{1,0:T(8,128)S(1)}, u32[]{:S(2)}, u32[]{:S(2)}) collective-permute-start(f32[8,1024]{1,0:T(8,128)S(1)} %get-tuple-element.57.refs_0_), channel_id=1, source_target_pairs={{0,2},{1,3},{2,0},{3,1},{4,6},{5,7},{6,4},{7,5},{8,10},{9,11},{10,... | collective-permute-start | bytes 98312 | tf_op jit(solution)/shard_map/ppermute | solution.py:444
  27.9 4.0 %collective-permute-start.6 = (f32[8,1024]{1,0:T(8,128)S(1)}, f32[8,1024]{1,0:T(8,128)S(1)}, u32[]{:S(2)}, u32[]{:S(2)}) collective-permute-start(f32[8,1024]{1,0:T(8,128)S(1)} %get-tuple-element.57.refs_0_), channel_id=1, source_target_pairs={{0,1},{1,0},{2,3},{3,2},{4,5},{5,4},{6,7},{7,6},{8,9},{9,8},{10,11... | collective-permute-start | bytes 98312 | tf_op jit(solution)/shard_map/ppermute | solution.py:444
  31.9 5.8 %collective-permute-start.11 = (f32[8,1024]{1,0:T(8,128)S(1)}, f32[8,1024]{1,0:T(8,128)S(1)}, u32[]{:S(2)}, u32[]{:S(2)}) collective-permute-start(f32[8,1024]{1,0:T(8,128)S(1)} %get-tuple-element.58.refs_0_), channel_id=1, source_target_pairs={{0,12},{1,13},{2,14},{3,15},{4,8},{5,9},{6,10},{7,11},{8,4},{9,5},... | collective-permute-start | bytes 98312 | tf_op jit(solution)/shard_map/ppermute | solution.py:444
  34.4 4.8 %collective-permute-start.10 = (f32[8,1024]{1,0:T(8,128)S(1)}, f32[8,1024]{1,0:T(8,128)S(1)}, u32[]{:S(2)}, u32[]{:S(2)}) collective-permute-start(f32[8,1024]{1,0:T(8,128)S(1)} %get-tuple-element.58.refs_0_), channel_id=1, source_target_pairs={{0,8},{1,9},{2,10},{3,11},{4,12},{5,13},{6,14},{7,15},{8,0},{9,1},... | collective-permute-start | bytes 98312 | tf_op jit(solution)/shard_map/ppermute | solution.py:444
  34.4 4.8 %collective-permute-start.9 = (f32[8,1024]{1,0:T(8,128)S(1)}, f32[8,1024]{1,0:T(8,128)S(1)}, u32[]{:S(2)}, u32[]{:S(2)}) collective-permute-start(f32[8,1024]{1,0:T(8,128)S(1)} %get-tuple-element.58.refs_0_), channel_id=1, source_target_pairs={{0,4},{1,5},{2,6},{3,7},{4,0},{5,1},{6,2},{7,3},{8,12},{9,13},{10,... | collective-permute-start | bytes 98312 | tf_op jit(solution)/shard_map/ppermute | solution.py:444

commit v5 on v4

--- a/solution.py
+++ b/solution.py
@@ -120,7 +120,7 @@
 
 def first_kernel(
     active_ref, right_ref, east_ref, north_ref, surface_ref, mask_ref, bt_ref,
-    residual_ref, search_ref, diag_ref, east_face_ref, north_face_ref, ocean_ref, east_end_ref, inner_ref, outer_ref, near_ref, far_ref,
+    residual_ref, search_ref, diag_ref, east_face_ref, north_face_ref, ocean_ref, east_end_ref, flow_ref, inner_ref, outer_ref, near_ref, far_ref,
 ):
     columns, rows = right_ref.shape
     count = lane_blocks(rows)
@@ -153,6 +153,7 @@
     search_ref[...] = search
     nothing = jnp.zeros_like(east_end)
     flow = apply_operator(jnp.zeros_like(search), -search, diag, east_face, north_face, nothing, nothing)
+    flow_ref[...] = flow
     edges = edge_products(bt_ref, flow)
     fields = (
         (PAIR_SEARCH, search[0:1], search[columns - 1 :]),
@@ -222,16 +223,40 @@
     return keep * (scale * search) + gain * (search - scale * flow + jnp.concatenate(parts, axis=1))
 
 
+def side_products(bt_ref, first, last):
+    count, columns = bt_ref.shape[:2]
+    index = gather_index()
+    blocks = []
+    for block in range(count):
+        west, east = expand(first, block, index), expand(last, block, index)
+        rows = [
+            jnp.sum(bt_ref[block, a, :SUBS] * west + bt_ref[block, a, LANES - SUBS :] * east, axis=0, keepdims=True)
+            for a in range(columns)
+        ]
+        blocks.append(jnp.concatenate(rows, axis=0))
+    return jnp.concatenate(blocks, axis=1)
+
+
+def add_sides(field, first, last):
+    lon = lax.broadcasted_iota(jnp.int32, field.shape, 0)
+    field = jnp.where(lon == 0, field + first, field)
+    return jnp.where(lon == field.shape[0] - 1, field + last, field)
+
+
+def product_kernel(bt_ref, field_ref, out_ref):
+    blocks_product(bt_ref, field_ref[...], out_ref)
+
+
 def second_kernel(
-    low_ref, high_ref, inner_ref, outer_ref, near_ref, far_ref, residual_ref, search_in, diag_ref, east_face_ref, north_face_ref, ocean_ref, east_end_ref, bt_ref,
-    residual_out, direction_out, solution_out, diag_out, faces_out, norms_out, coef_out, inner_out, outer_out,
-    search_ref,
+    low_ref, high_ref, inner_ref, outer_ref, near_ref, far_ref, residual_ref, search_ref, flow_ref, product_ref, diag_ref, east_face_ref, north_face_ref, ocean_ref, east_end_ref, bt_ref,
+    residual_out, direction_out, diag_out, faces_out, norms_out, coef_out, inner_out, outer_out,
 ):
     store_coefficients(low_ref, high_ref, coef_out)
     ocean = ocean_ref[...]
     columns, rows = ocean.shape
-    scale = repeat_row(coef_out[0:1], lane_blocks(rows))
-    search = search_in[...]
+    count = lane_blocks(rows)
+    scale, keep, gain, keep_next, gain_next = (repeat_row(coef_out[n : n + 1], count) for n in (0, 2, 3, 4, 5))
+    search = search_ref[...]
     even, low = even_device(), low_device()
     sides = [halo_rows(inner_ref, outer_ref, row, even) for row in range(PAIR_BACK_FACE + 1)]
     beyond = [
@@ -240,7 +265,7 @@
     ]
     here = (search[0:1], search[columns - 1 :])
     static = (ocean[0:1], east_end_ref[...])
-    faces, halos, later_halos = [], [], []
+    faces, pushes, later_halos = [], [], []
     for side in range(2):
         there, flow, face, back, back_face = (pair[side] for pair in sides)
         face = static[side] * face
@@ -251,39 +276,26 @@
             jnp.where(from_inner, inner_ref[row : row + SUBS], outer_ref[row : row + SUBS]) for row in (PAIR_OWN, PAIR_OPPOSITE)
         )
         faces.append(face)
-        halos.append(face * (scale * there))
+        pushes.append(-own_push)
         later_halos.append(face * neighbour_direction(own, opposite, there, flow, own_push, opposite_push, coef_out))
     faces_out[0:1] = faces[0]
     faces_out[1:2] = faces[1]
-    lon = lax.broadcasted_iota(jnp.int32, ocean.shape, 0)
-    diag = diag_ref[...]
-    diag = jnp.where(lon == 0, diag + faces[0], diag)
-    diag = jnp.where(lon == columns - 1, diag + faces[1], diag)
+    diag = add_sides(diag_ref[...], faces[0], faces[1])
     diag_out[...] = diag
-    east_face, north_face = east_face_ref[...], north_face_ref[...]
-    direction = search * scale
-    residual = apply_operator(residual_ref[...], direction, diag, east_face, north_face, halos[0], halos[1])
+    residual = add_sides(residual_ref[...] - scale * flow_ref[...], pushes[0], pushes[1])
     norms_out[...] = jnp.zeros_like(norms_out)
     norms_out[0:1, 0:LANES] = lane_partial(residual * residual)
-    later = search_step(bt_ref, residual, direction, ocean, coef_out, 1, search_ref)
-    answer = direction + later
-    residual = apply_operator(residual, later, diag, east_face, north_face, later_halos[0], later_halos[1])
-    norms_out[0:1, LANES : 2 * LANES] = lane_partial(residual * residual)
+    product = side_products(bt_ref, pushes[0], pushes[1]) - scale * product_ref[...]
+    direction = keep * (scale * search) + gain * (search + ocean * product)
+    direction_out[...] = direction
+    residual = apply_operator(residual, direction, diag, east_face_ref[...], north_face_ref[...], later_halos[0], later_halos[1])
     residual_out[...] = residual
-    later = search_step(bt_ref, residual, later, ocean, coef_out, 2, search_ref)
-    direction_out[...] = later
-    store_edges(inner_out, outer_out, 0, even, later[0:1], later[columns - 1 :])
-    solution_out[...] = answer + later
-
-
-def advance(k, west, east, residual_ref, direction_ref, solution_ref, diag_ref, east_face_ref, north_face_ref, ocean_ref, faces_ref, coef_ref, bt_ref, search_ref):
-    direction = direction_ref[...]
-    residual = apply_operator(
-        residual_ref[...], direction, diag_ref[...], east_face_ref[...], north_face_ref[...],
-        faces_ref[0:1] * west, faces_ref[1:2] * east,
+    first, last = edge_products(bt_ref, residual)
+    store_edges(
+        inner_out, outer_out, 0, even,
+        keep_next * direction[0:1] + gain_next * (ocean[0:1] * first),
+        keep_next * direction[columns - 1 :] + gain_next * (ocean[columns - 1 :] * last),
     )
-    later = search_step(bt_ref, residual, direction, ocean_ref[...], coef_ref, k, search_ref)
-    return residual, later, solution_ref[...] + later
 
 
 def store_norm(norms_out, norms_ref, k, squares):
@@ -291,37 +303,37 @@
     norms_out[0:1, k * LANES : (k + 1) * LANES] = lane_partial(squares)
 
 
-def middle_kernel(
-    k,
-    inner_ref, outer_ref, residual_ref, direction_ref, solution_ref, diag_ref, east_face_ref, north_face_ref, ocean_ref, faces_ref, coef_ref, norms_ref, bt_ref,
-    residual_out, direction_out, solution_out, norms_out, inner_out, outer_out,
-    search_ref,
+def ahead_kernel(
+    residual_ref, direction_ref, search_ref, diag_ref, east_face_ref, north_face_ref, ocean_ref, coef_ref, norms_ref, bt_ref,
+    residual_out, direction_out, solution_out, product_out, norms_out,
 ):
-    even = even_device()
-    west, east = halo_rows(inner_ref, outer_ref, 0, even)
-    residual, later, answer = advance(
-        k, west, east, residual_ref, direction_ref, solution_ref, diag_ref, east_face_ref, north_face_ref, ocean_ref, faces_ref, coef_ref, bt_ref, search_ref
-    )
+    residual = residual_ref[...]
+    direction = direction_ref[...]
+    store_norm(norms_out, norms_ref, 1, residual * residual)
+    later = search_step(bt_ref, residual, direction, ocean_ref[...], coef_ref, 2, product_out)
+    direction_out[...] = later
+    scale = repeat_row(coef_ref[0:1], lane_blocks(residual.shape[1]))
+    solution_out[...] = scale * search_ref[...] + direction + later
+    nothing = jnp.zeros((1, residual.shape[1]), F32)
+    residual = apply_operator(residual, later, diag_ref[...], east_face_ref[...], north_face_ref[...], nothing, nothing)
     residual_out[...] = residual
-    store_norm(norms_out, norms_ref, k - 1, residual * residual)
-    direction_out[...] = later
-    store_edges(inner_out, outer_out, 0, even, later[0:1], later[-1:])
-    solution_out[...] = answer
+    blocks_product(bt_ref, residual, product_out)
 
 
 FIRST_RES, FIRST_DIR, LAST_RES, LAST_DIR, LAST_FACE, SUMS, PACK_ROWS = 0, 1, 2, 3, 4, 5, 8
 
 
 def closing_kernel(
-    inner_ref, outer_ref, residual_ref, direction_ref, solution_ref, diag_ref, east_face_ref, north_face_ref, ocean_ref, faces_ref, coef_ref, norms_ref, bt_ref,
+    inner_ref, outer_ref, residual_ref, direction_ref, solution_ref, product_ref, diag_ref, east_face_ref, north_face_ref, ocean_ref, faces_ref, coef_ref, norms_ref, bt_ref,
     residual_out, solution_out, pack_out,
-    search_ref,
 ):
     west, east = halo_rows(inner_ref, outer_ref, 0, even_device())
-    residual, later, answer = advance(
-        ITERS - 1, west, east, residual_ref, direction_ref, solution_ref, diag_ref, east_face_ref, north_face_ref, ocean_ref, faces_ref, coef_ref, bt_ref, search_ref
-    )
-    solution_out[...] = answer
+    west, east = faces_ref[0:1] * west, faces_ref[1:2] * east
+    residual = add_sides(residual_ref[...], west, east)
+    keep, gain = (repeat_row(coef_ref[n : n + 1], lane_blocks(residual.shape[1])) for n in (2 * ITERS - 2, 2 * ITERS - 1))
+    product = product_ref[...] + side_products(bt_ref, west, east)
+    later = keep * direction_ref[...] + gain * (ocean_ref[...] * product)
+    solution_out[...] = solution_ref[...] + later
     columns = residual.shape[0]
     sums = pack_out.at[SUMS : SUMS + 1]
     store_norm(sums, norms_ref, ITERS - 2, residual * residual)
@@ -464,41 +476,41 @@
         pl.CostEstimate(flops=10**9, bytes_accessed=2 * inverse_blocks.size * 4, transcendentals=0),
     )(inverse_blocks)
     pair_shape = shape(PAIR_ROWS, rows)
-    residual, search, diag, east_face, north_face, ocean, east_end, inner, outer, near, far = call(
+    residual, search, diag, east_face, north_face, ocean, east_end, flow, inner, outer, near, far = call(
         first_kernel,
         [vmem()] * 7,
-        [field, field, field, field, field, field, row, pair_shape, pair_shape, two, two],
+        [field, field, field, field, field, field, row, field, pair_shape, pair_shape, two, two],
         [],
         24 * MIB,
     )(active_tiles.reshape(-1, LANES), right_side, east_coef, north_coef, surface_term, cell_mask, bt)
     low_bound, high_bound, inner = lax.optimization_barrier((low_bound, high_bound, inner))
     inner, outer = exchange(inner, outer)
     near, far = exchange_beyond(near, far)
-    residual, direction, answer, diag, faces, norms, coef, inner, outer = call(
+    work = pl.CostEstimate(flops=2 * bt.size, bytes_accessed=4 * bt.size, transcendentals=0)
+    (product,) = call(product_kernel, [vmem()] * 2, [field], [], 24 * MIB, work)(bt, flow)
+    residual, direction, diag, faces, norms, coef, inner, outer = call(
         second_kernel,
-        [smem()] * 2 + [vmem()] * 12,
-        [field, field, field, field, two, row, shape(SUBS, LANES), row, row],
-        [pltpu.VMEM((columns, rows), F32)],
+        [smem()] * 2 + [vmem()] * 14,
+        [field, field, field, two, row, shape(SUBS, LANES), row, row],
+        [],
         24 * MIB,
-    )(low_bound, high_bound, inner, outer, near, far, residual, search, diag, east_face, north_face, ocean, east_end, bt)
-    for k in range(3, ITERS - 1):
-        inner, outer = exchange(inner, outer)
-        residual, direction, answer, norms, inner, outer = call(
-            functools.partial(middle_kernel, k),
-            [vmem()] * 13,
-            [field, field, field, row, row, row],
-            [pltpu.VMEM((columns, rows), F32)],
-            24 * MIB,
-        )(inner, outer, residual, direction, answer, diag, east_face, north_face, ocean, faces, coef, norms, bt)
+    )(
+        low_bound, high_bound, inner, outer, near, far, residual, search, flow, product, diag, east_face, north_face,
+        ocean, east_end, bt,
+    )
     inner, outer = exchange(inner, outer)
+    residual, direction, answer, product, norms = call(
+        ahead_kernel,
+        [vmem()] * 10,
+        [field, field, field, field, row],
+        [],
+        24 * MIB,
+        work,
+    )(residual, direction, search, diag, east_face, north_face, ocean, coef, norms, bt)
     pack_shape = shape(PACK_ROWS, rows)
-    residual, answer, pack = call(
-        closing_kernel,
-        [vmem()] * 13,
-        [field, field, pack_shape],
-        [pltpu.VMEM((columns, rows), F32)],
-        24 * MIB,
-    )(inner, outer, residual, direction, answer, diag, east_face, north_face, ocean, faces, coef, norms, bt)
+    residual, answer, pack = call(closing_kernel, [vmem()] * 14, [field, field, pack_shape], [], 24 * MIB)(
+        inner, outer, residual, direction, answer, product, diag, east_face, north_face, ocean, faces, coef, norms, bt
+    )
     devices = lax.axis_size("lon")
     size, halo = 1, []
     while True:

time: 40.1 us -> 38.2 us (0.953)
  waiting for transfers between devices: 11.9 us -> 9.47 us
  Pallas kernels: 9.34 us -> 9.84 us
    ppermute x2, waiting for transfers between devices: 3.78 us -> 2.11 us  [exchange(): lax.ppermute(outer, 'lon', across)]
    ppermute x2, waiting for transfers between devices: 3.14 us -> 2.36 us  [exchange_beyond(): return (lax.ppermute(near, 'lon', within), lax.ppermute(far, 'lon', across))]
    pallas_call x2 -> x4, Pallas kernels: 2.96 us -> 3.45 us  [the longest x1 1.65 us: on_device(): call(ahead_kernel, [vmem()] * 10, [field, field, field, field, row], [],...]
  transfers between devices with their start and end apart: 12 -> 12, of which waited for: 7 -> 6; matrix products, arithmetic and copies ran while one was open for 0% -> 0% of each run, Pallas kernels for 0% -> 6%
where the time goes in v5:
time: 38.2 us; the launch traced here: 38 us
  starting transfers between devices  16.5 us (43%)
  Pallas kernels  9.84 us (26%)
  waiting for transfers between devices  9.47 us (25%)
  between operations  2.12 us (6%)
    ppermute x2, starting transfers between devices, exchange(): lax.ppermute(outer, 'lon', across)  7.68 us
    ppermute x6, starting transfers between devices, swap_runs(): lax.ppermute(pack, 'lon', [(i, i ^ s * size) for i in range(devices)])  6.36 us
    ppermute x6, waiting for transfers between devices, swap_runs(): lax.ppermute(pack, 'lon', [(i, i ^ s * size) for i in range(devices)])  4.99 us
    pallas_call x1, Pallas kernels, on_device(): call(transpose_kernel, [pl.BlockSpec(memory_space=pl.ANY)], [bt_shape], [...  4.07 us
    ppermute x2, waiting for transfers between devices, exchange_beyond(): return (lax.ppermute(near, 'lon', within), lax.ppermute(far, 'lon', across))  2.36 us
    ppermute x2, waiting for transfers between devices, exchange(): lax.ppermute(outer, 'lon', across)  2.11 us
    ppermute x2, starting transfers between devices, exchange_beyond(): return (lax.ppermute(near, 'lon', within), lax.ppermute(far, 'lon', across))  1.91 us
    pallas_call x1, Pallas kernels, on_device(): call(ahead_kernel, [vmem()] * 10, [field, field, field, field, row], [],...  1.65 us
  transfers between devices with their start and end apart: 12, of which 6 were waited for; matrix products, arithmetic and copies ran while one was open for 0% of the time, Pallas kernels for 6%

profile of v5, /device:TPU:0, one launch (start us, length us, event | category | flops | bytes accessed | tf_op | source)
XLA Modules:
  0.0 38.0 jit_solution(7727984061068558377)
XLA Ops:
  0.6 0.0 copy-start.5
  0.7 4.1 %shard_map.112.bt_ref = f32[8,16,128,128]{3,2,1,0:T(8,128)S(1)} custom-call(f32[128,128,128]{2,1,0:T(8,128)} %blocks_hbm.1), custom_call_target="tpu_custom_call" | custom-call | flops 1000000000 | bytes 16777216 | tf_op jit(solution)/shard_map/pallas_call | solution.py:470
  4.8 1.5 %shard_map.113 = (f32[16,1024]{1,0:T(8,128)S(1)}, f32[16,1024]{1,0:T(8,128)S(1)}, f32[16,1024]{1,0:T(8,128)S(1)}, f32[16,1024]{1,0:T(8,128)S(1)}, f32[16,1024]{1...) custom-call(s32[12,128]{1,0:T(8,128)S(1)} %bitcast.1, ...), custom_call_target="tpu_custom_call" | custom-call | tf_op jit(solution)/shard_map/pallas_call | solution.py:479
  6.4 0.5 %collective-permute-start = (f32[24,1024]{1,0:T(8,128)S(1)}, f32[24,1024]{1,0:T(8,128)S(1)}, u32[]{:S(2)}, u32[]{:S(2)}) collective-permute-start(f32[24,1024]{1,0:T(8,128)S(1)} %get-tuple-element.42), channel_id=1, source_target_pairs={{0,1},{1,0},{2,3},{3,2},{4,5},{5,4},{6,7},{7,6},{8,9},{9,8},{10,11... | collective-permute-start | bytes 294920 | tf_op jit(solution)/shard_map/ppermute | solution.py:443
  6.9 5.7 %collective-permute-start.1 = (f32[24,1024]{1,0:T(8,128)S(1)}, f32[24,1024]{1,0:T(8,128)S(1)}, u32[]{:S(2)}, u32[]{:S(2)}) collective-permute-start(f32[24,1024]{1,0:T(8,128)S(1)} %get-tuple-element.43), channel_id=1, source_target_pairs={{0,15},{1,2},{2,1},{3,4},{4,3},{5,6},{6,5},{7,8},{8,7},{9,10},{10,... | collective-permute-start | bytes 294920 | tf_op jit(solution)/shard_map/ppermute | solution.py:443
  12.6 0.0 collective-permute-start.2
  12.6 1.9 %collective-permute-start.3 = (f32[2,1024]{1,0:T(2,128)S(1)}, f32[2,1024]{1,0:T(2,128)S(1)}, u32[]{:S(2)}, u32[]{:S(2)}) collective-permute-start(f32[2,1024]{1,0:T(2,128)S(1)} %get-tuple-element.45), channel_id=1, source_target_pairs={{0,14},{1,15},{2,4},{3,5},{4,2},{5,3},{6,8},{7,9},{8,6},{9,7},{10,... | collective-permute-start | bytes 24584 | tf_op jit(solution)/shard_map/ppermute | solution.py:450
  15.8 0.8 %shard_map.114.product_ref = f32[16,1024]{1,0:T(8,128)S(1)} custom-call(f32[8,16,128,128]{3,2,1,0:T(8,128)S(1)} %shard_map.112.bt_ref, f32[16,1024]{1,0:T(8,128)S(1)} %get-tuple-element.48.field_ref.flow_ref), custom_call_target="tpu_custom_call" | custom-call | flops 4194304 | bytes 8388608 | tf_op jit(solution)/shard_map/pallas_call | solution.py:490
  16.5 0.0 collective-permute-done.2.near_ref
  16.6 2.4 %collective-permute-done.3.far_ref = f32[2,1024]{1,0:T(2,128)S(1)} collective-permute-done((f32[2,1024]{1,0:T(2,128)S(1)}, f32[2,1024]{1,0:T(2,128)S(1)}, u32[]{:S(2)}, u32[]{:S(2)}) %collective-permute-start.3) | collective-permute-done | bytes 8224 | tf_op jit(solution)/shard_map/ppermute | solution.py:450
  18.9 0.0 collective-permute-done.inner_ref
  18.9 0.0 collective-permute-done.1.outer_ref
  18.9 0.7 %shard_map.115 = (f32[16,1024]{1,0:T(8,128)S(1)}, f32[16,1024]{1,0:T(8,128)S(1)}, f32[16,1024]{1,0:T(8,128)S(1)}, f32[2,1024]{1,0:T(2,128)S(1)}, f32[1,1024]{1,0...) custom-call(f32[1]{0:T(128)S(6)} %copy.12.low_ref, f32[1]{0:T(128)S(6)} %copy.13.high_ref, ...), custom_call_target="tpu_custom_call" | custom-call | tf_op jit(solution)/shard_map/pallas_call | solution.py:491
  19.6 0.1 collective-permute-start.4
  19.7 2.0 %collective-permute-start.5 = (f32[1,1024]{1,0:T(1,128)S(1)}, f32[1,1024]{1,0:T(1,128)S(1)}, u32[]{:S(2)}, u32[]{:S(2)}) collective-permute-start(f32[1,1024]{1,0:T(1,128)S(1)} %get-tuple-element.55), channel_id=1, source_target_pairs={{0,15},{1,2},{2,1},{3,4},{4,3},{5,6},{6,5},{7,8},{8,7},{9,10},{10,... | collective-permute-start | bytes 12296 | tf_op jit(solution)/shard_map/ppermute | solution.py:443
  21.7 1.7 %shard_map.116 = (f32[16,1024]{1,0:T(8,128)S(1)}, f32[16,1024]{1,0:T(8,128)S(1)}, f32[16,1024]{1,0:T(8,128)S(1)}, f32[16,1024]{1,0:T(8,128)S(1)}, f32[1,1024]{1,0:T(1,128)S(1)}) custom-call(f32[16,1024]{1,0:T(8,128)S(1)} %get-tuple-element.56.residual_ref, f32[16,1024]{1,0:T(8,128)S(1)} %get-tuple-element.57.direction_ref, ...), custom_call_target="tpu_custom_call" | custom-call | flops 4194304 | bytes 8388608 | tf_op jit(solution)/shard_map/pallas_call | solution.py:502
  23.4 0.0 collective-permute-done.4.inner_ref
  23.4 2.1 %collective-permute-done.5.outer_ref = f32[1,1024]{1,0:T(1,128)S(1)} collective-permute-done((f32[1,1024]{1,0:T(1,128)S(1)}, f32[1,1024]{1,0:T(1,128)S(1)}, u32[]{:S(2)}, u32[]{:S(2)}) %collective-permute-start.5) | collective-permute-done | bytes 4128 | tf_op jit(solution)/shard_map/ppermute | solution.py:443
  25.5 0.4 shard_map.117
  25.8 0.1 collective-permute-start.8
  25.9 0.1 collective-permute-start.7
  26.0 1.8 %collective-permute-start.6 = (f32[8,1024]{1,0:T(8,128)S(1)}, f32[8,1024]{1,0:T(8,128)S(1)}, u32[]{:S(2)}, u32[]{:S(2)}) collective-permute-start(f32[8,1024]{1,0:T(8,128)S(1)} %get-tuple-element.67.refs_0_), channel_id=1, source_target_pairs={{0,1},{1,0},{2,3},{3,2},{4,5},{5,4},{6,7},{7,6},{8,9},{9,8},{10,11... | collective-permute-start | bytes 98312 | tf_op jit(solution)/shard_map/ppermute | solution.py:456
  27.8 1.5 %collective-permute-done.8.refs_3_ = f32[8,1024]{1,0:T(8,128)S(1)} collective-permute-done((f32[8,1024]{1,0:T(8,128)S(1)}, f32[8,1024]{1,0:T(8,128)S(1)}, u32[]{:S(2)}, u32[]{:S(2)}) %collective-permute-start.8) | collective-permute-done | bytes 32800 | tf_op jit(solution)/shard_map/ppermute | solution.py:456
  29.3 0.7 %collective-permute-done.7.refs_2_ = f32[8,1024]{1,0:T(8,128)S(1)} collective-permute-done((f32[8,1024]{1,0:T(8,128)S(1)}, f32[8,1024]{1,0:T(8,128)S(1)}, u32[]{:S(2)}, u32[]{:S(2)}) %collective-permute-start.7) | collective-permute-done | bytes 32800 | tf_op jit(solution)/shard_map/ppermute | solution.py:456
  30.0 0.0 collective-permute-done.6.refs_1_
  30.0 2.4 %collective-permute-start.11 = (f32[8,1024]{1,0:T(8,128)S(1)}, f32[8,1024]{1,0:T(8,128)S(1)}, u32[]{:S(2)}, u32[]{:S(2)}) collective-permute-start(f32[8,1024]{1,0:T(8,128)S(1)} %get-tuple-element.68.refs_0_), channel_id=1, source_target_pairs={{0,12},{1,13},{2,14},{3,15},{4,8},{5,9},{6,10},{7,11},{8,4},{9,5},... | collective-permute-start | bytes 98312 | tf_op jit(solution)/shard_map/ppermute | solution.py:456
  32.5 0.0 collective-permute-start.10
  32.5 2.0 %collective-permute-start.9 = (f32[8,1024]{1,0:T(8,128)S(1)}, f32[8,1024]{1,0:T(8,128)S(1)}, u32[]{:S(2)}, u32[]{:S(2)}) collective-permute-start(f32[8,1024]{1,0:T(8,128)S(1)} %get-tuple-element.68.refs_0_), channel_id=1, source_target_pairs={{0,4},{1,5},{2,6},{3,7},{4,0},{5,1},{6,2},{7,3},{8,12},{9,13},{10,... | collective-permute-start | bytes 98312 | tf_op jit(solution)/shard_map/ppermute | solution.py:456
  34.5 1.3 %collective-permute-done.11.refs_3_ = f32[8,1024]{1,0:T(8,128)S(1)} collective-permute-done((f32[8,1024]{1,0:T(8,128)S(1)}, f32[8,1024]{1,0:T(8,128)S(1)}, u32[]{:S(2)}, u32[]{:S(2)}) %collective-permute-start.11) | collective-permute-done | bytes 32800 | tf_op jit(solution)/shard_map/ppermute | solution.py:456
  35.8 1.5 %collective-permute-done.10.refs_2_ = f32[8,1024]{1,0:T(8,128)S(1)} collective-permute-done((f32[8,1024]{1,0:T(8,128)S(1)}, f32[8,1024]{1,0:T(8,128)S(1)}, u32[]{:S(2)}, u32[]{:S(2)}) %collective-permute-start.10) | collective-permute-done | bytes 32800 | tf_op jit(solution)/shard_map/ppermute | solution.py:456
  37.3 0.0 collective-permute-done.9.refs_1_
  37.3 0.7 %shard_map.119 = (f32[16,1024]{1,0:T(8,128)}, f32[16,1024]{1,0:T(8,128)}, f32[4]{0:T(128)}) custom-call(f32[8,1024]{1,0:T(8,128)S(1)} %get-tuple-element.68.refs_0_, f32[8,1024]{1,0:T(8,128)S(1)} %collective-permute-done.9.refs_1_, f32[8,1024]{1,0:T(8,128)S(1)} %collective-permute-done.10.refs_2_, f32[8,1024]{1,0:T(8,128)S(1)} %collective-permute-done.11.refs_3_, ...), custom_call_target="tpu_custom_call" | custom-call | tf_op jit(solution)/shard_map/pallas_call | solution.py:530
  (12 shorter events, 0.1 us)
Async XLA Ops:
  0.6 4.1 %copy-start.5 = (s32[1536]{0:T(1024)S(1)}, s32[1536]{0:T(1024)}, u32[]{:S(2)}) copy-start(s32[1536]{0:T(1024)} %param.15) | copy-start | bytes 18436
  0.6 4.1 %copy-start.4 = (s32[16,1024]{1,0:T(8,128)S(1)}, s32[16,1024]{1,0:T(8,128)}, u32[]{:S(2)}) copy-start(s32[16,1024]{1,0:T(8,128)} %mask_ref.1) | copy-start | bytes 196612
  0.7 4.1 %copy-start.3 = (f32[16,1024]{1,0:T(8,128)S(1)}, f32[16,1024]{1,0:T(8,128)}, u32[]{:S(2)}) copy-start(f32[16,1024]{1,0:T(8,128)} %surface_ref.1) | copy-start | bytes 196612
  0.7 4.1 %copy-start.2 = (f32[16,1024]{1,0:T(8,128)S(1)}, f32[16,1024]{1,0:T(8,128)}, u32[]{:S(2)}) copy-start(f32[16,1024]{1,0:T(8,128)} %north_ref.1) | copy-start | bytes 196612
  0.7 4.1 %copy-start.1 = (f32[16,1024]{1,0:T(8,128)S(1)}, f32[16,1024]{1,0:T(8,128)}, u32[]{:S(2)}) copy-start(f32[16,1024]{1,0:T(8,128)} %east_ref.1) | copy-start | bytes 196612
  0.7 4.1 %copy-start = (f32[16,1024]{1,0:T(8,128)S(1)}, f32[16,1024]{1,0:T(8,128)}, u32[]{:S(2)}) copy-start(f32[16,1024]{1,0:T(8,128)} %right_ref.1) | copy-start | bytes 196612
  6.4 12.5 %collective-permute-start = (f32[24,1024]{1,0:T(8,128)S(1)}, f32[24,1024]{1,0:T(8,128)S(1)}, u32[]{:S(2)}, u32[]{:S(2)}) collective-permute-start(f32[24,1024]{1,0:T(8,128)S(1)} %get-tuple-element.42), channel_id=1, source_target_pairs={{0,1},{1,0},{2,3},{3,2},{4,5},{5,4},{6,7},{7,6},{8,9},{9,8},{10,11... | collective-permute-start | bytes 294920 | tf_op jit(solution)/shard_map/ppermute | solution.py:443
  6.9 12.0 %collective-permute-start.1 = (f32[24,1024]{1,0:T(8,128)S(1)}, f32[24,1024]{1,0:T(8,128)S(1)}, u32[]{:S(2)}, u32[]{:S(2)}) collective-permute-start(f32[24,1024]{1,0:T(8,128)S(1)} %get-tuple-element.43), channel_id=1, source_target_pairs={{0,15},{1,2},{2,1},{3,4},{4,3},{5,6},{6,5},{7,8},{8,7},{9,10},{10,... | collective-permute-start | bytes 294920 | tf_op jit(solution)/shard_map/ppermute | solution.py:443
  12.6 4.0 %collective-permute-start.2 = (f32[2,1024]{1,0:T(2,128)S(1)}, f32[2,1024]{1,0:T(2,128)S(1)}, u32[]{:S(2)}, u32[]{:S(2)}) collective-permute-start(f32[2,1024]{1,0:T(2,128)S(1)} %get-tuple-element.44), channel_id=1, source_target_pairs={{0,2},{1,3},{2,0},{3,1},{4,6},{5,7},{6,4},{7,5},{8,10},{9,11},{10,... | collective-permute-start | bytes 24584 | tf_op jit(solution)/shard_map/ppermute | solution.py:450
  12.6 6.3 %collective-permute-start.3 = (f32[2,1024]{1,0:T(2,128)S(1)}, f32[2,1024]{1,0:T(2,128)S(1)}, u32[]{:S(2)}, u32[]{:S(2)}) collective-permute-start(f32[2,1024]{1,0:T(2,128)S(1)} %get-tuple-element.45), channel_id=1, source_target_pairs={{0,14},{1,15},{2,4},{3,5},{4,2},{5,3},{6,8},{7,9},{8,6},{9,7},{10,... | collective-permute-start | bytes 24584 | tf_op jit(solution)/shard_map/ppermute | solution.py:450
  19.6 3.8 %collective-permute-start.4 = (f32[1,1024]{1,0:T(1,128)S(1)}, f32[1,1024]{1,0:T(1,128)S(1)}, u32[]{:S(2)}, u32[]{:S(2)}) collective-permute-start(f32[1,1024]{1,0:T(1,128)S(1)} %get-tuple-element.54), channel_id=1, source_target_pairs={{0,1},{1,0},{2,3},{3,2},{4,5},{5,4},{6,7},{7,6},{8,9},{9,8},{10,11... | collective-permute-start | bytes 12296 | tf_op jit(solution)/shard_map/ppermute | solution.py:443
  19.7 5.8 %collective-permute-start.5 = (f32[1,1024]{1,0:T(1,128)S(1)}, f32[1,1024]{1,0:T(1,128)S(1)}, u32[]{:S(2)}, u32[]{:S(2)}) collective-permute-start(f32[1,1024]{1,0:T(1,128)S(1)} %get-tuple-element.55), channel_id=1, source_target_pairs={{0,15},{1,2},{2,1},{3,4},{4,3},{5,6},{6,5},{7,8},{8,7},{9,10},{10,... | collective-permute-start | bytes 12296 | tf_op jit(solution)/shard_map/ppermute | solution.py:443
  25.8 3.4 %collective-permute-start.8 = (f32[8,1024]{1,0:T(8,128)S(1)}, f32[8,1024]{1,0:T(8,128)S(1)}, u32[]{:S(2)}, u32[]{:S(2)}) collective-permute-start(f32[8,1024]{1,0:T(8,128)S(1)} %get-tuple-element.67.refs_0_), channel_id=1, source_target_pairs={{0,3},{1,2},{2,1},{3,0},{4,7},{5,6},{6,5},{7,4},{8,11},{9,10},{10,... | collective-permute-start | bytes 98312 | tf_op jit(solution)/shard_map/ppermute | solution.py:456
  25.9 4.0 %collective-permute-start.7 = (f32[8,1024]{1,0:T(8,128)S(1)}, f32[8,1024]{1,0:T(8,128)S(1)}, u32[]{:S(2)}, u32[]{:S(2)}) collective-permute-start(f32[8,1024]{1,0:T(8,128)S(1)} %get-tuple-element.67.refs_0_), channel_id=1, source_target_pairs={{0,2},{1,3},{2,0},{3,1},{4,6},{5,7},{6,4},{7,5},{8,10},{9,11},{10,... | collective-permute-start | bytes 98312 | tf_op jit(solution)/shard_map/ppermute | solution.py:456
  26.0 4.0 %collective-permute-start.6 = (f32[8,1024]{1,0:T(8,128)S(1)}, f32[8,1024]{1,0:T(8,128)S(1)}, u32[]{:S(2)}, u32[]{:S(2)}) collective-permute-start(f32[8,1024]{1,0:T(8,128)S(1)} %get-tuple-element.67.refs_0_), channel_id=1, source_target_pairs={{0,1},{1,0},{2,3},{3,2},{4,5},{5,4},{6,7},{7,6},{8,9},{9,8},{10,11... | collective-permute-start | bytes 98312 | tf_op jit(solution)/shard_map/ppermute | solution.py:456
  30.0 5.8 %collective-permute-start.11 = (f32[8,1024]{1,0:T(8,128)S(1)}, f32[8,1024]{1,0:T(8,128)S(1)}, u32[]{:S(2)}, u32[]{:S(2)}) collective-permute-start(f32[8,1024]{1,0:T(8,128)S(1)} %get-tuple-element.68.refs_0_), channel_id=1, source_target_pairs={{0,12},{1,13},{2,14},{3,15},{4,8},{5,9},{6,10},{7,11},{8,4},{9,5},... | collective-permute-start | bytes 98312 | tf_op jit(solution)/shard_map/ppermute | solution.py:456
  32.5 4.8 %collective-permute-start.10 = (f32[8,1024]{1,0:T(8,128)S(1)}, f32[8,1024]{1,0:T(8,128)S(1)}, u32[]{:S(2)}, u32[]{:S(2)}) collective-permute-start(f32[8,1024]{1,0:T(8,128)S(1)} %get-tuple-element.68.refs_0_), channel_id=1, source_target_pairs={{0,8},{1,9},{2,10},{3,11},{4,12},{5,13},{6,14},{7,15},{8,0},{9,1},... | collective-permute-start | bytes 98312 | tf_op jit(solution)/shard_map/ppermute | solution.py:456
  32.5 4.8 %collective-permute-start.9 = (f32[8,1024]{1,0:T(8,128)S(1)}, f32[8,1024]{1,0:T(8,128)S(1)}, u32[]{:S(2)}, u32[]{:S(2)}) collective-permute-start(f32[8,1024]{1,0:T(8,128)S(1)} %get-tuple-element.68.refs_0_), channel_id=1, source_target_pairs={{0,4},{1,5},{2,6},{3,7},{4,0},{5,1},{6,2},{7,3},{8,12},{9,13},{10,... | collective-permute-start | bytes 98312 | tf_op jit(solution)/shard_map/ppermute | solution.py:456

commit v6 on v5

--- a/solution.py
+++ b/solution.py
@@ -248,7 +248,7 @@
 
 
 def second_kernel(
-    low_ref, high_ref, inner_ref, outer_ref, near_ref, far_ref, residual_ref, search_ref, flow_ref, product_ref, diag_ref, east_face_ref, north_face_ref, ocean_ref, east_end_ref, bt_ref,
+    low_ref, high_ref, far_ref, outer_ref, near_ref, inner_ref, residual_ref, search_ref, flow_ref, product_ref, diag_ref, east_face_ref, north_face_ref, ocean_ref, east_end_ref, bt_ref,
     residual_out, direction_out, diag_out, faces_out, norms_out, coef_out, inner_out, outer_out,
 ):
     store_coefficients(low_ref, high_ref, coef_out)
@@ -324,7 +324,7 @@
 
 
 def closing_kernel(
-    inner_ref, outer_ref, residual_ref, direction_ref, solution_ref, product_ref, diag_ref, east_face_ref, north_face_ref, ocean_ref, faces_ref, coef_ref, norms_ref, bt_ref,
+    outer_ref, inner_ref, residual_ref, direction_ref, solution_ref, product_ref, diag_ref, east_face_ref, north_face_ref, ocean_ref, faces_ref, coef_ref, norms_ref, bt_ref,
     residual_out, solution_out, pack_out,
 ):
     west, east = halo_rows(inner_ref, outer_ref, 0, even_device())
@@ -351,11 +351,15 @@
     pack_out[SUMS + 1 :] = jnp.zeros_like(pack_out[SUMS + 1 :])
 
 
+def swap_order(size, radix):
+    return (1,) if radix == 2 else (1, 2, 3) if size == 1 else (1, 3, 2)
+
+
 def join_packs(size, radix, is_last, pack_ref, others, halo, packs):
     me = lax.axis_index("lon")
     mine = lax.rem(me // size, radix)
     packs[mine] = pack_ref[...]
-    for s, other in enumerate(others, start=1):
+    for s, other in zip(swap_order(size, radix), others):
         packs[mine ^ s] = other[...]
 
     def row(run, name):
@@ -453,8 +457,8 @@
 def swap_runs(pack, size, radix):
     devices = lax.axis_size("lon")
     return [
-        lax.ppermute(pack, "lon", [(i, i ^ (s * size)) for i in range(devices)]) for s in range(radix - 1, 0, -1)
-    ][::-1]
+        lax.ppermute(pack, "lon", [(i, i ^ (s * size)) for i in range(devices)]) for s in swap_order(size, radix)
+    ]
 
 
 def on_device(
@@ -483,7 +487,7 @@
         [],
         24 * MIB,
     )(active_tiles.reshape(-1, LANES), right_side, east_coef, north_coef, surface_term, cell_mask, bt)
-    low_bound, high_bound, inner = lax.optimization_barrier((low_bound, high_bound, inner))
+    low_bound, high_bound, outer = lax.optimization_barrier((low_bound, high_bound, outer))
     inner, outer = exchange(inner, outer)
     near, far = exchange_beyond(near, far)
     work = pl.CostEstimate(flops=2 * bt.size, bytes_accessed=4 * bt.size, transcendentals=0)
@@ -495,7 +499,7 @@
         [],
         24 * MIB,
     )(
-        low_bound, high_bound, inner, outer, near, far, residual, search, flow, product, diag, east_face, north_face,
+        low_bound, high_bound, far, outer, near, inner, residual, search, flow, product, diag, east_face, north_face,
         ocean, east_end, bt,
     )
     inner, outer = exchange(inner, outer)
@@ -509,7 +513,7 @@
     )(residual, direction, search, diag, east_face, north_face, ocean, coef, norms, bt)
     pack_shape = shape(PACK_ROWS, rows)
     residual, answer, pack = call(closing_kernel, [vmem()] * 14, [field, field, pack_shape], [], 24 * MIB)(
-        inner, outer, residual, direction, answer, product, diag, east_face, north_face, ocean, faces, coef, norms, bt
+        outer, inner, residual, direction, answer, product, diag, east_face, north_face, ocean, faces, coef, norms, bt
     )
     devices = lax.axis_size("lon")
     size, halo = 1, []

time: 38.2 us -> 36 us (0.942)
  starting transfers between devices: 16.5 us -> 12.6 us
  waiting for transfers between devices: 9.47 us -> 11.3 us
    ppermute x2, starting transfers between devices: 7.68 us -> 6.42 us  [exchange(): lax.ppermute(outer, 'lon', across)]
    ppermute x2, waiting for transfers between devices: 2.36 us -> 3.56 us  [exchange_beyond(): return (lax.ppermute(near, 'lon', within), lax.ppermute(far, 'lon', across))]
    ppermute x2, starting transfers between devices: 1.91 us -> 0.72 us  [exchange_beyond(): return (lax.ppermute(near, 'lon', within), lax.ppermute(far, 'lon', across))]
    ppermute x2, waiting for transfers between devices: 2.11 us -> 3.22 us  [exchange(): lax.ppermute(outer, 'lon', across)]
    ppermute x6, starting transfers between devices: 6.36 us -> 5.46 us  [swap_runs(): lax.ppermute(pack, 'lon', [(i, i ^ s * size) for i in range(devices)])]
    ppermute x2, starting transfers between devices: 0.59 us -> 0.01 us  [exchange(): lax.ppermute(inner, 'lon', pairs)]
    ppermute x6, waiting for transfers between devices: 4.99 us -> 4.49 us  [swap_runs(): lax.ppermute(pack, 'lon', [(i, i ^ s * size) for i in range(devices)])]
  transfers between devices with their start and end apart: 12 -> 12, of which waited for: 6 -> 6; matrix products, arithmetic and copies ran while one was open for 0% -> 0% of each run, Pallas kernels for 6% -> 7%
where the time goes in v6:
time: 36 us; the launch traced here: 35.9 us
  starting transfers between devices  12.6 us (35%)
  waiting for transfers between devices  11.3 us (31%)
  Pallas kernels  9.85 us (27%)
  between operations  2.11 us (6%)
    ppermute x2, starting transfers between devices, exchange(): lax.ppermute(outer, 'lon', across)  6.42 us
    ppermute x6, starting transfers between devices, swap_runs(): lax.ppermute(pack, 'lon', [(i, i ^ s * size) for i in range(devices)])  5.46 us
    ppermute x6, waiting for transfers between devices, swap_runs(): lax.ppermute(pack, 'lon', [(i, i ^ s * size) for i in range(devices)])  4.49 us
    pallas_call x1, Pallas kernels, on_device(): call(transpose_kernel, [pl.BlockSpec(memory_space=pl.ANY)], [bt_shape], [...  4.07 us
    ppermute x2, waiting for transfers between devices, exchange_beyond(): return (lax.ppermute(near, 'lon', within), lax.ppermute(far, 'lon', across))  3.56 us
    ppermute x2, waiting for transfers between devices, exchange(): lax.ppermute(outer, 'lon', across)  3.22 us
    pallas_call x1, Pallas kernels, on_device(): call(ahead_kernel, [vmem()] * 10, [field, field, field, field, row], [],...  1.66 us
    pallas_call x1, Pallas kernels, on_device(): call(first_kernel, [vmem()] * 7, [field, field, field, field, field, fiel...  1.55 us
  transfers between devices with their start and end apart: 12, of which 6 were waited for; matrix products, arithmetic and copies ran while one was open for 0% of the time, Pallas kernels for 7%

profile of v6, /device:TPU:0, one launch (start us, length us, event | category | flops | bytes accessed | tf_op | source)
XLA Modules:
  0.0 35.9 jit_solution(11891565858996286485)
XLA Ops:
  0.6 0.0 copy-start.5
  0.7 4.1 %shard_map.112.bt_ref = f32[8,16,128,128]{3,2,1,0:T(8,128)S(1)} custom-call(f32[128,128,128]{2,1,0:T(8,128)} %blocks_hbm.1), custom_call_target="tpu_custom_call" | custom-call | flops 1000000000 | bytes 16777216 | tf_op jit(solution)/shard_map/pallas_call | solution.py:474
  4.8 1.5 %shard_map.113 = (f32[16,1024]{1,0:T(8,128)S(1)}, f32[16,1024]{1,0:T(8,128)S(1)}, f32[16,1024]{1,0:T(8,128)S(1)}, f32[16,1024]{1,0:T(8,128)S(1)}, f32[16,1024]{1...) custom-call(s32[12,128]{1,0:T(8,128)S(1)} %bitcast.1, ...), custom_call_target="tpu_custom_call" | custom-call | tf_op jit(solution)/shard_map/pallas_call | solution.py:483
  6.4 5.5 %collective-permute-start.1 = (f32[24,1024]{1,0:T(8,128)S(1)}, f32[24,1024]{1,0:T(8,128)S(1)}, u32[]{:S(2)}, u32[]{:S(2)}) collective-permute-start(f32[24,1024]{1,0:T(8,128)S(1)} %get-tuple-element.43), channel_id=1, source_target_pairs={{0,15},{1,2},{2,1},{3,4},{4,3},{5,6},{6,5},{7,8},{8,7},{9,10},{10,... | collective-permute-start | bytes 294920 | tf_op jit(solution)/shard_map/ppermute | solution.py:447
  11.9 0.0 collective-permute-start.3
  11.9 0.7 %collective-permute-start = (f32[2,1024]{1,0:T(2,128)S(1)}, f32[2,1024]{1,0:T(2,128)S(1)}, u32[]{:S(2)}, u32[]{:S(2)}) collective-permute-start(f32[2,1024]{1,0:T(2,128)S(1)} %get-tuple-element.42), channel_id=1, source_target_pairs={{0,14},{1,15},{2,4},{3,5},{4,2},{5,3},{6,8},{7,9},{8,6},{9,7},{10,... | collective-permute-start | bytes 24584 | tf_op jit(solution)/shard_map/ppermute | solution.py:454
  12.6 0.0 collective-permute-start.2
  13.9 0.8 %shard_map.114.product_ref = f32[16,1024]{1,0:T(8,128)S(1)} custom-call(f32[8,16,128,128]{3,2,1,0:T(8,128)S(1)} %shard_map.112.bt_ref, f32[16,1024]{1,0:T(8,128)S(1)} %get-tuple-element.48.field_ref.flow_ref), custom_call_target="tpu_custom_call" | custom-call | flops 4194304 | bytes 8388608 | tf_op jit(solution)/shard_map/pallas_call | solution.py:494
  14.7 3.6 %collective-permute-done.far_ref = f32[2,1024]{1,0:T(2,128)S(1)} collective-permute-done((f32[2,1024]{1,0:T(2,128)S(1)}, f32[2,1024]{1,0:T(2,128)S(1)}, u32[]{:S(2)}, u32[]{:S(2)}) %collective-permute-start) | collective-permute-done | bytes 8224 | tf_op jit(solution)/shard_map/ppermute | solution.py:454
  18.2 0.0 collective-permute-done.2.near_ref
  18.2 0.0 collective-permute-done.1.outer_ref
  18.2 0.0 collective-permute-done.3.inner_ref
  18.3 0.7 %shard_map.115 = (f32[16,1024]{1,0:T(8,128)S(1)}, f32[16,1024]{1,0:T(8,128)S(1)}, f32[16,1024]{1,0:T(8,128)S(1)}, f32[2,1024]{1,0:T(2,128)S(1)}, f32[1,1024]{1,0...) custom-call(f32[1]{0:T(128)S(6)} %copy.12.low_ref, f32[1]{0:T(128)S(6)} %copy.13.high_ref, ...), custom_call_target="tpu_custom_call" | custom-call | tf_op jit(solution)/shard_map/pallas_call | solution.py:495
  18.9 0.9 %collective-permute-start.4 = (f32[1,1024]{1,0:T(1,128)S(1)}, f32[1,1024]{1,0:T(1,128)S(1)}, u32[]{:S(2)}, u32[]{:S(2)}) collective-permute-start(f32[1,1024]{1,0:T(1,128)S(1)} %get-tuple-element.54), channel_id=1, source_target_pairs={{0,15},{1,2},{2,1},{3,4},{4,3},{5,6},{6,5},{7,8},{8,7},{9,10},{10,... | collective-permute-start | bytes 12296 | tf_op jit(solution)/shard_map/ppermute | solution.py:447
  19.8 0.0 collective-permute-start.5
  19.8 1.7 %shard_map.116 = (f32[16,1024]{1,0:T(8,128)S(1)}, f32[16,1024]{1,0:T(8,128)S(1)}, f32[16,1024]{1,0:T(8,128)S(1)}, f32[16,1024]{1,0:T(8,128)S(1)}, f32[1,1024]{1,0:T(1,128)S(1)}) custom-call(f32[16,1024]{1,0:T(8,128)S(1)} %get-tuple-element.56.residual_ref, f32[16,1024]{1,0:T(8,128)S(1)} %get-tuple-element.57.direction_ref, ...), custom_call_target="tpu_custom_call" | custom-call | flops 4194304 | bytes 8388608 | tf_op jit(solution)/shard_map/pallas_call | solution.py:506
  21.5 3.2 %collective-permute-done.4.outer_ref = f32[1,1024]{1,0:T(1,128)S(1)} collective-permute-done((f32[1,1024]{1,0:T(1,128)S(1)}, f32[1,1024]{1,0:T(1,128)S(1)}, u32[]{:S(2)}, u32[]{:S(2)}) %collective-permute-start.4) | collective-permute-done | bytes 4128 | tf_op jit(solution)/shard_map/ppermute | solution.py:447
  24.7 0.0 collective-permute-done.5.inner_ref
  24.7 0.4 %shard_map.117 = (f32[16,1024]{1,0:T(8,128)S(1)}, f32[16,1024]{1,0:T(8,128)S(1)}, f32[8,1024]{1,0:T(8,128)S(1)}) custom-call(f32[1,1024]{1,0:T(1,128)S(1)} %collective-permute-done.4.outer_ref, f32[1,1024]{1,0:T(1,128)S(1)} %collective-permute-done.5.inner_ref, f32[16,1024]{1,0:T(8,128)S(1)} %get-tuple-element.61.residual_ref, ...), custom_call_target="tpu_custom_call" | custom-call | tf_op jit(solution)/shard_map/pallas_call | solution.py:515
  25.1 0.1 collective-permute-start.8
  25.2 0.1 collective-permute-start.7
  25.3 1.8 %collective-permute-start.6 = (f32[8,1024]{1,0:T(8,128)S(1)}, f32[8,1024]{1,0:T(8,128)S(1)}, u32[]{:S(2)}, u32[]{:S(2)}) collective-permute-start(f32[8,1024]{1,0:T(8,128)S(1)} %get-tuple-element.67.refs_0_), channel_id=1, source_target_pairs={{0,1},{1,0},{2,3},{3,2},{4,5},{5,4},{6,7},{7,6},{8,9},{9,8},{10,11... | collective-permute-start | bytes 98312 | tf_op jit(solution)/shard_map/ppermute | solution.py:460
  27.0 1.5 %collective-permute-done.8.refs_3_ = f32[8,1024]{1,0:T(8,128)S(1)} collective-permute-done((f32[8,1024]{1,0:T(8,128)S(1)}, f32[8,1024]{1,0:T(8,128)S(1)}, u32[]{:S(2)}, u32[]{:S(2)}) %collective-permute-start.8) | collective-permute-done | bytes 32800 | tf_op jit(solution)/shard_map/ppermute | solution.py:460
  28.5 0.7 %collective-permute-done.7.refs_2_ = f32[8,1024]{1,0:T(8,128)S(1)} collective-permute-done((f32[8,1024]{1,0:T(8,128)S(1)}, f32[8,1024]{1,0:T(8,128)S(1)}, u32[]{:S(2)}, u32[]{:S(2)}) %collective-permute-start.7) | collective-permute-done | bytes 32800 | tf_op jit(solution)/shard_map/ppermute | solution.py:460
  29.2 0.0 collective-permute-done.6.refs_1_
  29.3 0.1 collective-permute-start.11
  29.3 1.3 %collective-permute-start.10 = (f32[8,1024]{1,0:T(8,128)S(1)}, f32[8,1024]{1,0:T(8,128)S(1)}, u32[]{:S(2)}, u32[]{:S(2)}) collective-permute-start(f32[8,1024]{1,0:T(8,128)S(1)} %get-tuple-element.68.refs_0_), channel_id=1, source_target_pairs={{0,12},{1,13},{2,14},{3,15},{4,8},{5,9},{6,10},{7,11},{8,4},{9,5},... | collective-permute-start | bytes 98312 | tf_op jit(solution)/shard_map/ppermute | solution.py:460
  30.7 2.1 %collective-permute-start.9 = (f32[8,1024]{1,0:T(8,128)S(1)}, f32[8,1024]{1,0:T(8,128)S(1)}, u32[]{:S(2)}, u32[]{:S(2)}) collective-permute-start(f32[8,1024]{1,0:T(8,128)S(1)} %get-tuple-element.68.refs_0_), channel_id=1, source_target_pairs={{0,4},{1,5},{2,6},{3,7},{4,0},{5,1},{6,2},{7,3},{8,12},{9,13},{10,... | collective-permute-start | bytes 98312 | tf_op jit(solution)/shard_map/ppermute | solution.py:460
  32.8 1.5 %collective-permute-done.11.refs_3_ = f32[8,1024]{1,0:T(8,128)S(1)} collective-permute-done((f32[8,1024]{1,0:T(8,128)S(1)}, f32[8,1024]{1,0:T(8,128)S(1)}, u32[]{:S(2)}, u32[]{:S(2)}) %collective-permute-start.11) | collective-permute-done | bytes 32800 | tf_op jit(solution)/shard_map/ppermute | solution.py:460
  34.4 0.8 %collective-permute-done.10.refs_2_ = f32[8,1024]{1,0:T(8,128)S(1)} collective-permute-done((f32[8,1024]{1,0:T(8,128)S(1)}, f32[8,1024]{1,0:T(8,128)S(1)}, u32[]{:S(2)}, u32[]{:S(2)}) %collective-permute-start.10) | collective-permute-done | bytes 32800 | tf_op jit(solution)/shard_map/ppermute | solution.py:460
  35.1 0.0 collective-permute-done.9.refs_1_
  35.1 0.7 %shard_map.119 = (f32[16,1024]{1,0:T(8,128)}, f32[16,1024]{1,0:T(8,128)}, f32[4]{0:T(128)}) custom-call(f32[8,1024]{1,0:T(8,128)S(1)} %get-tuple-element.68.refs_0_, f32[8,1024]{1,0:T(8,128)S(1)} %collective-permute-done.9.refs_1_, f32[8,1024]{1,0:T(8,128)S(1)} %collective-permute-done.10.refs_2_, f32[8,1024]{1,0:T(8,128)S(1)} %collective-permute-done.11.refs_3_, ...), custom_call_target="tpu_custom_call" | custom-call | tf_op jit(solution)/shard_map/pallas_call | solution.py:534
  (12 shorter events, 0.1 us)
Async XLA Ops:
  0.6 4.1 %copy-start.5 = (s32[1536]{0:T(1024)S(1)}, s32[1536]{0:T(1024)}, u32[]{:S(2)}) copy-start(s32[1536]{0:T(1024)} %param.15) | copy-start | bytes 18436
  0.6 4.1 %copy-start.4 = (s32[16,1024]{1,0:T(8,128)S(1)}, s32[16,1024]{1,0:T(8,128)}, u32[]{:S(2)}) copy-start(s32[16,1024]{1,0:T(8,128)} %mask_ref.1) | copy-start | bytes 196612
  0.7 4.1 %copy-start.3 = (f32[16,1024]{1,0:T(8,128)S(1)}, f32[16,1024]{1,0:T(8,128)}, u32[]{:S(2)}) copy-start(f32[16,1024]{1,0:T(8,128)} %surface_ref.1) | copy-start | bytes 196612
  0.7 4.1 %copy-start.2 = (f32[16,1024]{1,0:T(8,128)S(1)}, f32[16,1024]{1,0:T(8,128)}, u32[]{:S(2)}) copy-start(f32[16,1024]{1,0:T(8,128)} %north_ref.1) | copy-start | bytes 196612
  0.7 4.1 %copy-start.1 = (f32[16,1024]{1,0:T(8,128)S(1)}, f32[16,1024]{1,0:T(8,128)}, u32[]{:S(2)}) copy-start(f32[16,1024]{1,0:T(8,128)} %east_ref.1) | copy-start | bytes 196612
  0.7 4.1 %copy-start = (f32[16,1024]{1,0:T(8,128)S(1)}, f32[16,1024]{1,0:T(8,128)}, u32[]{:S(2)}) copy-start(f32[16,1024]{1,0:T(8,128)} %right_ref.1) | copy-start | bytes 196612
  6.4 11.9 %collective-permute-start.1 = (f32[24,1024]{1,0:T(8,128)S(1)}, f32[24,1024]{1,0:T(8,128)S(1)}, u32[]{:S(2)}, u32[]{:S(2)}) collective-permute-start(f32[24,1024]{1,0:T(8,128)S(1)} %get-tuple-element.43), channel_id=1, source_target_pairs={{0,15},{1,2},{2,1},{3,4},{4,3},{5,6},{6,5},{7,8},{8,7},{9,10},{10,... | collective-permute-start | bytes 294920 | tf_op jit(solution)/shard_map/ppermute | solution.py:447
  11.9 6.4 %collective-permute-start.3 = (f32[24,1024]{1,0:T(8,128)S(1)}, f32[24,1024]{1,0:T(8,128)S(1)}, u32[]{:S(2)}, u32[]{:S(2)}) collective-permute-start(f32[24,1024]{1,0:T(8,128)S(1)} %get-tuple-element.45), channel_id=1, source_target_pairs={{0,1},{1,0},{2,3},{3,2},{4,5},{5,4},{6,7},{7,6},{8,9},{9,8},{10,11... | collective-permute-start | bytes 294920 | tf_op jit(solution)/shard_map/ppermute | solution.py:447
  11.9 6.3 %collective-permute-start = (f32[2,1024]{1,0:T(2,128)S(1)}, f32[2,1024]{1,0:T(2,128)S(1)}, u32[]{:S(2)}, u32[]{:S(2)}) collective-permute-start(f32[2,1024]{1,0:T(2,128)S(1)} %get-tuple-element.42), channel_id=1, source_target_pairs={{0,14},{1,15},{2,4},{3,5},{4,2},{5,3},{6,8},{7,9},{8,6},{9,7},{10,... | collective-permute-start | bytes 24584 | tf_op jit(solution)/shard_map/ppermute | solution.py:454
  12.6 5.6 %collective-permute-start.2 = (f32[2,1024]{1,0:T(2,128)S(1)}, f32[2,1024]{1,0:T(2,128)S(1)}, u32[]{:S(2)}, u32[]{:S(2)}) collective-permute-start(f32[2,1024]{1,0:T(2,128)S(1)} %get-tuple-element.44), channel_id=1, source_target_pairs={{0,2},{1,3},{2,0},{3,1},{4,6},{5,7},{6,4},{7,5},{8,10},{9,11},{10,... | collective-permute-start | bytes 24584 | tf_op jit(solution)/shard_map/ppermute | solution.py:454
  18.9 5.8 %collective-permute-start.4 = (f32[1,1024]{1,0:T(1,128)S(1)}, f32[1,1024]{1,0:T(1,128)S(1)}, u32[]{:S(2)}, u32[]{:S(2)}) collective-permute-start(f32[1,1024]{1,0:T(1,128)S(1)} %get-tuple-element.54), channel_id=1, source_target_pairs={{0,15},{1,2},{2,1},{3,4},{4,3},{5,6},{6,5},{7,8},{8,7},{9,10},{10,... | collective-permute-start | bytes 12296 | tf_op jit(solution)/shard_map/ppermute | solution.py:447
  19.8 4.9 %collective-permute-start.5 = (f32[1,1024]{1,0:T(1,128)S(1)}, f32[1,1024]{1,0:T(1,128)S(1)}, u32[]{:S(2)}, u32[]{:S(2)}) collective-permute-start(f32[1,1024]{1,0:T(1,128)S(1)} %get-tuple-element.55), channel_id=1, source_target_pairs={{0,1},{1,0},{2,3},{3,2},{4,5},{5,4},{6,7},{7,6},{8,9},{9,8},{10,11... | collective-permute-start | bytes 12296 | tf_op jit(solution)/shard_map/ppermute | solution.py:447
  25.1 3.4 %collective-permute-start.8 = (f32[8,1024]{1,0:T(8,128)S(1)}, f32[8,1024]{1,0:T(8,128)S(1)}, u32[]{:S(2)}, u32[]{:S(2)}) collective-permute-start(f32[8,1024]{1,0:T(8,128)S(1)} %get-tuple-element.67.refs_0_), channel_id=1, source_target_pairs={{0,3},{1,2},{2,1},{3,0},{4,7},{5,6},{6,5},{7,4},{8,11},{9,10},{10,... | collective-permute-start | bytes 98312 | tf_op jit(solution)/shard_map/ppermute | solution.py:460
  25.2 4.0 %collective-permute-start.7 = (f32[8,1024]{1,0:T(8,128)S(1)}, f32[8,1024]{1,0:T(8,128)S(1)}, u32[]{:S(2)}, u32[]{:S(2)}) collective-permute-start(f32[8,1024]{1,0:T(8,128)S(1)} %get-tuple-element.67.refs_0_), channel_id=1, source_target_pairs={{0,2},{1,3},{2,0},{3,1},{4,6},{5,7},{6,4},{7,5},{8,10},{9,11},{10,... | collective-permute-start | bytes 98312 | tf_op jit(solution)/shard_map/ppermute | solution.py:460
  25.3 4.0 %collective-permute-start.6 = (f32[8,1024]{1,0:T(8,128)S(1)}, f32[8,1024]{1,0:T(8,128)S(1)}, u32[]{:S(2)}, u32[]{:S(2)}) collective-permute-start(f32[8,1024]{1,0:T(8,128)S(1)} %get-tuple-element.67.refs_0_), channel_id=1, source_target_pairs={{0,1},{1,0},{2,3},{3,2},{4,5},{5,4},{6,7},{7,6},{8,9},{9,8},{10,11... | collective-permute-start | bytes 98312 | tf_op jit(solution)/shard_map/ppermute | solution.py:460
  29.3 5.1 %collective-permute-start.11 = (f32[8,1024]{1,0:T(8,128)S(1)}, f32[8,1024]{1,0:T(8,128)S(1)}, u32[]{:S(2)}, u32[]{:S(2)}) collective-permute-start(f32[8,1024]{1,0:T(8,128)S(1)} %get-tuple-element.68.refs_0_), channel_id=1, source_target_pairs={{0,8},{1,9},{2,10},{3,11},{4,12},{5,13},{6,14},{7,15},{8,0},{9,1},... | collective-permute-start | bytes 98312 | tf_op jit(solution)/shard_map/ppermute | solution.py:460
  29.3 5.8 %collective-permute-start.10 = (f32[8,1024]{1,0:T(8,128)S(1)}, f32[8,1024]{1,0:T(8,128)S(1)}, u32[]{:S(2)}, u32[]{:S(2)}) collective-permute-start(f32[8,1024]{1,0:T(8,128)S(1)} %get-tuple-element.68.refs_0_), channel_id=1, source_target_pairs={{0,12},{1,13},{2,14},{3,15},{4,8},{5,9},{6,10},{7,11},{8,4},{9,5},... | collective-permute-start | bytes 98312 | tf_op jit(solution)/shard_map/ppermute | solution.py:460
  30.7 4.4 %collective-permute-start.9 = (f32[8,1024]{1,0:T(8,128)S(1)}, f32[8,1024]{1,0:T(8,128)S(1)}, u32[]{:S(2)}, u32[]{:S(2)}) collective-permute-start(f32[8,1024]{1,0:T(8,128)S(1)} %get-tuple-element.68.refs_0_), channel_id=1, source_target_pairs={{0,4},{1,5},{2,6},{3,7},{4,0},{5,1},{6,2},{7,3},{8,12},{9,13},{10,... | collective-permute-start | bytes 98312 | tf_op jit(solution)/shard_map/ppermute | solution.py:460

commit v7 on v6

--- a/solution.py
+++ b/solution.py
@@ -41,15 +41,31 @@
     return jnp.concatenate(rows, axis=0)
 
 
+def fold(parts):
+    sub = lax.broadcasted_iota(jnp.int32, (SUBS, LANES), 0)
+    half = SUBS // 2
+    while half:
+        upper = (sub & half) == 0
+        parts = [
+            jnp.where(upper, low, high) + jnp.where(upper, roll(low, -half, 0), roll(high, half, 0))
+            for low, high in zip(parts[:half], parts[half:])
+        ]
+        half //= 2
+    return parts[0]
+
+
+def row_sums(product):
+    return functools.reduce(jnp.add, [product[i : i + SUBS] for i in range(0, product.shape[0], SUBS)])
+
+
 def blocks_product(bt_ref, field, out_ref):
     index = gather_index()
     columns, rows = field.shape
     for block in range(lane_blocks(rows)):
         spread = expand(field, block, index)
-        for a in range(columns):
-            out_ref[a : a + 1, block * LANES : (block + 1) * LANES] = jnp.sum(
-                bt_ref[block, a] * spread, axis=0, keepdims=True
-            )
+        for first in range(0, columns, SUBS):
+            parts = [row_sums(bt_ref[block, a] * spread) for a in range(first, first + SUBS)]
+            out_ref[first : first + SUBS, block * LANES : (block + 1) * LANES] = fold(parts)
 
 
 def even_device():
@@ -127,6 +143,8 @@
     tiles = rows // SUBS
     even = even_device()
     flags = tile_flags(active_ref, lax.axis_index("lon") * tiles, tiles)
+    right = right_ref[...] * mask_ref[...].astype(F32)
+    blocks_product(bt_ref, right, search_ref)
     lane = lax.broadcasted_iota(jnp.int32, (SUBS, LANES), 1)
     spread = [
         jnp.take_along_axis(jnp.broadcast_to(flags, (SUBS, tiles)), i * (LANES // SUBS) + lane // SUBS, axis=1)
@@ -148,7 +166,6 @@
     residual_ref[...] = residual
     east_end = east_ocean[columns - 1 :]
     east_end_ref[...] = east_end
-    blocks_product(bt_ref, residual, search_ref)
     search = search_ref[...] * ocean
     search_ref[...] = search
     nothing = jnp.zeros_like(east_end)
@@ -229,10 +246,8 @@
     blocks = []
     for block in range(count):
         west, east = expand(first, block, index), expand(last, block, index)
-        rows = [
-            jnp.sum(bt_ref[block, a, :SUBS] * west + bt_ref[block, a, LANES - SUBS :] * east, axis=0, keepdims=True)
-            for a in range(columns)
-        ]
+        parts = [bt_ref[block, a, :SUBS] * west + bt_ref[block, a, LANES - SUBS :] * east for a in range(columns)]
+        rows = [fold(parts[a : a + SUBS]) for a in range(0, columns, SUBS)]
         blocks.append(jnp.concatenate(rows, axis=0))
     return jnp.concatenate(blocks, axis=1)
 

time: 36 us -> 35.5 us (0.986)
  Pallas kernels: 9.85 us -> 9.27 us
    pallas_call x1, Pallas kernels: 1.55 us -> 1.13 us  [on_device(): call(first_kernel, [vmem()] * 7, [field, field, field, field, field, fiel...]
where the time goes in v7:
time: 35.5 us; the launch traced here: 35.4 us
  starting transfers between devices  12.6 us (35%)
  waiting for transfers between devices  11.3 us (32%)
  Pallas kernels  9.27 us (26%)
  between operations  2.11 us (6%)
    ppermute x2, starting transfers between devices, exchange(): lax.ppermute(outer, 'lon', across)  6.42 us
    ppermute x6, starting transfers between devices, swap_runs(): lax.ppermute(pack, 'lon', [(i, i ^ s * size) for i in range(devices)])  5.46 us
    ppermute x6, waiting for transfers between devices, swap_runs(): lax.ppermute(pack, 'lon', [(i, i ^ s * size) for i in range(devices)])  4.49 us
    pallas_call x1, Pallas kernels, on_device(): call(transpose_kernel, [pl.BlockSpec(memory_space=pl.ANY)], [bt_shape], [...  4.07 us
    ppermute x2, waiting for transfers between devices, exchange_beyond(): return (lax.ppermute(near, 'lon', within), lax.ppermute(far, 'lon', across))  3.59 us
    ppermute x2, waiting for transfers between devices, exchange(): lax.ppermute(outer, 'lon', across)  3.27 us
    pallas_call x1, Pallas kernels, on_device(): call(ahead_kernel, [vmem()] * 10, [field, field, field, field, row], [],...  1.61 us
    pallas_call x1, Pallas kernels, on_device(): call(first_kernel, [vmem()] * 7, [field, field, field, field, field, fiel...  1.13 us
  transfers between devices with their start and end apart: 12, of which 6 were waited for; matrix products, arithmetic and copies ran while one was open for 0% of the time, Pallas kernels for 7%

profile of v7, /device:TPU:0, one launch (start us, length us, event | category | flops | bytes accessed | tf_op | source)
XLA Modules:
  0.0 35.4 jit_solution(1333689197074114761)
XLA Ops:
  0.6 0.0 copy-start.5
  0.7 4.1 %shard_map.112.bt_ref = f32[8,16,128,128]{3,2,1,0:T(8,128)S(1)} custom-call(f32[128,128,128]{2,1,0:T(8,128)} %blocks_hbm.1), custom_call_target="tpu_custom_call" | custom-call | flops 1000000000 | bytes 16777216 | tf_op jit(solution)/shard_map/pallas_call | solution.py:489
  4.8 1.1 %shard_map.113 = (f32[16,1024]{1,0:T(8,128)S(1)}, f32[16,1024]{1,0:T(8,128)S(1)}, f32[16,1024]{1,0:T(8,128)S(1)}, f32[16,1024]{1,0:T(8,128)S(1)}, f32[16,1024]{1...) custom-call(s32[12,128]{1,0:T(8,128)S(1)} %bitcast.1, ...), custom_call_target="tpu_custom_call" | custom-call | tf_op jit(solution)/shard_map/pallas_call | solution.py:498
  6.0 5.5 %collective-permute-start.1 = (f32[24,1024]{1,0:T(8,128)S(1)}, f32[24,1024]{1,0:T(8,128)S(1)}, u32[]{:S(2)}, u32[]{:S(2)}) collective-permute-start(f32[24,1024]{1,0:T(8,128)S(1)} %get-tuple-element.43), channel_id=1, source_target_pairs={{0,15},{1,2},{2,1},{3,4},{4,3},{5,6},{6,5},{7,8},{8,7},{9,10},{10,... | collective-permute-start | bytes 294920 | tf_op jit(solution)/shard_map/ppermute | solution.py:462
  11.5 0.0 collective-permute-start.3
  11.5 0.7 %collective-permute-start = (f32[2,1024]{1,0:T(2,128)S(1)}, f32[2,1024]{1,0:T(2,128)S(1)}, u32[]{:S(2)}, u32[]{:S(2)}) collective-permute-start(f32[2,1024]{1,0:T(2,128)S(1)} %get-tuple-element.42), channel_id=1, source_target_pairs={{0,14},{1,15},{2,4},{3,5},{4,2},{5,3},{6,8},{7,9},{8,6},{9,7},{10,... | collective-permute-start | bytes 24584 | tf_op jit(solution)/shard_map/ppermute | solution.py:469
  12.2 0.0 collective-permute-start.2
  13.5 0.7 %shard_map.114.product_ref = f32[16,1024]{1,0:T(8,128)S(1)} custom-call(f32[8,16,128,128]{3,2,1,0:T(8,128)S(1)} %shard_map.112.bt_ref, f32[16,1024]{1,0:T(8,128)S(1)} %get-tuple-element.48.field_ref.flow_ref), custom_call_target="tpu_custom_call" | custom-call | flops 4194304 | bytes 8388608 | tf_op jit(solution)/shard_map/pallas_call | solution.py:509
  14.2 3.6 %collective-permute-done.far_ref = f32[2,1024]{1,0:T(2,128)S(1)} collective-permute-done((f32[2,1024]{1,0:T(2,128)S(1)}, f32[2,1024]{1,0:T(2,128)S(1)}, u32[]{:S(2)}, u32[]{:S(2)}) %collective-permute-start) | collective-permute-done | bytes 8224 | tf_op jit(solution)/shard_map/ppermute | solution.py:469
  17.8 0.0 collective-permute-done.2.near_ref
  17.8 0.0 collective-permute-done.1.outer_ref
  17.8 0.0 collective-permute-done.3.inner_ref
  17.8 0.6 %shard_map.115 = (f32[16,1024]{1,0:T(8,128)S(1)}, f32[16,1024]{1,0:T(8,128)S(1)}, f32[16,1024]{1,0:T(8,128)S(1)}, f32[2,1024]{1,0:T(2,128)S(1)}, f32[1,1024]{1,0...) custom-call(f32[1]{0:T(128)S(6)} %copy.12.low_ref, f32[1]{0:T(128)S(6)} %copy.13.high_ref, ...), custom_call_target="tpu_custom_call" | custom-call | tf_op jit(solution)/shard_map/pallas_call | solution.py:510
  18.5 0.9 %collective-permute-start.4 = (f32[1,1024]{1,0:T(1,128)S(1)}, f32[1,1024]{1,0:T(1,128)S(1)}, u32[]{:S(2)}, u32[]{:S(2)}) collective-permute-start(f32[1,1024]{1,0:T(1,128)S(1)} %get-tuple-element.54), channel_id=1, source_target_pairs={{0,15},{1,2},{2,1},{3,4},{4,3},{5,6},{6,5},{7,8},{8,7},{9,10},{10,... | collective-permute-start | bytes 12296 | tf_op jit(solution)/shard_map/ppermute | solution.py:462
  19.4 0.0 collective-permute-start.5
  19.4 1.6 %shard_map.116 = (f32[16,1024]{1,0:T(8,128)S(1)}, f32[16,1024]{1,0:T(8,128)S(1)}, f32[16,1024]{1,0:T(8,128)S(1)}, f32[16,1024]{1,0:T(8,128)S(1)}, f32[1,1024]{1,0:T(1,128)S(1)}) custom-call(f32[16,1024]{1,0:T(8,128)S(1)} %get-tuple-element.56.residual_ref, f32[16,1024]{1,0:T(8,128)S(1)} %get-tuple-element.57.direction_ref, ...), custom_call_target="tpu_custom_call" | custom-call | flops 4194304 | bytes 8388608 | tf_op jit(solution)/shard_map/pallas_call | solution.py:521
  21.0 3.3 %collective-permute-done.4.outer_ref = f32[1,1024]{1,0:T(1,128)S(1)} collective-permute-done((f32[1,1024]{1,0:T(1,128)S(1)}, f32[1,1024]{1,0:T(1,128)S(1)}, u32[]{:S(2)}, u32[]{:S(2)}) %collective-permute-start.4) | collective-permute-done | bytes 4128 | tf_op jit(solution)/shard_map/ppermute | solution.py:462
  24.3 0.0 collective-permute-done.5.inner_ref
  24.3 0.3 shard_map.117
  24.6 0.1 collective-permute-start.8
  24.7 0.1 collective-permute-start.7
  24.8 1.8 %collective-permute-start.6 = (f32[8,1024]{1,0:T(8,128)S(1)}, f32[8,1024]{1,0:T(8,128)S(1)}, u32[]{:S(2)}, u32[]{:S(2)}) collective-permute-start(f32[8,1024]{1,0:T(8,128)S(1)} %get-tuple-element.67.refs_0_), channel_id=1, source_target_pairs={{0,1},{1,0},{2,3},{3,2},{4,5},{5,4},{6,7},{7,6},{8,9},{9,8},{10,11... | collective-permute-start | bytes 98312 | tf_op jit(solution)/shard_map/ppermute | solution.py:475
  26.5 1.5 %collective-permute-done.8.refs_3_ = f32[8,1024]{1,0:T(8,128)S(1)} collective-permute-done((f32[8,1024]{1,0:T(8,128)S(1)}, f32[8,1024]{1,0:T(8,128)S(1)}, u32[]{:S(2)}, u32[]{:S(2)}) %collective-permute-start.8) | collective-permute-done | bytes 32800 | tf_op jit(solution)/shard_map/ppermute | solution.py:475
  28.0 0.7 %collective-permute-done.7.refs_2_ = f32[8,1024]{1,0:T(8,128)S(1)} collective-permute-done((f32[8,1024]{1,0:T(8,128)S(1)}, f32[8,1024]{1,0:T(8,128)S(1)}, u32[]{:S(2)}, u32[]{:S(2)}) %collective-permute-start.7) | collective-permute-done | bytes 32800 | tf_op jit(solution)/shard_map/ppermute | solution.py:475
  28.7 0.0 collective-permute-done.6.refs_1_
  28.8 0.1 collective-permute-start.11
  28.8 1.4 %collective-permute-start.10 = (f32[8,1024]{1,0:T(8,128)S(1)}, f32[8,1024]{1,0:T(8,128)S(1)}, u32[]{:S(2)}, u32[]{:S(2)}) collective-permute-start(f32[8,1024]{1,0:T(8,128)S(1)} %get-tuple-element.68.refs_0_), channel_id=1, source_target_pairs={{0,12},{1,13},{2,14},{3,15},{4,8},{5,9},{6,10},{7,11},{8,4},{9,5},... | collective-permute-start | bytes 98312 | tf_op jit(solution)/shard_map/ppermute | solution.py:475
  30.2 2.1 %collective-permute-start.9 = (f32[8,1024]{1,0:T(8,128)S(1)}, f32[8,1024]{1,0:T(8,128)S(1)}, u32[]{:S(2)}, u32[]{:S(2)}) collective-permute-start(f32[8,1024]{1,0:T(8,128)S(1)} %get-tuple-element.68.refs_0_), channel_id=1, source_target_pairs={{0,4},{1,5},{2,6},{3,7},{4,0},{5,1},{6,2},{7,3},{8,12},{9,13},{10,... | collective-permute-start | bytes 98312 | tf_op jit(solution)/shard_map/ppermute | solution.py:475
  32.3 1.5 %collective-permute-done.11.refs_3_ = f32[8,1024]{1,0:T(8,128)S(1)} collective-permute-done((f32[8,1024]{1,0:T(8,128)S(1)}, f32[8,1024]{1,0:T(8,128)S(1)}, u32[]{:S(2)}, u32[]{:S(2)}) %collective-permute-start.11) | collective-permute-done | bytes 32800 | tf_op jit(solution)/shard_map/ppermute | solution.py:475
  33.9 0.8 %collective-permute-done.10.refs_2_ = f32[8,1024]{1,0:T(8,128)S(1)} collective-permute-done((f32[8,1024]{1,0:T(8,128)S(1)}, f32[8,1024]{1,0:T(8,128)S(1)}, u32[]{:S(2)}, u32[]{:S(2)}) %collective-permute-start.10) | collective-permute-done | bytes 32800 | tf_op jit(solution)/shard_map/ppermute | solution.py:475
  34.6 0.0 collective-permute-done.9.refs_1_
  34.6 0.7 %shard_map.119 = (f32[16,1024]{1,0:T(8,128)}, f32[16,1024]{1,0:T(8,128)}, f32[4]{0:T(128)}) custom-call(f32[8,1024]{1,0:T(8,128)S(1)} %get-tuple-element.68.refs_0_, f32[8,1024]{1,0:T(8,128)S(1)} %collective-permute-done.9.refs_1_, f32[8,1024]{1,0:T(8,128)S(1)} %collective-permute-done.10.refs_2_, f32[8,1024]{1,0:T(8,128)S(1)} %collective-permute-done.11.refs_3_, ...), custom_call_target="tpu_custom_call" | custom-call | tf_op jit(solution)/shard_map/pallas_call | solution.py:549
  (12 shorter events, 0.1 us)
Async XLA Ops:
  0.6 4.1 %copy-start.5 = (s32[1536]{0:T(1024)S(1)}, s32[1536]{0:T(1024)}, u32[]{:S(2)}) copy-start(s32[1536]{0:T(1024)} %param.15) | copy-start | bytes 18436
  0.6 4.1 %copy-start.4 = (s32[16,1024]{1,0:T(8,128)S(1)}, s32[16,1024]{1,0:T(8,128)}, u32[]{:S(2)}) copy-start(s32[16,1024]{1,0:T(8,128)} %mask_ref.1) | copy-start | bytes 196612
  0.7 4.1 %copy-start.3 = (f32[16,1024]{1,0:T(8,128)S(1)}, f32[16,1024]{1,0:T(8,128)}, u32[]{:S(2)}) copy-start(f32[16,1024]{1,0:T(8,128)} %surface_ref.1) | copy-start | bytes 196612
  0.7 4.1 %copy-start.2 = (f32[16,1024]{1,0:T(8,128)S(1)}, f32[16,1024]{1,0:T(8,128)}, u32[]{:S(2)}) copy-start(f32[16,1024]{1,0:T(8,128)} %north_ref.1) | copy-start | bytes 196612
  0.7 4.1 %copy-start.1 = (f32[16,1024]{1,0:T(8,128)S(1)}, f32[16,1024]{1,0:T(8,128)}, u32[]{:S(2)}) copy-start(f32[16,1024]{1,0:T(8,128)} %east_ref.1) | copy-start | bytes 196612
  0.7 4.1 %copy-start = (f32[16,1024]{1,0:T(8,128)S(1)}, f32[16,1024]{1,0:T(8,128)}, u32[]{:S(2)}) copy-start(f32[16,1024]{1,0:T(8,128)} %right_ref.1) | copy-start | bytes 196612
  6.0 11.9 %collective-permute-start.1 = (f32[24,1024]{1,0:T(8,128)S(1)}, f32[24,1024]{1,0:T(8,128)S(1)}, u32[]{:S(2)}, u32[]{:S(2)}) collective-permute-start(f32[24,1024]{1,0:T(8,128)S(1)} %get-tuple-element.43), channel_id=1, source_target_pairs={{0,15},{1,2},{2,1},{3,4},{4,3},{5,6},{6,5},{7,8},{8,7},{9,10},{10,... | collective-permute-start | bytes 294920 | tf_op jit(solution)/shard_map/ppermute | solution.py:462
  11.5 6.4 %collective-permute-start.3 = (f32[24,1024]{1,0:T(8,128)S(1)}, f32[24,1024]{1,0:T(8,128)S(1)}, u32[]{:S(2)}, u32[]{:S(2)}) collective-permute-start(f32[24,1024]{1,0:T(8,128)S(1)} %get-tuple-element.45), channel_id=1, source_target_pairs={{0,1},{1,0},{2,3},{3,2},{4,5},{5,4},{6,7},{7,6},{8,9},{9,8},{10,11... | collective-permute-start | bytes 294920 | tf_op jit(solution)/shard_map/ppermute | solution.py:462
  11.5 6.3 %collective-permute-start = (f32[2,1024]{1,0:T(2,128)S(1)}, f32[2,1024]{1,0:T(2,128)S(1)}, u32[]{:S(2)}, u32[]{:S(2)}) collective-permute-start(f32[2,1024]{1,0:T(2,128)S(1)} %get-tuple-element.42), channel_id=1, source_target_pairs={{0,14},{1,15},{2,4},{3,5},{4,2},{5,3},{6,8},{7,9},{8,6},{9,7},{10,... | collective-permute-start | bytes 24584 | tf_op jit(solution)/shard_map/ppermute | solution.py:469
  12.2 5.6 %collective-permute-start.2 = (f32[2,1024]{1,0:T(2,128)S(1)}, f32[2,1024]{1,0:T(2,128)S(1)}, u32[]{:S(2)}, u32[]{:S(2)}) collective-permute-start(f32[2,1024]{1,0:T(2,128)S(1)} %get-tuple-element.44), channel_id=1, source_target_pairs={{0,2},{1,3},{2,0},{3,1},{4,6},{5,7},{6,4},{7,5},{8,10},{9,11},{10,... | collective-permute-start | bytes 24584 | tf_op jit(solution)/shard_map/ppermute | solution.py:469
  18.5 5.8 %collective-permute-start.4 = (f32[1,1024]{1,0:T(1,128)S(1)}, f32[1,1024]{1,0:T(1,128)S(1)}, u32[]{:S(2)}, u32[]{:S(2)}) collective-permute-start(f32[1,1024]{1,0:T(1,128)S(1)} %get-tuple-element.54), channel_id=1, source_target_pairs={{0,15},{1,2},{2,1},{3,4},{4,3},{5,6},{6,5},{7,8},{8,7},{9,10},{10,... | collective-permute-start | bytes 12296 | tf_op jit(solution)/shard_map/ppermute | solution.py:462
  19.4 4.9 %collective-permute-start.5 = (f32[1,1024]{1,0:T(1,128)S(1)}, f32[1,1024]{1,0:T(1,128)S(1)}, u32[]{:S(2)}, u32[]{:S(2)}) collective-permute-start(f32[1,1024]{1,0:T(1,128)S(1)} %get-tuple-element.55), channel_id=1, source_target_pairs={{0,1},{1,0},{2,3},{3,2},{4,5},{5,4},{6,7},{7,6},{8,9},{9,8},{10,11... | collective-permute-start | bytes 12296 | tf_op jit(solution)/shard_map/ppermute | solution.py:462
  24.6 3.4 %collective-permute-start.8 = (f32[8,1024]{1,0:T(8,128)S(1)}, f32[8,1024]{1,0:T(8,128)S(1)}, u32[]{:S(2)}, u32[]{:S(2)}) collective-permute-start(f32[8,1024]{1,0:T(8,128)S(1)} %get-tuple-element.67.refs_0_), channel_id=1, source_target_pairs={{0,3},{1,2},{2,1},{3,0},{4,7},{5,6},{6,5},{7,4},{8,11},{9,10},{10,... | collective-permute-start | bytes 98312 | tf_op jit(solution)/shard_map/ppermute | solution.py:475
  24.7 4.0 %collective-permute-start.7 = (f32[8,1024]{1,0:T(8,128)S(1)}, f32[8,1024]{1,0:T(8,128)S(1)}, u32[]{:S(2)}, u32[]{:S(2)}) collective-permute-start(f32[8,1024]{1,0:T(8,128)S(1)} %get-tuple-element.67.refs_0_), channel_id=1, source_target_pairs={{0,2},{1,3},{2,0},{3,1},{4,6},{5,7},{6,4},{7,5},{8,10},{9,11},{10,... | collective-permute-start | bytes 98312 | tf_op jit(solution)/shard_map/ppermute | solution.py:475
  24.8 4.0 %collective-permute-start.6 = (f32[8,1024]{1,0:T(8,128)S(1)}, f32[8,1024]{1,0:T(8,128)S(1)}, u32[]{:S(2)}, u32[]{:S(2)}) collective-permute-start(f32[8,1024]{1,0:T(8,128)S(1)} %get-tuple-element.67.refs_0_), channel_id=1, source_target_pairs={{0,1},{1,0},{2,3},{3,2},{4,5},{5,4},{6,7},{7,6},{8,9},{9,8},{10,11... | collective-permute-start | bytes 98312 | tf_op jit(solution)/shard_map/ppermute | solution.py:475
  28.8 5.1 %collective-permute-start.11 = (f32[8,1024]{1,0:T(8,128)S(1)}, f32[8,1024]{1,0:T(8,128)S(1)}, u32[]{:S(2)}, u32[]{:S(2)}) collective-permute-start(f32[8,1024]{1,0:T(8,128)S(1)} %get-tuple-element.68.refs_0_), channel_id=1, source_target_pairs={{0,8},{1,9},{2,10},{3,11},{4,12},{5,13},{6,14},{7,15},{8,0},{9,1},... | collective-permute-start | bytes 98312 | tf_op jit(solution)/shard_map/ppermute | solution.py:475
  28.8 5.8 %collective-permute-start.10 = (f32[8,1024]{1,0:T(8,128)S(1)}, f32[8,1024]{1,0:T(8,128)S(1)}, u32[]{:S(2)}, u32[]{:S(2)}) collective-permute-start(f32[8,1024]{1,0:T(8,128)S(1)} %get-tuple-element.68.refs_0_), channel_id=1, source_target_pairs={{0,12},{1,13},{2,14},{3,15},{4,8},{5,9},{6,10},{7,11},{8,4},{9,5},... | collective-permute-start | bytes 98312 | tf_op jit(solution)/shard_map/ppermute | solution.py:475
  30.2 4.4 %collective-permute-start.9 = (f32[8,1024]{1,0:T(8,128)S(1)}, f32[8,1024]{1,0:T(8,128)S(1)}, u32[]{:S(2)}, u32[]{:S(2)}) collective-permute-start(f32[8,1024]{1,0:T(8,128)S(1)} %get-tuple-element.68.refs_0_), channel_id=1, source_target_pairs={{0,4},{1,5},{2,6},{3,7},{4,0},{5,1},{6,2},{7,3},{8,12},{9,13},{10,... | collective-permute-start | bytes 98312 | tf_op jit(solution)/shard_map/ppermute | solution.py:475

commit v8 on v7

--- a/solution.py
+++ b/solution.py
@@ -335,7 +335,12 @@
     blocks_product(bt_ref, residual, product_out)
 
 
-FIRST_RES, FIRST_DIR, LAST_RES, LAST_DIR, LAST_FACE, SUMS, PACK_ROWS = 0, 1, 2, 3, 4, 5, 8
+FIRST_RES, FIRST_PUSH, LAST_RES, LAST_PUSH, SUMS, PACK_PARTS = 0, 1, 2, 3, 4, 5
+
+
+def store_row(pack_ref, part, row):
+    for i in range(pack_ref.shape[1]):
+        pack_ref[part, i : i + 1, :] = row[:, i * LANES : (i + 1) * LANES]
 
 
 def closing_kernel(
@@ -350,20 +355,20 @@
     later = keep * direction_ref[...] + gain * (ocean_ref[...] * product)
     solution_out[...] = solution_ref[...] + later
     columns = residual.shape[0]
-    sums = pack_out.at[SUMS : SUMS + 1]
-    store_norm(sums, norms_ref, ITERS - 2, residual * residual)
+    pack_out[SUMS] = jnp.zeros(pack_out.shape[1:], F32)
+    for k in range(ITERS - 2):
+        pack_out[SUMS, k : k + 1, :] = norms_ref[0:1, k * LANES : (k + 1) * LANES]
+    pack_out[SUMS, ITERS - 2 : ITERS - 1, :] = lane_partial(residual * residual)
     nothing = jnp.zeros_like(west)
     residual = apply_operator(residual, later, diag_ref[...], east_face_ref[...], north_face_ref[...], nothing, nothing)
     residual_out[...] = residual
     lon = lax.broadcasted_iota(jnp.int32, residual.shape, 0)
     inside = jnp.where((lon > 0) & (lon < columns - 1), residual, 0.0)
-    sums[0:1, (ITERS - 1) * LANES : ITERS * LANES] = lane_partial(inside * inside)
-    pack_out[FIRST_RES : FIRST_RES + 1] = residual[0:1]
-    pack_out[FIRST_DIR : FIRST_DIR + 1] = later[0:1]
-    pack_out[LAST_RES : LAST_RES + 1] = residual[columns - 1 :]
-    pack_out[LAST_DIR : LAST_DIR + 1] = later[columns - 1 :]
-    pack_out[LAST_FACE : LAST_FACE + 1] = faces_ref[1:2]
-    pack_out[SUMS + 1 :] = jnp.zeros_like(pack_out[SUMS + 1 :])
+    pack_out[SUMS, ITERS - 1 : ITERS, :] = lane_partial(inside * inside)
+    store_row(pack_out, FIRST_RES, residual[0:1])
+    store_row(pack_out, FIRST_PUSH, faces_ref[0:1] * later[0:1])
+    store_row(pack_out, LAST_RES, residual[columns - 1 :])
+    store_row(pack_out, LAST_PUSH, faces_ref[1:2] * later[columns - 1 :])
 
 
 def swap_order(size, radix):
@@ -377,21 +382,20 @@
     for s, other in zip(swap_order(size, radix), others):
         packs[mine ^ s] = other[...]
 
-    def row(run, name):
-        return packs[run % radix, name : name + 1, :]
-
-    sums = functools.reduce(jnp.add, [row(run, SUMS) for run in range(radix)])
-    total = None
+    def part(run, name):
+        return packs[run % radix, name]
+
+    sums = functools.reduce(jnp.add, [part(run, SUMS) for run in range(radix)])
+    squares = []
     for run in range(radix if is_last else radix - 1):
-        face = row(run, LAST_FACE)
-        left = row(run, LAST_RES) + face * row(run + 1, FIRST_DIR)
-        right = row(run + 1, FIRST_RES) + face * row(run, LAST_DIR)
-        squares = lane_partial(left * left + right * right)
-        total = squares if total is None else total + squares
-    parts = [sums[:, i * LANES : (i + 1) * LANES] for i in range(sums.shape[1] // LANES)]
-    parts[ITERS - 1] = parts[ITERS - 1] + total
-    before = packs[lax.rem(mine + radix - 1, radix)][LAST_DIR : LAST_DIR + 1]
-    after = packs[lax.rem(mine + 1, radix)][FIRST_DIR : FIRST_DIR + 1]
+        left = part(run, LAST_RES) + part(run + 1, FIRST_PUSH)
+        right = part(run + 1, FIRST_RES) + part(run, LAST_PUSH)
+        squares.append(left * left + right * right)
+    total = jnp.sum(functools.reduce(jnp.add, squares), axis=0, keepdims=True)
+    sub = lax.broadcasted_iota(jnp.int32, sums.shape, 0)
+    sums = jnp.where(sub == ITERS - 1, sums + total, sums)
+    before = packs[lax.rem(mine + radix - 1, radix), LAST_PUSH]
+    after = packs[lax.rem(mine + 1, radix), FIRST_PUSH]
     place = lax.rem(me, size)
     west_now = place == 0
     east_now = place == size - 1
@@ -399,36 +403,35 @@
         west_now = west_now & (mine > 0)
         east_now = east_now & (mine < radix - 1)
     west, east = halo
-    return parts, jnp.where(west_now, before, west), jnp.where(east_now, after, east)
+    return sums, jnp.where(west_now, before, west), jnp.where(east_now, after, east)
 
 
 def stage_kernel(size, radix, *refs):
     pack_ref, others, halo_ref = refs[0], refs[1:radix], refs[radix] if size > 1 else None
     pack_out, halo_out, packs = refs[-3:]
-    nothing = jnp.zeros((1, pack_ref.shape[1]), F32)
-    halo = (nothing, nothing) if halo_ref is None else (halo_ref[0:1], halo_ref[1:2])
-    parts, west, east = join_packs(size, radix, False, pack_ref, others, halo, packs)
+    nothing = jnp.zeros(pack_ref.shape[1:], F32)
+    halo = (nothing, nothing) if halo_ref is None else (halo_ref[0], halo_ref[1])
+    sums, west, east = join_packs(size, radix, False, pack_ref, others, halo, packs)
     pack_out[...] = packs[0]
-    for name in (LAST_RES, LAST_DIR, LAST_FACE):
-        pack_out[name : name + 1] = packs[radix - 1, name : name + 1, :]
-    pack_out[SUMS : SUMS + 1] = jnp.concatenate(parts, axis=1)
-    halo_out[0:1] = west
-    halo_out[1:2] = east
+    for name in (LAST_RES, LAST_PUSH):
+        pack_out[name] = packs[radix - 1, name]
+    pack_out[SUMS] = sums
+    halo_out[0] = west
+    halo_out[1] = east
 
 
 def finish_kernel(size, radix, cells_all, *refs):
     pack_ref, others, halo_ref = refs[0], refs[1:radix], refs[radix]
-    residual_ref, faces_ref, answer_ref = refs[radix + 1 : radix + 4]
-    residual_out, answer_out, norms_out, packs = refs[radix + 4 :]
-    parts, west, east = join_packs(size, radix, True, pack_ref, others, (halo_ref[0:1], halo_ref[1:2]), packs)
+    residual_ref, answer_ref = refs[radix + 1 : radix + 3]
+    residual_out, answer_out, norms_out, packs = refs[radix + 3 :]
+    sums, *pushes = join_packs(size, radix, True, pack_ref, others, (halo_ref[0], halo_ref[1]), packs)
     answer_out[...] = answer_ref[...]
-    residual = residual_ref[...]
-    lon = lax.broadcasted_iota(jnp.int32, residual.shape, 0)
-    residual = jnp.where(lon == 0, residual + faces_ref[0:1] * west, residual)
-    residual = jnp.where(lon == residual.shape[0] - 1, residual + faces_ref[1:2] * east, residual)
-    residual_out[...] = residual
+    west, east = (
+        jnp.concatenate([push[i : i + 1] for i in range(push.shape[0])], axis=1) for push in pushes
+    )
+    residual_out[...] = add_sides(residual_ref[...], west, east)
     for k in range(ITERS):
-        norms_out[k] = jnp.sum(parts[k]) / cells_all
+        norms_out[k] = jnp.sum(sums[k : k + 1]) / cells_all
 
 
 def vmem():
@@ -526,7 +529,7 @@
         24 * MIB,
         work,
     )(residual, direction, search, diag, east_face, north_face, ocean, coef, norms, bt)
-    pack_shape = shape(PACK_ROWS, rows)
+    pack_shape = shape(PACK_PARTS, count, LANES)
     residual, answer, pack = call(closing_kernel, [vmem()] * 14, [field, field, pack_shape], [], 24 * MIB)(
         outer, inner, residual, direction, answer, product, diag, east_face, north_face, ocean, faces, coef, norms, bt
     )
@@ -535,25 +538,25 @@
     while True:
         radix = 4 if (devices // size) % 4 == 0 else 2
         others = swap_runs(pack, size, radix)
-        packs = [pltpu.VMEM((radix, PACK_ROWS, rows), F32)]
+        packs = [pltpu.VMEM((radix, PACK_PARTS, count, LANES), F32)]
         if size * radix == devices:
             break
         pack, *halo = call(
             functools.partial(stage_kernel, size, radix),
             [vmem()] * (radix + len(halo)),
-            [pack_shape, two],
+            [pack_shape, shape(2, count, LANES)],
             packs,
             24 * MIB,
         )(pack, *others, *halo)
         size *= radix
     residual, answer, norms = call(
         functools.partial(finish_kernel, size, radix, float(columns * devices * rows)),
-        [vmem()] * (radix + 4),
+        [vmem()] * (radix + 3),
         [field, field, shape(ITERS)],
         packs,
         24 * MIB,
         out_specs=[vmem(), vmem(), smem()],
-    )(pack, *others, *halo, residual, faces, answer)
+    )(pack, *others, *halo, residual, answer)
     return answer, residual, norms
 
 

time: 35.5 us -> 35.2 us (level)
  no operation moved by 1% of the time
where the time goes in v8:
time: 35.2 us; the launch traced here: 35 us
  starting transfers between devices  12.6 us (36%)
  waiting for transfers between devices  11 us (31%)
  Pallas kernels  9.23 us (26%)
  between operations  2.1 us (6%)
    ppermute x2, starting transfers between devices, exchange(): lax.ppermute(outer, 'lon', across)  6.42 us
    ppermute x6, starting transfers between devices, swap_runs(): lax.ppermute(pack, 'lon', [(i, i ^ s * size) for i in range(devices)])  5.46 us
    ppermute x6, waiting for transfers between devices, swap_runs(): lax.ppermute(pack, 'lon', [(i, i ^ s * size) for i in range(devices)])  4.17 us
    pallas_call x1, Pallas kernels, on_device(): call(transpose_kernel, [pl.BlockSpec(memory_space=pl.ANY)], [bt_shape], [...  4.07 us
    ppermute x2, waiting for transfers between devices, exchange_beyond(): return (lax.ppermute(near, 'lon', within), lax.ppermute(far, 'lon', across))  3.59 us
    ppermute x2, waiting for transfers between devices, exchange(): lax.ppermute(outer, 'lon', across)  3.27 us
    pallas_call x1, Pallas kernels, on_device(): call(ahead_kernel, [vmem()] * 10, [field, field, field, field, row], [],...  1.61 us
    pallas_call x1, Pallas kernels, on_device(): call(first_kernel, [vmem()] * 7, [field, field, field, field, field, fiel...  1.13 us
  transfers between devices with their start and end apart: 12, of which 6 were waited for; matrix products, arithmetic and copies ran while one was open for 0% of the time, Pallas kernels for 7%

profile of v8, /device:TPU:0, one launch (start us, length us, event | category | flops | bytes accessed | tf_op | source)
XLA Modules:
  0.0 35.0 jit_solution(8721262981057380170)
XLA Ops:
  0.6 0.0 copy-start.5
  0.7 4.1 %shard_map.112.bt_ref = f32[8,16,128,128]{3,2,1,0:T(8,128)S(1)} custom-call(f32[128,128,128]{2,1,0:T(8,128)} %blocks_hbm.1), custom_call_target="tpu_custom_call" | custom-call | flops 1000000000 | bytes 16777216 | tf_op jit(solution)/shard_map/pallas_call | solution.py:492
  4.8 1.1 %shard_map.113 = (f32[16,1024]{1,0:T(8,128)S(1)}, f32[16,1024]{1,0:T(8,128)S(1)}, f32[16,1024]{1,0:T(8,128)S(1)}, f32[16,1024]{1,0:T(8,128)S(1)}, f32[16,1024]{1...) custom-call(s32[12,128]{1,0:T(8,128)S(1)} %bitcast.1, ...), custom_call_target="tpu_custom_call" | custom-call | tf_op jit(solution)/shard_map/pallas_call | solution.py:501
  6.0 5.5 %collective-permute-start.1 = (f32[24,1024]{1,0:T(8,128)S(1)}, f32[24,1024]{1,0:T(8,128)S(1)}, u32[]{:S(2)}, u32[]{:S(2)}) collective-permute-start(f32[24,1024]{1,0:T(8,128)S(1)} %get-tuple-element.43), channel_id=1, source_target_pairs={{0,15},{1,2},{2,1},{3,4},{4,3},{5,6},{6,5},{7,8},{8,7},{9,10},{10,... | collective-permute-start | bytes 294920 | tf_op jit(solution)/shard_map/ppermute | solution.py:465
  11.5 0.0 collective-permute-start.3
  11.5 0.7 %collective-permute-start = (f32[2,1024]{1,0:T(2,128)S(1)}, f32[2,1024]{1,0:T(2,128)S(1)}, u32[]{:S(2)}, u32[]{:S(2)}) collective-permute-start(f32[2,1024]{1,0:T(2,128)S(1)} %get-tuple-element.42), channel_id=1, source_target_pairs={{0,14},{1,15},{2,4},{3,5},{4,2},{5,3},{6,8},{7,9},{8,6},{9,7},{10,... | collective-permute-start | bytes 24584 | tf_op jit(solution)/shard_map/ppermute | solution.py:472
  12.2 0.0 collective-permute-start.2
  13.5 0.7 %shard_map.114.product_ref = f32[16,1024]{1,0:T(8,128)S(1)} custom-call(f32[8,16,128,128]{3,2,1,0:T(8,128)S(1)} %shard_map.112.bt_ref, f32[16,1024]{1,0:T(8,128)S(1)} %get-tuple-element.48.field_ref.flow_ref), custom_call_target="tpu_custom_call" | custom-call | flops 4194304 | bytes 8388608 | tf_op jit(solution)/shard_map/pallas_call | solution.py:512
  14.2 3.6 %collective-permute-done.far_ref = f32[2,1024]{1,0:T(2,128)S(1)} collective-permute-done((f32[2,1024]{1,0:T(2,128)S(1)}, f32[2,1024]{1,0:T(2,128)S(1)}, u32[]{:S(2)}, u32[]{:S(2)}) %collective-permute-start) | collective-permute-done | bytes 8224 | tf_op jit(solution)/shard_map/ppermute | solution.py:472
  17.8 0.0 collective-permute-done.2.near_ref
  17.8 0.0 collective-permute-done.1.outer_ref
  17.8 0.0 collective-permute-done.3.inner_ref
  17.8 0.6 %shard_map.115 = (f32[16,1024]{1,0:T(8,128)S(1)}, f32[16,1024]{1,0:T(8,128)S(1)}, f32[16,1024]{1,0:T(8,128)S(1)}, f32[2,1024]{1,0:T(2,128)S(1)}, f32[1,1024]{1,0...) custom-call(f32[1]{0:T(128)S(6)} %copy.12.low_ref, f32[1]{0:T(128)S(6)} %copy.13.high_ref, ...), custom_call_target="tpu_custom_call" | custom-call | tf_op jit(solution)/shard_map/pallas_call | solution.py:513
  18.5 0.9 %collective-permute-start.4 = (f32[1,1024]{1,0:T(1,128)S(1)}, f32[1,1024]{1,0:T(1,128)S(1)}, u32[]{:S(2)}, u32[]{:S(2)}) collective-permute-start(f32[1,1024]{1,0:T(1,128)S(1)} %get-tuple-element.54), channel_id=1, source_target_pairs={{0,15},{1,2},{2,1},{3,4},{4,3},{5,6},{6,5},{7,8},{8,7},{9,10},{10,... | collective-permute-start | bytes 12296 | tf_op jit(solution)/shard_map/ppermute | solution.py:465
  19.4 0.0 collective-permute-start.5
  19.4 1.6 %shard_map.116 = (f32[16,1024]{1,0:T(8,128)S(1)}, f32[16,1024]{1,0:T(8,128)S(1)}, f32[16,1024]{1,0:T(8,128)S(1)}, f32[16,1024]{1,0:T(8,128)S(1)}, f32[1,1024]{1,0:T(1,128)S(1)}) custom-call(f32[16,1024]{1,0:T(8,128)S(1)} %get-tuple-element.56.residual_ref, f32[16,1024]{1,0:T(8,128)S(1)} %get-tuple-element.57.direction_ref, ...), custom_call_target="tpu_custom_call" | custom-call | flops 4194304 | bytes 8388608 | tf_op jit(solution)/shard_map/pallas_call | solution.py:524
  21.0 3.3 %collective-permute-done.4.outer_ref = f32[1,1024]{1,0:T(1,128)S(1)} collective-permute-done((f32[1,1024]{1,0:T(1,128)S(1)}, f32[1,1024]{1,0:T(1,128)S(1)}, u32[]{:S(2)}, u32[]{:S(2)}) %collective-permute-start.4) | collective-permute-done | bytes 4128 | tf_op jit(solution)/shard_map/ppermute | solution.py:465
  24.3 0.0 collective-permute-done.5.inner_ref
  24.3 0.3 shard_map.117
  24.6 0.1 collective-permute-start.8
  24.7 0.1 collective-permute-start.7
  24.8 1.8 %collective-permute-start.6 = (f32[5,8,128]{2,1,0:T(8,128)S(1)}, f32[5,8,128]{2,1,0:T(8,128)S(1)}, u32[]{:S(2)}, u32[]{:S(2)}) collective-permute-start(f32[5,8,128]{2,1,0:T(8,128)S(1)} %get-tuple-element.67.refs_0_), channel_id=1, source_target_pairs={{0,1},{1,0},{2,3},{3,2},{4,5},{5,4},{6,7},{7,6},{8,9},{9,8},{10,11... | collective-permute-start | bytes 61448 | tf_op jit(solution)/shard_map/ppermute | solution.py:478
  26.5 1.3 %collective-permute-done.8.refs_3_ = f32[5,8,128]{2,1,0:T(8,128)S(1)} collective-permute-done((f32[5,8,128]{2,1,0:T(8,128)S(1)}, f32[5,8,128]{2,1,0:T(8,128)S(1)}, u32[]{:S(2)}, u32[]{:S(2)}) %collective-permute-start.8) | collective-permute-done | bytes 20512 | tf_op jit(solution)/shard_map/ppermute | solution.py:478
  27.9 0.7 %collective-permute-done.7.refs_2_ = f32[5,8,128]{2,1,0:T(8,128)S(1)} collective-permute-done((f32[5,8,128]{2,1,0:T(8,128)S(1)}, f32[5,8,128]{2,1,0:T(8,128)S(1)}, u32[]{:S(2)}, u32[]{:S(2)}) %collective-permute-start.7) | collective-permute-done | bytes 20512 | tf_op jit(solution)/shard_map/ppermute | solution.py:478
  28.5 0.0 collective-permute-done.6.refs_1_
  28.6 0.1 collective-permute-start.11
  28.6 1.4 %collective-permute-start.10 = (f32[5,8,128]{2,1,0:T(8,128)S(1)}, f32[5,8,128]{2,1,0:T(8,128)S(1)}, u32[]{:S(2)}, u32[]{:S(2)}) collective-permute-start(f32[5,8,128]{2,1,0:T(8,128)S(1)} %get-tuple-element.68.refs_0_), channel_id=1, source_target_pairs={{0,12},{1,13},{2,14},{3,15},{4,8},{5,9},{6,10},{7,11},{8,4},{9,5},... | collective-permute-start | bytes 61448 | tf_op jit(solution)/shard_map/ppermute | solution.py:478
  30.1 2.1 %collective-permute-start.9 = (f32[5,8,128]{2,1,0:T(8,128)S(1)}, f32[5,8,128]{2,1,0:T(8,128)S(1)}, u32[]{:S(2)}, u32[]{:S(2)}) collective-permute-start(f32[5,8,128]{2,1,0:T(8,128)S(1)} %get-tuple-element.68.refs_0_), channel_id=1, source_target_pairs={{0,4},{1,5},{2,6},{3,7},{4,0},{5,1},{6,2},{7,3},{8,12},{9,13},{10,... | collective-permute-start | bytes 61448 | tf_op jit(solution)/shard_map/ppermute | solution.py:478
  32.1 1.2 %collective-permute-done.11.refs_3_ = f32[5,8,128]{2,1,0:T(8,128)S(1)} collective-permute-done((f32[5,8,128]{2,1,0:T(8,128)S(1)}, f32[5,8,128]{2,1,0:T(8,128)S(1)}, u32[]{:S(2)}, u32[]{:S(2)}) %collective-permute-start.11) | collective-permute-done | bytes 20512 | tf_op jit(solution)/shard_map/ppermute | solution.py:478
  33.3 1.0 %collective-permute-done.10.refs_2_ = f32[5,8,128]{2,1,0:T(8,128)S(1)} collective-permute-done((f32[5,8,128]{2,1,0:T(8,128)S(1)}, f32[5,8,128]{2,1,0:T(8,128)S(1)}, u32[]{:S(2)}, u32[]{:S(2)}) %collective-permute-start.10) | collective-permute-done | bytes 20512 | tf_op jit(solution)/shard_map/ppermute | solution.py:478
  34.3 0.0 collective-permute-done.9.refs_1_
  34.3 0.7 %shard_map.119 = (f32[16,1024]{1,0:T(8,128)}, f32[16,1024]{1,0:T(8,128)}, f32[4]{0:T(128)}) custom-call(f32[5,8,128]{2,1,0:T(8,128)S(1)} %get-tuple-element.68.refs_0_, f32[5,8,128]{2,1,0:T(8,128)S(1)} %collective-permute-done.9.refs_1_, f32[5,8,128]{2,1,0:T(8,128)S(1)} %collective-permute-done.10.refs_2_, f32[5,8,128]{2,1,0:T(8,128)S(1)} %collective-permute-done.11.refs_3_, ...), custom_call_target="tpu_custom_call" | custom-call | tf_op jit(solution)/shard_map/pallas_call | solution.py:552
  (12 shorter events, 0.1 us)
Async XLA Ops:
  0.6 4.1 %copy-start.5 = (s32[1536]{0:T(1024)S(1)}, s32[1536]{0:T(1024)}, u32[]{:S(2)}) copy-start(s32[1536]{0:T(1024)} %param.15) | copy-start | bytes 18436
  0.6 4.1 %copy-start.4 = (s32[16,1024]{1,0:T(8,128)S(1)}, s32[16,1024]{1,0:T(8,128)}, u32[]{:S(2)}) copy-start(s32[16,1024]{1,0:T(8,128)} %mask_ref.1) | copy-start | bytes 196612
  0.7 4.1 %copy-start.3 = (f32[16,1024]{1,0:T(8,128)S(1)}, f32[16,1024]{1,0:T(8,128)}, u32[]{:S(2)}) copy-start(f32[16,1024]{1,0:T(8,128)} %surface_ref.1) | copy-start | bytes 196612
  0.7 4.1 %copy-start.2 = (f32[16,1024]{1,0:T(8,128)S(1)}, f32[16,1024]{1,0:T(8,128)}, u32[]{:S(2)}) copy-start(f32[16,1024]{1,0:T(8,128)} %north_ref.1) | copy-start | bytes 196612
  0.7 4.1 %copy-start.1 = (f32[16,1024]{1,0:T(8,128)S(1)}, f32[16,1024]{1,0:T(8,128)}, u32[]{:S(2)}) copy-start(f32[16,1024]{1,0:T(8,128)} %east_ref.1) | copy-start | bytes 196612
  0.7 4.1 %copy-start = (f32[16,1024]{1,0:T(8,128)S(1)}, f32[16,1024]{1,0:T(8,128)}, u32[]{:S(2)}) copy-start(f32[16,1024]{1,0:T(8,128)} %right_ref.1) | copy-start | bytes 196612
  6.0 11.9 %collective-permute-start.1 = (f32[24,1024]{1,0:T(8,128)S(1)}, f32[24,1024]{1,0:T(8,128)S(1)}, u32[]{:S(2)}, u32[]{:S(2)}) collective-permute-start(f32[24,1024]{1,0:T(8,128)S(1)} %get-tuple-element.43), channel_id=1, source_target_pairs={{0,15},{1,2},{2,1},{3,4},{4,3},{5,6},{6,5},{7,8},{8,7},{9,10},{10,... | collective-permute-start | bytes 294920 | tf_op jit(solution)/shard_map/ppermute | solution.py:465
  11.5 6.4 %collective-permute-start.3 = (f32[24,1024]{1,0:T(8,128)S(1)}, f32[24,1024]{1,0:T(8,128)S(1)}, u32[]{:S(2)}, u32[]{:S(2)}) collective-permute-start(f32[24,1024]{1,0:T(8,128)S(1)} %get-tuple-element.45), channel_id=1, source_target_pairs={{0,1},{1,0},{2,3},{3,2},{4,5},{5,4},{6,7},{7,6},{8,9},{9,8},{10,11... | collective-permute-start | bytes 294920 | tf_op jit(solution)/shard_map/ppermute | solution.py:465
  11.5 6.3 %collective-permute-start = (f32[2,1024]{1,0:T(2,128)S(1)}, f32[2,1024]{1,0:T(2,128)S(1)}, u32[]{:S(2)}, u32[]{:S(2)}) collective-permute-start(f32[2,1024]{1,0:T(2,128)S(1)} %get-tuple-element.42), channel_id=1, source_target_pairs={{0,14},{1,15},{2,4},{3,5},{4,2},{5,3},{6,8},{7,9},{8,6},{9,7},{10,... | collective-permute-start | bytes 24584 | tf_op jit(solution)/shard_map/ppermute | solution.py:472
  12.2 5.6 %collective-permute-start.2 = (f32[2,1024]{1,0:T(2,128)S(1)}, f32[2,1024]{1,0:T(2,128)S(1)}, u32[]{:S(2)}, u32[]{:S(2)}) collective-permute-start(f32[2,1024]{1,0:T(2,128)S(1)} %get-tuple-element.44), channel_id=1, source_target_pairs={{0,2},{1,3},{2,0},{3,1},{4,6},{5,7},{6,4},{7,5},{8,10},{9,11},{10,... | collective-permute-start | bytes 24584 | tf_op jit(solution)/shard_map/ppermute | solution.py:472
  18.5 5.8 %collective-permute-start.4 = (f32[1,1024]{1,0:T(1,128)S(1)}, f32[1,1024]{1,0:T(1,128)S(1)}, u32[]{:S(2)}, u32[]{:S(2)}) collective-permute-start(f32[1,1024]{1,0:T(1,128)S(1)} %get-tuple-element.54), channel_id=1, source_target_pairs={{0,15},{1,2},{2,1},{3,4},{4,3},{5,6},{6,5},{7,8},{8,7},{9,10},{10,... | collective-permute-start | bytes 12296 | tf_op jit(solution)/shard_map/ppermute | solution.py:465
  19.4 4.9 %collective-permute-start.5 = (f32[1,1024]{1,0:T(1,128)S(1)}, f32[1,1024]{1,0:T(1,128)S(1)}, u32[]{:S(2)}, u32[]{:S(2)}) collective-permute-start(f32[1,1024]{1,0:T(1,128)S(1)} %get-tuple-element.55), channel_id=1, source_target_pairs={{0,1},{1,0},{2,3},{3,2},{4,5},{5,4},{6,7},{7,6},{8,9},{9,8},{10,11... | collective-permute-start | bytes 12296 | tf_op jit(solution)/shard_map/ppermute | solution.py:465
  24.6 3.3 %collective-permute-start.8 = (f32[5,8,128]{2,1,0:T(8,128)S(1)}, f32[5,8,128]{2,1,0:T(8,128)S(1)}, u32[]{:S(2)}, u32[]{:S(2)}) collective-permute-start(f32[5,8,128]{2,1,0:T(8,128)S(1)} %get-tuple-element.67.refs_0_), channel_id=1, source_target_pairs={{0,3},{1,2},{2,1},{3,0},{4,7},{5,6},{6,5},{7,4},{8,11},{9,10},{10,... | collective-permute-start | bytes 61448 | tf_op jit(solution)/shard_map/ppermute | solution.py:478
  24.7 3.8 %collective-permute-start.7 = (f32[5,8,128]{2,1,0:T(8,128)S(1)}, f32[5,8,128]{2,1,0:T(8,128)S(1)}, u32[]{:S(2)}, u32[]{:S(2)}) collective-permute-start(f32[5,8,128]{2,1,0:T(8,128)S(1)} %get-tuple-element.67.refs_0_), channel_id=1, source_target_pairs={{0,2},{1,3},{2,0},{3,1},{4,6},{5,7},{6,4},{7,5},{8,10},{9,11},{10,... | collective-permute-start | bytes 61448 | tf_op jit(solution)/shard_map/ppermute | solution.py:478
  24.8 3.8 %collective-permute-start.6 = (f32[5,8,128]{2,1,0:T(8,128)S(1)}, f32[5,8,128]{2,1,0:T(8,128)S(1)}, u32[]{:S(2)}, u32[]{:S(2)}) collective-permute-start(f32[5,8,128]{2,1,0:T(8,128)S(1)} %get-tuple-element.67.refs_0_), channel_id=1, source_target_pairs={{0,1},{1,0},{2,3},{3,2},{4,5},{5,4},{6,7},{7,6},{8,9},{9,8},{10,11... | collective-permute-start | bytes 61448 | tf_op jit(solution)/shard_map/ppermute | solution.py:478
  28.6 4.7 %collective-permute-start.11 = (f32[5,8,128]{2,1,0:T(8,128)S(1)}, f32[5,8,128]{2,1,0:T(8,128)S(1)}, u32[]{:S(2)}, u32[]{:S(2)}) collective-permute-start(f32[5,8,128]{2,1,0:T(8,128)S(1)} %get-tuple-element.68.refs_0_), channel_id=1, source_target_pairs={{0,8},{1,9},{2,10},{3,11},{4,12},{5,13},{6,14},{7,15},{8,0},{9,1},... | collective-permute-start | bytes 61448 | tf_op jit(solution)/shard_map/ppermute | solution.py:478
  28.6 5.6 %collective-permute-start.10 = (f32[5,8,128]{2,1,0:T(8,128)S(1)}, f32[5,8,128]{2,1,0:T(8,128)S(1)}, u32[]{:S(2)}, u32[]{:S(2)}) collective-permute-start(f32[5,8,128]{2,1,0:T(8,128)S(1)} %get-tuple-element.68.refs_0_), channel_id=1, source_target_pairs={{0,12},{1,13},{2,14},{3,15},{4,8},{5,9},{6,10},{7,11},{8,4},{9,5},... | collective-permute-start | bytes 61448 | tf_op jit(solution)/shard_map/ppermute | solution.py:478
  30.1 4.2 %collective-permute-start.9 = (f32[5,8,128]{2,1,0:T(8,128)S(1)}, f32[5,8,128]{2,1,0:T(8,128)S(1)}, u32[]{:S(2)}, u32[]{:S(2)}) collective-permute-start(f32[5,8,128]{2,1,0:T(8,128)S(1)} %get-tuple-element.68.refs_0_), channel_id=1, source_target_pairs={{0,4},{1,5},{2,6},{3,7},{4,0},{5,1},{6,2},{7,3},{8,12},{9,13},{10,... | collective-permute-start | bytes 61448 | tf_op jit(solution)/shard_map/ppermute | solution.py:478

commit v9 on v8

--- a/solution.py
+++ b/solution.py
@@ -420,12 +420,15 @@
     halo_out[1] = east
 
 
+def copy_kernel(field_ref, out_ref):
+    out_ref[...] = field_ref[...]
+
+
 def finish_kernel(size, radix, cells_all, *refs):
     pack_ref, others, halo_ref = refs[0], refs[1:radix], refs[radix]
-    residual_ref, answer_ref = refs[radix + 1 : radix + 3]
-    residual_out, answer_out, norms_out, packs = refs[radix + 3 :]
+    residual_ref = refs[radix + 1]
+    residual_out, norms_out, packs = refs[radix + 2 :]
     sums, *pushes = join_packs(size, radix, True, pack_ref, others, (halo_ref[0], halo_ref[1]), packs)
-    answer_out[...] = answer_ref[...]
     west, east = (
         jnp.concatenate([push[i : i + 1] for i in range(push.shape[0])], axis=1) for push in pushes
     )
@@ -533,6 +536,7 @@
     residual, answer, pack = call(closing_kernel, [vmem()] * 14, [field, field, pack_shape], [], 24 * MIB)(
         outer, inner, residual, direction, answer, product, diag, east_face, north_face, ocean, faces, coef, norms, bt
     )
+    (answer,) = call(copy_kernel, [vmem()], [field], [], 24 * MIB, work)(answer)
     devices = lax.axis_size("lon")
     size, halo = 1, []
     while True:
@@ -549,14 +553,14 @@
             24 * MIB,
         )(pack, *others, *halo)
         size *= radix
-    residual, answer, norms = call(
+    residual, norms = call(
         functools.partial(finish_kernel, size, radix, float(columns * devices * rows)),
-        [vmem()] * (radix + 3),
-        [field, field, shape(ITERS)],
+        [vmem()] * (radix + 2),
+        [field, shape(ITERS)],
         packs,
         24 * MIB,
-        out_specs=[vmem(), vmem(), smem()],
-    )(pack, *others, *halo, residual, answer)
+        out_specs=[vmem(), smem()],
+    )(pack, *others, *halo, residual)
     return answer, residual, norms
 
 

time: 35.2 us -> 35.1 us (level)
  Pallas kernels: 9.23 us -> 9.84 us
  waiting for transfers between devices: 11 us -> 10.4 us
    ppermute x6, waiting for transfers between devices: 4.17 us -> 3.54 us  [swap_runs(): lax.ppermute(pack, 'lon', [(i, i ^ s * size) for i in range(devices)])]
    pallas_call x0 -> x1, Pallas kernels: none -> 0.63 us  [on_device(): answer, = call(copy_kernel, [vmem()], [field], [], 24 * MIB, work)(answer)]
  transfers between devices with their start and end apart: 12 -> 12, of which waited for: 6 -> 6; matrix products, arithmetic and copies ran while one was open for 0% -> 0% of each run, Pallas kernels for 7% -> 9%
where the time goes in v9:
time: 35.1 us; the launch traced here: 35 us
  starting transfers between devices  12.6 us (36%)
  waiting for transfers between devices  10.4 us (30%)
  Pallas kernels  9.84 us (28%)
  between operations  2.1 us (6%)
    ppermute x2, starting transfers between devices, exchange(): lax.ppermute(outer, 'lon', across)  6.42 us
    ppermute x6, starting transfers between devices, swap_runs(): lax.ppermute(pack, 'lon', [(i, i ^ s * size) for i in range(devices)])  5.46 us
    pallas_call x1, Pallas kernels, on_device(): call(transpose_kernel, [pl.BlockSpec(memory_space=pl.ANY)], [bt_shape], [...  4.07 us
    ppermute x2, waiting for transfers between devices, exchange_beyond(): return (lax.ppermute(near, 'lon', within), lax.ppermute(far, 'lon', across))  3.59 us
    ppermute x6, waiting for transfers between devices, swap_runs(): lax.ppermute(pack, 'lon', [(i, i ^ s * size) for i in range(devices)])  3.54 us
    ppermute x2, waiting for transfers between devices, exchange(): lax.ppermute(outer, 'lon', across)  3.27 us
    pallas_call x1, Pallas kernels, on_device(): call(ahead_kernel, [vmem()] * 10, [field, field, field, field, row], [],...  1.61 us
    pallas_call x1, Pallas kernels, on_device(): call(first_kernel, [vmem()] * 7, [field, field, field, field, field, fiel...  1.13 us
  transfers between devices with their start and end apart: 12, of which 6 were waited for; matrix products, arithmetic and copies ran while one was open for 0% of the time, Pallas kernels for 9%

profile of v9, /device:TPU:0, one launch (start us, length us, event | category | flops | bytes accessed | tf_op | source)
XLA Modules:
  0.0 35.0 jit_solution(8308730335009375711)
XLA Ops:
  0.7 4.1 %shard_map.112.bt_ref = f32[8,16,128,128]{3,2,1,0:T(8,128)S(1)} custom-call(f32[128,128,128]{2,1,0:T(8,128)} %blocks_hbm.1), custom_call_target="tpu_custom_call" | custom-call | flops 1000000000 | bytes 16777216 | tf_op jit(solution)/shard_map/pallas_call | solution.py:495
  4.8 1.1 %shard_map.113 = (f32[16,1024]{1,0:T(8,128)S(1)}, f32[16,1024]{1,0:T(8,128)S(1)}, f32[16,1024]{1,0:T(8,128)S(1)}, f32[16,1024]{1,0:T(8,128)S(1)}, f32[16,1024]{1...) custom-call(s32[12,128]{1,0:T(8,128)S(1)} %bitcast.1, ...), custom_call_target="tpu_custom_call" | custom-call | tf_op jit(solution)/shard_map/pallas_call | solution.py:504
  6.0 5.5 %collective-permute-start.1 = (f32[24,1024]{1,0:T(8,128)S(1)}, f32[24,1024]{1,0:T(8,128)S(1)}, u32[]{:S(2)}, u32[]{:S(2)}) collective-permute-start(f32[24,1024]{1,0:T(8,128)S(1)} %get-tuple-element.42), channel_id=1, source_target_pairs={{0,15},{1,2},{2,1},{3,4},{4,3},{5,6},{6,5},{7,8},{8,7},{9,10},{10,... | collective-permute-start | bytes 294920 | tf_op jit(solution)/shard_map/ppermute | solution.py:468
  11.5 0.0 collective-permute-start.3
  11.5 0.7 %collective-permute-start = (f32[2,1024]{1,0:T(2,128)S(1)}, f32[2,1024]{1,0:T(2,128)S(1)}, u32[]{:S(2)}, u32[]{:S(2)}) collective-permute-start(f32[2,1024]{1,0:T(2,128)S(1)} %get-tuple-element.41), channel_id=1, source_target_pairs={{0,14},{1,15},{2,4},{3,5},{4,2},{5,3},{6,8},{7,9},{8,6},{9,7},{10,... | collective-permute-start | bytes 24584 | tf_op jit(solution)/shard_map/ppermute | solution.py:475
  12.2 0.0 collective-permute-start.2
  13.5 0.7 %shard_map.114.product_ref = f32[16,1024]{1,0:T(8,128)S(1)} custom-call(f32[8,16,128,128]{3,2,1,0:T(8,128)S(1)} %shard_map.112.bt_ref, f32[16,1024]{1,0:T(8,128)S(1)} %get-tuple-element.47.field_ref.flow_ref), custom_call_target="tpu_custom_call" | custom-call | flops 4194304 | bytes 8388608 | tf_op jit(solution)/shard_map/pallas_call | solution.py:515
  14.2 3.6 %collective-permute-done.far_ref = f32[2,1024]{1,0:T(2,128)S(1)} collective-permute-done((f32[2,1024]{1,0:T(2,128)S(1)}, f32[2,1024]{1,0:T(2,128)S(1)}, u32[]{:S(2)}, u32[]{:S(2)}) %collective-permute-start) | collective-permute-done | bytes 8224 | tf_op jit(solution)/shard_map/ppermute | solution.py:475
  17.8 0.0 collective-permute-done.2.near_ref
  17.8 0.0 collective-permute-done.1.outer_ref
  17.8 0.0 collective-permute-done.3.inner_ref
  17.8 0.6 %shard_map.115 = (f32[16,1024]{1,0:T(8,128)S(1)}, f32[16,1024]{1,0:T(8,128)S(1)}, f32[16,1024]{1,0:T(8,128)S(1)}, f32[2,1024]{1,0:T(2,128)S(1)}, f32[1,1024]{1,0...) custom-call(f32[1]{0:T(128)S(6)} %copy.12.low_ref, f32[1]{0:T(128)S(6)} %copy.13.high_ref, ...), custom_call_target="tpu_custom_call" | custom-call | tf_op jit(solution)/shard_map/pallas_call | solution.py:516
  18.5 0.9 %collective-permute-start.4 = (f32[1,1024]{1,0:T(1,128)S(1)}, f32[1,1024]{1,0:T(1,128)S(1)}, u32[]{:S(2)}, u32[]{:S(2)}) collective-permute-start(f32[1,1024]{1,0:T(1,128)S(1)} %get-tuple-element.53), channel_id=1, source_target_pairs={{0,15},{1,2},{2,1},{3,4},{4,3},{5,6},{6,5},{7,8},{8,7},{9,10},{10,... | collective-permute-start | bytes 12296 | tf_op jit(solution)/shard_map/ppermute | solution.py:468
  19.4 0.0 collective-permute-start.5
  19.4 1.6 %shard_map.116 = (f32[16,1024]{1,0:T(8,128)S(1)}, f32[16,1024]{1,0:T(8,128)S(1)}, f32[16,1024]{1,0:T(8,128)S(1)}, f32[16,1024]{1,0:T(8,128)S(1)}, f32[1,1024]{1,0:T(1,128)S(1)}) custom-call(f32[16,1024]{1,0:T(8,128)S(1)} %get-tuple-element.55.residual_ref, f32[16,1024]{1,0:T(8,128)S(1)} %get-tuple-element.56.direction_ref, ...), custom_call_target="tpu_custom_call" | custom-call | flops 4194304 | bytes 8388608 | tf_op jit(solution)/shard_map/pallas_call | solution.py:527
  21.0 3.3 %collective-permute-done.4.outer_ref = f32[1,1024]{1,0:T(1,128)S(1)} collective-permute-done((f32[1,1024]{1,0:T(1,128)S(1)}, f32[1,1024]{1,0:T(1,128)S(1)}, u32[]{:S(2)}, u32[]{:S(2)}) %collective-permute-start.4) | collective-permute-done | bytes 4128 | tf_op jit(solution)/shard_map/ppermute | solution.py:468
  24.3 0.0 collective-permute-done.5.inner_ref
  24.3 0.3 shard_map.117
  24.6 0.1 collective-permute-start.8
  24.7 0.1 collective-permute-start.7
  24.8 1.8 %collective-permute-start.6 = (f32[5,8,128]{2,1,0:T(8,128)S(1)}, f32[5,8,128]{2,1,0:T(8,128)S(1)}, u32[]{:S(2)}, u32[]{:S(2)}) collective-permute-start(f32[5,8,128]{2,1,0:T(8,128)S(1)} %get-tuple-element.67.refs_0_), channel_id=1, source_target_pairs={{0,1},{1,0},{2,3},{3,2},{4,5},{5,4},{6,7},{7,6},{8,9},{9,8},{10,11... | collective-permute-start | bytes 61448 | tf_op jit(solution)/shard_map/ppermute | solution.py:481
  26.5 1.3 %collective-permute-done.8.refs_3_ = f32[5,8,128]{2,1,0:T(8,128)S(1)} collective-permute-done((f32[5,8,128]{2,1,0:T(8,128)S(1)}, f32[5,8,128]{2,1,0:T(8,128)S(1)}, u32[]{:S(2)}, u32[]{:S(2)}) %collective-permute-start.8) | collective-permute-done | bytes 20512 | tf_op jit(solution)/shard_map/ppermute | solution.py:481
  27.9 0.7 %collective-permute-done.7.refs_2_ = f32[5,8,128]{2,1,0:T(8,128)S(1)} collective-permute-done((f32[5,8,128]{2,1,0:T(8,128)S(1)}, f32[5,8,128]{2,1,0:T(8,128)S(1)}, u32[]{:S(2)}, u32[]{:S(2)}) %collective-permute-start.7) | collective-permute-done | bytes 20512 | tf_op jit(solution)/shard_map/ppermute | solution.py:481
  28.5 0.0 collective-permute-done.6.refs_1_
  28.6 0.1 collective-permute-start.11
  28.6 1.4 %collective-permute-start.10 = (f32[5,8,128]{2,1,0:T(8,128)S(1)}, f32[5,8,128]{2,1,0:T(8,128)S(1)}, u32[]{:S(2)}, u32[]{:S(2)}) collective-permute-start(f32[5,8,128]{2,1,0:T(8,128)S(1)} %get-tuple-element.68.refs_0_), channel_id=1, source_target_pairs={{0,12},{1,13},{2,14},{3,15},{4,8},{5,9},{6,10},{7,11},{8,4},{9,5},... | collective-permute-start | bytes 61448 | tf_op jit(solution)/shard_map/ppermute | solution.py:481
  30.1 2.1 %collective-permute-start.9 = (f32[5,8,128]{2,1,0:T(8,128)S(1)}, f32[5,8,128]{2,1,0:T(8,128)S(1)}, u32[]{:S(2)}, u32[]{:S(2)}) collective-permute-start(f32[5,8,128]{2,1,0:T(8,128)S(1)} %get-tuple-element.68.refs_0_), channel_id=1, source_target_pairs={{0,4},{1,5},{2,6},{3,7},{4,0},{5,1},{6,2},{7,3},{8,12},{9,13},{10,... | collective-permute-start | bytes 61448 | tf_op jit(solution)/shard_map/ppermute | solution.py:481
  32.1 0.6 %shard_map.118 = f32[16,1024]{1,0:T(8,128)} custom-call(f32[16,1024]{1,0:T(8,128)S(1)} %get-tuple-element.66.field_ref), custom_call_target="tpu_custom_call" | custom-call | flops 4194304 | bytes 8388608 | tf_op jit(solution)/shard_map/pallas_call | solution.py:539
  32.8 0.6 %collective-permute-done.11.refs_3_ = f32[5,8,128]{2,1,0:T(8,128)S(1)} collective-permute-done((f32[5,8,128]{2,1,0:T(8,128)S(1)}, f32[5,8,128]{2,1,0:T(8,128)S(1)}, u32[]{:S(2)}, u32[]{:S(2)}) %collective-permute-start.11) | collective-permute-done | bytes 20512 | tf_op jit(solution)/shard_map/ppermute | solution.py:481
  33.3 1.0 %collective-permute-done.10.refs_2_ = f32[5,8,128]{2,1,0:T(8,128)S(1)} collective-permute-done((f32[5,8,128]{2,1,0:T(8,128)S(1)}, f32[5,8,128]{2,1,0:T(8,128)S(1)}, u32[]{:S(2)}, u32[]{:S(2)}) %collective-permute-start.10) | collective-permute-done | bytes 20512 | tf_op jit(solution)/shard_map/ppermute | solution.py:481
  34.3 0.0 collective-permute-done.9.refs_1_
  34.3 0.7 %shard_map.120 = (f32[16,1024]{1,0:T(8,128)}, f32[4]{0:T(128)}) custom-call(f32[5,8,128]{2,1,0:T(8,128)S(1)} %get-tuple-element.68.refs_0_, f32[5,8,128]{2,1,0:T(8,128)S(1)} %collective-permute-done.9.refs_1_, f32[5,8,128]{2,1,0:T(8,128)S(1)} %collective-permute-done.10.refs_2_, f32[5,8,128]{2,1,0:T(8,128)S(1)} %collective-permute-done.11.refs_3_, ...), custom_call_target="tpu_custom_call" | custom-call | tf_op jit(solution)/shard_map/pallas_call | solution.py:556
  (13 shorter events, 0.1 us)
Async XLA Ops:
  0.6 4.1 %copy-start.5 = (s32[1536]{0:T(1024)S(1)}, s32[1536]{0:T(1024)}, u32[]{:S(2)}) copy-start(s32[1536]{0:T(1024)} %param.15) | copy-start | bytes 18436
  0.6 4.1 %copy-start.4 = (s32[16,1024]{1,0:T(8,128)S(1)}, s32[16,1024]{1,0:T(8,128)}, u32[]{:S(2)}) copy-start(s32[16,1024]{1,0:T(8,128)} %mask_ref.1) | copy-start | bytes 196612
  0.7 4.1 %copy-start.3 = (f32[16,1024]{1,0:T(8,128)S(1)}, f32[16,1024]{1,0:T(8,128)}, u32[]{:S(2)}) copy-start(f32[16,1024]{1,0:T(8,128)} %surface_ref.1) | copy-start | bytes 196612
  0.7 4.1 %copy-start.2 = (f32[16,1024]{1,0:T(8,128)S(1)}, f32[16,1024]{1,0:T(8,128)}, u32[]{:S(2)}) copy-start(f32[16,1024]{1,0:T(8,128)} %north_ref.1) | copy-start | bytes 196612
  0.7 4.1 %copy-start.1 = (f32[16,1024]{1,0:T(8,128)S(1)}, f32[16,1024]{1,0:T(8,128)}, u32[]{:S(2)}) copy-start(f32[16,1024]{1,0:T(8,128)} %east_ref.1) | copy-start | bytes 196612
  0.7 4.1 %copy-start = (f32[16,1024]{1,0:T(8,128)S(1)}, f32[16,1024]{1,0:T(8,128)}, u32[]{:S(2)}) copy-start(f32[16,1024]{1,0:T(8,128)} %right_ref.1) | copy-start | bytes 196612
  6.0 11.9 %collective-permute-start.1 = (f32[24,1024]{1,0:T(8,128)S(1)}, f32[24,1024]{1,0:T(8,128)S(1)}, u32[]{:S(2)}, u32[]{:S(2)}) collective-permute-start(f32[24,1024]{1,0:T(8,128)S(1)} %get-tuple-element.42), channel_id=1, source_target_pairs={{0,15},{1,2},{2,1},{3,4},{4,3},{5,6},{6,5},{7,8},{8,7},{9,10},{10,... | collective-permute-start | bytes 294920 | tf_op jit(solution)/shard_map/ppermute | solution.py:468
  11.5 6.4 %collective-permute-start.3 = (f32[24,1024]{1,0:T(8,128)S(1)}, f32[24,1024]{1,0:T(8,128)S(1)}, u32[]{:S(2)}, u32[]{:S(2)}) collective-permute-start(f32[24,1024]{1,0:T(8,128)S(1)} %get-tuple-element.44), channel_id=1, source_target_pairs={{0,1},{1,0},{2,3},{3,2},{4,5},{5,4},{6,7},{7,6},{8,9},{9,8},{10,11... | collective-permute-start | bytes 294920 | tf_op jit(solution)/shard_map/ppermute | solution.py:468
  11.5 6.3 %collective-permute-start = (f32[2,1024]{1,0:T(2,128)S(1)}, f32[2,1024]{1,0:T(2,128)S(1)}, u32[]{:S(2)}, u32[]{:S(2)}) collective-permute-start(f32[2,1024]{1,0:T(2,128)S(1)} %get-tuple-element.41), channel_id=1, source_target_pairs={{0,14},{1,15},{2,4},{3,5},{4,2},{5,3},{6,8},{7,9},{8,6},{9,7},{10,... | collective-permute-start | bytes 24584 | tf_op jit(solution)/shard_map/ppermute | solution.py:475
  12.2 5.6 %collective-permute-start.2 = (f32[2,1024]{1,0:T(2,128)S(1)}, f32[2,1024]{1,0:T(2,128)S(1)}, u32[]{:S(2)}, u32[]{:S(2)}) collective-permute-start(f32[2,1024]{1,0:T(2,128)S(1)} %get-tuple-element.43), channel_id=1, source_target_pairs={{0,2},{1,3},{2,0},{3,1},{4,6},{5,7},{6,4},{7,5},{8,10},{9,11},{10,... | collective-permute-start | bytes 24584 | tf_op jit(solution)/shard_map/ppermute | solution.py:475
  18.5 5.8 %collective-permute-start.4 = (f32[1,1024]{1,0:T(1,128)S(1)}, f32[1,1024]{1,0:T(1,128)S(1)}, u32[]{:S(2)}, u32[]{:S(2)}) collective-permute-start(f32[1,1024]{1,0:T(1,128)S(1)} %get-tuple-element.53), channel_id=1, source_target_pairs={{0,15},{1,2},{2,1},{3,4},{4,3},{5,6},{6,5},{7,8},{8,7},{9,10},{10,... | collective-permute-start | bytes 12296 | tf_op jit(solution)/shard_map/ppermute | solution.py:468
  19.4 4.9 %collective-permute-start.5 = (f32[1,1024]{1,0:T(1,128)S(1)}, f32[1,1024]{1,0:T(1,128)S(1)}, u32[]{:S(2)}, u32[]{:S(2)}) collective-permute-start(f32[1,1024]{1,0:T(1,128)S(1)} %get-tuple-element.54), channel_id=1, source_target_pairs={{0,1},{1,0},{2,3},{3,2},{4,5},{5,4},{6,7},{7,6},{8,9},{9,8},{10,11... | collective-permute-start | bytes 12296 | tf_op jit(solution)/shard_map/ppermute | solution.py:468
  24.6 3.3 %collective-permute-start.8 = (f32[5,8,128]{2,1,0:T(8,128)S(1)}, f32[5,8,128]{2,1,0:T(8,128)S(1)}, u32[]{:S(2)}, u32[]{:S(2)}) collective-permute-start(f32[5,8,128]{2,1,0:T(8,128)S(1)} %get-tuple-element.67.refs_0_), channel_id=1, source_target_pairs={{0,3},{1,2},{2,1},{3,0},{4,7},{5,6},{6,5},{7,4},{8,11},{9,10},{10,... | collective-permute-start | bytes 61448 | tf_op jit(solution)/shard_map/ppermute | solution.py:481
  24.7 3.8 %collective-permute-start.7 = (f32[5,8,128]{2,1,0:T(8,128)S(1)}, f32[5,8,128]{2,1,0:T(8,128)S(1)}, u32[]{:S(2)}, u32[]{:S(2)}) collective-permute-start(f32[5,8,128]{2,1,0:T(8,128)S(1)} %get-tuple-element.67.refs_0_), channel_id=1, source_target_pairs={{0,2},{1,3},{2,0},{3,1},{4,6},{5,7},{6,4},{7,5},{8,10},{9,11},{10,... | collective-permute-start | bytes 61448 | tf_op jit(solution)/shard_map/ppermute | solution.py:481
  24.8 3.8 %collective-permute-start.6 = (f32[5,8,128]{2,1,0:T(8,128)S(1)}, f32[5,8,128]{2,1,0:T(8,128)S(1)}, u32[]{:S(2)}, u32[]{:S(2)}) collective-permute-start(f32[5,8,128]{2,1,0:T(8,128)S(1)} %get-tuple-element.67.refs_0_), channel_id=1, source_target_pairs={{0,1},{1,0},{2,3},{3,2},{4,5},{5,4},{6,7},{7,6},{8,9},{9,8},{10,11... | collective-permute-start | bytes 61448 | tf_op jit(solution)/shard_map/ppermute | solution.py:481
  28.6 4.7 %collective-permute-start.11 = (f32[5,8,128]{2,1,0:T(8,128)S(1)}, f32[5,8,128]{2,1,0:T(8,128)S(1)}, u32[]{:S(2)}, u32[]{:S(2)}) collective-permute-start(f32[5,8,128]{2,1,0:T(8,128)S(1)} %get-tuple-element.68.refs_0_), channel_id=1, source_target_pairs={{0,8},{1,9},{2,10},{3,11},{4,12},{5,13},{6,14},{7,15},{8,0},{9,1},... | collective-permute-start | bytes 61448 | tf_op jit(solution)/shard_map/ppermute | solution.py:481
  28.6 5.6 %collective-permute-start.10 = (f32[5,8,128]{2,1,0:T(8,128)S(1)}, f32[5,8,128]{2,1,0:T(8,128)S(1)}, u32[]{:S(2)}, u32[]{:S(2)}) collective-permute-start(f32[5,8,128]{2,1,0:T(8,128)S(1)} %get-tuple-element.68.refs_0_), channel_id=1, source_target_pairs={{0,12},{1,13},{2,14},{3,15},{4,8},{5,9},{6,10},{7,11},{8,4},{9,5},... | collective-permute-start | bytes 61448 | tf_op jit(solution)/shard_map/ppermute | solution.py:481
  30.1 4.2 %collective-permute-start.9 = (f32[5,8,128]{2,1,0:T(8,128)S(1)}, f32[5,8,128]{2,1,0:T(8,128)S(1)}, u32[]{:S(2)}, u32[]{:S(2)}) collective-permute-start(f32[5,8,128]{2,1,0:T(8,128)S(1)} %get-tuple-element.68.refs_0_), channel_id=1, source_target_pairs={{0,4},{1,5},{2,6},{3,7},{4,0},{5,1},{6,2},{7,3},{8,12},{9,13},{10,... | collective-permute-start | bytes 61448 | tf_op jit(solution)/shard_map/ppermute | solution.py:481
